TPU v7x, 32 devices: a whole 2x2x4 slice. The times are simulated.
32 devices in a mesh: section: 2 (over core), dp: 4 (over z), expert: 4 (over y, x).
Axes of the slice: x: 2, y: 2, z: 4, core: 2. Of those that a mesh axis runs over, the one named last changes fastest.
Arguments:
- layer_input: bfloat16 [2, 2048, 1536], P(None, ('dp', 'expert')), may hold values from -6 to 6
- output_cotangent: bfloat16 [2, 2048, 1536], P(None, ('dp', 'expert')), may hold values from -6 to 6
- documents: int32 [2, 2048], P(None, 'dp'), may hold values from 0 to 2, as said below
- expert_routes: int32 [2, 2, 2048, 8], P('section', None, ('dp', 'expert')), may hold values from 0 to 11, as said below
- attention_gain: float32 [2, 1536], P('section'), may hold values from 0.5 to 1.5
- query_weight: bfloat16 [2, 1536, 1536], P('section', 'dp'), may hold values from -0.15625 to 0.15625
- key_weight: bfloat16 [2, 1536, 512], P('section', 'dp'), may hold values from -0.15625 to 0.15625
- value_weight: bfloat16 [2, 1536, 512], P('section', 'dp'), may hold values from -0.15625 to 0.15625
- output_weight: bfloat16 [2, 1536, 1536], P('section', 'dp'), may hold values from -1.25 to 1.25
- router_weight: bfloat16 [2, 1536, 12], P('section', 'dp'), may hold values from -0.078125 to 0.078125
- mixture_gain: float32 [2, 1536], P('section'), may hold values from 0.5 to 1.5
- expert_gate: bfloat16 [2, 12, 1536, 512], P('section', 'expert'), may hold values from -0.15625 to 0.15625
- expert_up: bfloat16 [2, 12, 1536, 512], P('section', 'expert'), may hold values from -0.15625 to 0.15625
- expert_down: bfloat16 [2, 12, 512, 1536], P('section', 'expert'), may hold values from -1 to 1
Outputs:
- layer_outputs: bfloat16 [2, 2, 2048, 1536], P('section', None, ('dp', 'expert'))
- input_grads: float32 [2, 2, 2048, 1536], P('section', None, ('dp', 'expert'))
- attention_gain_gradient: float32 [2, 1536], P('section')
- query_weight_gradient: float32 [2, 1536, 1536], P('section', 'dp')
- key_weight_gradient: float32 [2, 1536, 512], P('section', 'dp')
- value_weight_gradient: float32 [2, 1536, 512], P('section', 'dp')
- output_weight_gradient: float32 [2, 1536, 1536], P('section', 'dp')
- router_weight_gradient: float32 [2, 1536, 12], P('section', 'dp')
- mixture_gain_gradient: float32 [2, 1536], P('section')
- expert_gate_gradient: float32 [2, 12, 1536, 512], P('section', 'expert')
- expert_up_gradient: float32 [2, 12, 1536, 512], P('section', 'expert')
- expert_down_gradient: float32 [2, 12, 512, 1536], P('section', 'expert')
Inputs may be any that keep to these rules, and one draw needn't show every extreme that they name: `documents`: along each sequence of 512 tokens the numbers never fall, and every sequence holds 0, 1 and 2. `expert_routes`: each token names 8 different experts. In every micro-batch and layer some expert is named by all tokens of a sequence, so one device's 128 rows may all go to one expert.
All inputs are finite; a program needn't handle non-finite values.
Results may differ from a plain program's by a relative error of at most 0.03.
Values may be sent and summed in bfloat16 or wider, within the bound.
A program may use at most 320 MiB of HBM per device.

v0:
```python
import jax
import jax.numpy as jnp
from jax import lax
from jax.sharding import PartitionSpec as P

H = 24
KVH = 8
HD = 64


EPS = 1e-06
THETA = 10000.0
BIG = 1e30


def from_behind(block, axis, distance):
    devices = range(lax.axis_size(axis))
    route = [(i - distance, i) for i in devices if i - distance in devices]
    return lax.ppermute(block, axis, route)


def norm_rows(values, gain):
    scale = lax.rsqrt(jnp.mean(values * values, axis=-1, keepdims=True) + EPS)
    return values * scale * gain


def rotate(values, offset, heads):
    rows_here = values.shape[0]
    half_dim = HD // 2
    places = (offset + jnp.arange(rows_here, dtype=jnp.int32)).astype(jnp.float32)
    inverse = THETA ** (-jnp.arange(half_dim, dtype=jnp.float32) * 2.0 / HD)
    angles = places[:, None] * inverse[None, :]
    cosine = jnp.cos(angles)[:, None, :]
    sine_table = jnp.sin(angles)[:, None, :]
    shaped = values.reshape(rows_here, heads, HD)
    leading = shaped[..., :half_dim]
    trailing = shaped[..., half_dim:]
    turned = jnp.concatenate(
        [leading * cosine - trailing * sine_table, trailing * cosine + leading * sine_table],
        axis=-1,
    )
    return turned.reshape(rows_here, heads * HD)


def masked_scores(queries, keys_all, labels, offset):
    rows_here = queries.shape[0]
    length = keys_all.shape[0]
    grouped = queries.reshape(rows_here, KVH, H // KVH, HD)
    raw_scores = jnp.einsum(
        "tkgd,skd->kgts",
        grouped,
        keys_all.reshape(length, KVH, HD),
        preferred_element_type=jnp.float32,
    ) * HD ** (-0.5)
    places = offset + jnp.arange(rows_here, dtype=jnp.int32)
    own_labels = lax.dynamic_slice_in_dim(labels, offset, rows_here)
    allowed = (own_labels[:, None] == labels[None, :]) & (
        jnp.arange(length, dtype=jnp.int32)[None, :] <= places[:, None]
    )
    return jnp.where(allowed[None, None], raw_scores, -BIG)


def plan_slots(route, experts_all, capacity):
    flattened = route.reshape(-1)
    member_hot = (flattened[:, None] == jnp.arange(experts_all, dtype=jnp.int32)[None, :]).astype(
        jnp.int32
    )
    earlier = jnp.cumsum(member_hot, axis=0) - member_hot
    position = jnp.sum(earlier * member_hot, axis=1)
    slot_of = flattened * capacity + position
    owners = jnp.arange(flattened.shape[0], dtype=jnp.int32) // route.shape[1]
    source = jnp.full((experts_all * capacity,), capacity, jnp.int32).at[slot_of].set(owners)
    return (slot_of, source)


def forward_layer(section_entry, labels, route, offset, layer_weights, experts_all):
    (
        gain_one,
        query_full,
        key_full,
        value_full,
        out_full,
        router_full,
        gain_two,
        gate_all,
        up_all,
        down_all,
    ) = layer_weights
    rows_here, model_width = section_entry.shape
    groups = lax.axis_size("expert")
    local_count = gate_all.shape[0]
    normed_one = norm_rows(section_entry, gain_one).astype(jnp.bfloat16)
    query_raw = jnp.dot(normed_one, query_full, preferred_element_type=jnp.float32)
    key_raw = jnp.dot(normed_one, key_full, preferred_element_type=jnp.float32)
    value_raw = jnp.dot(normed_one, value_full, preferred_element_type=jnp.float32)
    queries = rotate(query_raw, offset, H).astype(jnp.bfloat16)
    keys_local = rotate(key_raw, offset, KVH).astype(jnp.bfloat16)
    values_local = value_raw.astype(jnp.bfloat16)
    keys_all, values_all = (
        lax.all_gather(keys_local, "expert", axis=0, tiled=True),
        lax.all_gather(values_local, "expert", axis=0, tiled=True),
    )
    length = keys_all.shape[0]
    scores = masked_scores(queries, keys_all, labels, offset)
    highest = jnp.max(scores, axis=-1, keepdims=True)
    powers = jnp.exp(scores - highest)
    totals = jnp.sum(powers, axis=-1, keepdims=True)
    probabilities = (powers / totals).astype(jnp.bfloat16)
    log_totals = highest + jnp.log(totals)
    mixed = jnp.einsum(
        "kgts,skd->tkgd",
        probabilities,
        values_all.reshape(length, KVH, HD),
        preferred_element_type=jnp.float32,
    )
    attended = mixed.reshape(rows_here, H * HD).astype(jnp.bfloat16)
    middle = section_entry + jnp.dot(attended, out_full, preferred_element_type=jnp.float32)
    normed_two = norm_rows(middle, gain_two).astype(jnp.bfloat16)
    logits = jnp.dot(normed_two, router_full, preferred_element_type=jnp.float32)
    choose = (route[:, :, None] == jnp.arange(experts_all, dtype=jnp.int32)[None, None, :]).astype(
        jnp.float32
    )
    chosen = jnp.sum(choose * logits[:, None, :], axis=-1)
    gate_values = jax.nn.softmax(chosen, axis=-1)
    slot_of, source = plan_slots(route, experts_all, rows_here)
    padded = jnp.concatenate([normed_two, jnp.zeros((1, model_width), jnp.bfloat16)], axis=0)
    outgoing = padded[source]
    inputs = lax.all_to_all(
        outgoing.reshape(groups, local_count * rows_here, model_width),
        "expert",
        split_axis=0,
        concat_axis=0,
        tiled=True,
    ).reshape(groups, local_count, rows_here, model_width)
    gate_val = jnp.einsum("secd,edf->secf", inputs, gate_all, preferred_element_type=jnp.float32)
    up_val = jnp.einsum("secd,edf->secf", inputs, up_all, preferred_element_type=jnp.float32)
    hidden = (jax.nn.silu(gate_val) * up_val).astype(jnp.bfloat16)
    results = jnp.einsum(
        "secf,efd->secd", hidden, down_all, preferred_element_type=jnp.float32
    ).astype(jnp.bfloat16)
    returned = lax.all_to_all(
        results.reshape(groups, local_count * rows_here, model_width),
        "expert",
        split_axis=0,
        concat_axis=0,
        tiled=True,
    ).reshape(-1, model_width)
    picked = returned[slot_of].reshape(rows_here, route.shape[1], model_width)
    output = middle + jnp.sum(gate_values[:, :, None] * picked.astype(jnp.float32), axis=1)
    stored = {
        "entry": section_entry,
        "labels": labels,
        "normed_one": normed_one,
        "queries": queries,
        "keys_all": keys_all,
        "values_all": values_all,
        "log_totals": log_totals,
        "attended": attended,
        "middle": middle,
        "normed_two": normed_two,
        "choose": choose,
        "chosen": chosen,
        "gate_values": gate_values,
        "slot_of": slot_of,
        "inputs": inputs,
        "gate_val": gate_val,
        "up_val": up_val,
        "hidden": hidden,
        "picked": picked,
    }
    return (output, stored)


def backward_layer(grad_output, stored, offset, layer_weights, experts_all):
    (
        gain_one,
        query_full,
        key_full,
        value_full,
        out_full,
        router_full,
        gain_two,
        gate_all,
        up_all,
        down_all,
    ) = layer_weights
    rows_here, model_width = grad_output.shape
    groups = lax.axis_size("expert")
    local_count = gate_all.shape[0]
    share_grad = jnp.sum(grad_output[:, None, :] * stored["picked"].astype(jnp.float32), axis=-1)
    gate_pullback = jax.vjp(lambda values: jax.nn.softmax(values, axis=-1), stored["chosen"])[1]
    chosen_grad = gate_pullback(share_grad)[0]
    logit_grad = jnp.sum(stored["choose"] * chosen_grad[:, :, None], axis=1).astype(jnp.bfloat16)
    router_grad = jnp.einsum(
        "td,te->de", stored["normed_two"], logit_grad, preferred_element_type=jnp.float32
    )
    mixture_grad = jnp.einsum(
        "te,de->td", logit_grad, router_full, preferred_element_type=jnp.float32
    )
    route_grads = (
        (stored["gate_values"][:, :, None] * grad_output[:, None, :])
        .astype(jnp.bfloat16)
        .reshape(-1, model_width)
    )
    slots_back = (
        jnp.zeros((experts_all * rows_here, model_width), jnp.bfloat16)
        .at[stored["slot_of"]]
        .set(route_grads)
    )
    result_grad = lax.all_to_all(
        slots_back.reshape(groups, local_count * rows_here, model_width),
        "expert",
        split_axis=0,
        concat_axis=0,
        tiled=True,
    ).reshape(groups, local_count, rows_here, model_width)
    down_grad = jnp.einsum(
        "secf,secd->efd", stored["hidden"], result_grad, preferred_element_type=jnp.float32
    )
    hidden_grad = jnp.einsum(
        "secd,efd->secf", result_grad, down_all, preferred_element_type=jnp.float32
    )
    act_pullback = jax.vjp(
        lambda gate_arg, up_arg: jax.nn.silu(gate_arg) * up_arg,
        stored["gate_val"],
        stored["up_val"],
    )[1]
    gate_part, up_part = act_pullback(hidden_grad)
    gate_part = gate_part.astype(jnp.bfloat16)
    up_part = up_part.astype(jnp.bfloat16)
    inputs = stored["inputs"]
    gate_grad = jnp.einsum("secd,secf->edf", inputs, gate_part, preferred_element_type=jnp.float32)
    up_grad = jnp.einsum("secd,secf->edf", inputs, up_part, preferred_element_type=jnp.float32)
    input_grad = (
        jnp.einsum("secf,edf->secd", gate_part, gate_all, preferred_element_type=jnp.float32)
        + jnp.einsum("secf,edf->secd", up_part, up_all, preferred_element_type=jnp.float32)
    ).astype(jnp.bfloat16)
    back_rows = lax.all_to_all(
        input_grad.reshape(groups, local_count * rows_here, model_width),
        "expert",
        split_axis=0,
        concat_axis=0,
        tiled=True,
    ).reshape(-1, model_width)
    mixture_grad = mixture_grad + jnp.sum(
        back_rows[stored["slot_of"]].reshape(rows_here, -1, model_width).astype(jnp.float32), axis=1
    )
    middle_part, gain_two_grad = jax.vjp(norm_rows, stored["middle"], gain_two)[1](mixture_grad)
    middle_grad = grad_output + middle_part
    branch_grad = middle_grad.astype(jnp.bfloat16)
    out_grad = jnp.einsum(
        "tc,td->cd", stored["attended"], branch_grad, preferred_element_type=jnp.float32
    )
    attended_grad = jnp.einsum(
        "td,cd->tc", branch_grad, out_full, preferred_element_type=jnp.float32
    ).astype(jnp.bfloat16)
    keys_all = stored["keys_all"]
    values_all = stored["values_all"]
    length = keys_all.shape[0]
    scores = masked_scores(stored["queries"], keys_all, stored["labels"], offset)
    probabilities = jnp.exp(scores - stored["log_totals"])
    grouped_grad = attended_grad.reshape(rows_here, KVH, H // KVH, HD)
    probability_grad = jnp.einsum(
        "tkgd,skd->kgts",
        grouped_grad,
        values_all.reshape(length, KVH, HD),
        preferred_element_type=jnp.float32,
    )
    centre = jnp.sum(probabilities * probability_grad, axis=-1, keepdims=True)
    score_grad = (probabilities * (probability_grad - centre)).astype(jnp.bfloat16)
    score_scale = HD ** (-0.5)
    query_part = (
        jnp.einsum(
            "kgts,skd->tkgd",
            score_grad,
            keys_all.reshape(length, KVH, HD),
            preferred_element_type=jnp.float32,
        ).reshape(rows_here, H * HD)
        * score_scale
    )
    grouped_queries = stored["queries"].reshape(rows_here, KVH, H // KVH, HD)
    key_part = (
        jnp.einsum(
            "kgts,tkgd->skd", score_grad, grouped_queries, preferred_element_type=jnp.float32
        ).reshape(length, KVH * HD)
        * score_scale
    )
    value_part = jnp.einsum(
        "kgts,tkgd->skd",
        probabilities.astype(jnp.bfloat16),
        grouped_grad,
        preferred_element_type=jnp.float32,
    ).reshape(length, KVH * HD)
    key_sum, value_sum = (
        lax.psum_scatter(
            key_part.astype(jnp.bfloat16), "expert", scatter_dimension=0, tiled=True
        ).astype(jnp.float32),
        lax.psum_scatter(
            value_part.astype(jnp.bfloat16), "expert", scatter_dimension=0, tiled=True
        ).astype(jnp.float32),
    )
    query_turn = jax.vjp(
        lambda values: rotate(values, offset, H), jnp.zeros((rows_here, H * HD), jnp.float32)
    )[1]
    key_turn = jax.vjp(
        lambda values: rotate(values, offset, KVH), jnp.zeros((rows_here, KVH * HD), jnp.float32)
    )[1]
    query_raw_grad = query_turn(query_part)[0].astype(jnp.bfloat16)
    key_raw_grad = key_turn(key_sum)[0].astype(jnp.bfloat16)
    value_raw_grad = value_sum.astype(jnp.bfloat16)
    normed_one = stored["normed_one"]
    query_grad = jnp.einsum(
        "td,tc->dc", normed_one, query_raw_grad, preferred_element_type=jnp.float32
    )
    key_grad = jnp.einsum("td,tc->dc", normed_one, key_raw_grad, preferred_element_type=jnp.float32)
    value_grad = jnp.einsum(
        "td,tc->dc", normed_one, value_raw_grad, preferred_element_type=jnp.float32
    )
    normed_grad = jnp.einsum(
        "tc,dc->td", query_raw_grad, query_full, preferred_element_type=jnp.float32
    )
    normed_grad = normed_grad + jnp.einsum(
        "tc,dc->td", key_raw_grad, key_full, preferred_element_type=jnp.float32
    )
    normed_grad = normed_grad + jnp.einsum(
        "tc,dc->td", value_raw_grad, value_full, preferred_element_type=jnp.float32
    )
    entry_part, gain_one_grad = jax.vjp(norm_rows, stored["entry"], gain_one)[1](normed_grad)
    parts = (
        gain_one_grad,
        query_grad,
        key_grad,
        value_grad,
        out_grad,
        router_grad,
        gain_two_grad,
        gate_grad,
        up_grad,
        down_grad,
    )
    return (middle_grad + entry_part, parts)


def body(
    layer_input,
    output_cotangent,
    documents,
    expert_routes,
    attention_gain,
    query_weight,
    key_weight,
    value_weight,
    output_weight,
    router_weight,
    mixture_gain,
    expert_gate,
    expert_up,
    expert_down,
):
    batches, rows_here, model_width = layer_input.shape
    groups = lax.axis_size("expert")
    experts_all = expert_gate.shape[1] * groups
    section_index = lax.axis_index("section")
    first_section = section_index == 0
    offset = lax.axis_index("expert") * rows_here
    query_full, key_full, value_full, out_full, router_full = (
        lax.all_gather(query_weight[0], "dp", axis=0, tiled=True),
        lax.all_gather(key_weight[0], "dp", axis=0, tiled=True),
        lax.all_gather(value_weight[0], "dp", axis=0, tiled=True),
        lax.all_gather(output_weight[0], "dp", axis=0, tiled=True),
        lax.all_gather(router_weight[0], "dp", axis=0, tiled=True),
    )
    gate_all, up_all, down_all = (expert_gate[0], expert_up[0], expert_down[0])
    layer_weights = (
        attention_gain[0],
        query_full,
        key_full,
        value_full,
        out_full,
        router_full,
        mixture_gain[0],
        gate_all,
        up_all,
        down_all,
    )
    section_routes = expert_routes[0]
    inbound = jnp.zeros((rows_here, model_width), jnp.bfloat16)
    stored_list = []
    produced = []
    for moment in range(batches + 1):
        batch_here = jnp.clip(moment - section_index, 0, batches - 1)
        own_rows = layer_input[min(moment, batches - 1)]
        section_entry = jnp.where(first_section, own_rows, inbound).astype(jnp.float32)
        labels = lax.dynamic_index_in_dim(documents, batch_here, 0, keepdims=False)
        route = lax.dynamic_index_in_dim(section_routes, batch_here, 0, keepdims=False)
        output, stored = forward_layer(
            section_entry, labels, route, offset, layer_weights, experts_all
        )
        stored_list.append(stored)
        produced.append(output)
        if moment < batches:
            inbound = from_behind(output.astype(jnp.bfloat16), "section", 1)
    received = jnp.zeros((rows_here, model_width), jnp.bfloat16)
    sent_back = []
    for moment in range(batches + 1):
        if moment < batches:
            final_grad = output_cotangent[moment].astype(jnp.float32)
        else:
            final_grad = jnp.zeros((rows_here, model_width), jnp.float32)
        incoming = jnp.where(first_section, received.astype(jnp.float32), final_grad)
        stored = jax.tree.map(
            lambda upper, lower: jnp.where(first_section, upper, lower),
            stored_list[max(moment - 1, 0)],
            stored_list[min(moment + 1, batches)],
        )
        entry_grad, parts = backward_layer(incoming, stored, offset, layer_weights, experts_all)
        if moment == 0:
            totals = parts
        else:
            totals = jax.tree.map(jnp.add, totals, parts)
        sent_back.append(entry_grad)
        if moment < batches:
            received = from_behind(entry_grad.astype(jnp.bfloat16), "section", -1)
    layer_outputs = jnp.stack(
        [jnp.where(first_section, produced[index], produced[index + 1]) for index in range(batches)]
    ).astype(jnp.bfloat16)
    input_grads = jnp.stack(
        [
            jnp.where(first_section, sent_back[index + 1], sent_back[index])
            for index in range(batches)
        ]
    )
    (
        gain_one_grad,
        query_grad,
        key_grad,
        value_grad,
        out_grad,
        router_grad,
        gain_two_grad,
        gate_grad,
        up_grad,
        down_grad,
    ) = totals
    query_grad, key_grad, value_grad, out_grad, router_grad = (
        lax.psum_scatter(
            query_grad.astype(jnp.bfloat16), "dp", scatter_dimension=0, tiled=True
        ).astype(jnp.float32),
        lax.psum_scatter(
            key_grad.astype(jnp.bfloat16), "dp", scatter_dimension=0, tiled=True
        ).astype(jnp.float32),
        lax.psum_scatter(
            value_grad.astype(jnp.bfloat16), "dp", scatter_dimension=0, tiled=True
        ).astype(jnp.float32),
        lax.psum_scatter(
            out_grad.astype(jnp.bfloat16), "dp", scatter_dimension=0, tiled=True
        ).astype(jnp.float32),
        lax.psum_scatter(
            router_grad.astype(jnp.bfloat16), "dp", scatter_dimension=0, tiled=True
        ).astype(jnp.float32),
    )
    query_grad, key_grad, value_grad, out_grad, router_grad, gain_one_grad, gain_two_grad = (
        lax.psum(query_grad.astype(jnp.bfloat16), "expert").astype(jnp.float32),
        lax.psum(key_grad.astype(jnp.bfloat16), "expert").astype(jnp.float32),
        lax.psum(value_grad.astype(jnp.bfloat16), "expert").astype(jnp.float32),
        lax.psum(out_grad.astype(jnp.bfloat16), "expert").astype(jnp.float32),
        lax.psum(router_grad.astype(jnp.bfloat16), "expert").astype(jnp.float32),
        lax.psum(gain_one_grad.astype(jnp.bfloat16), "expert").astype(jnp.float32),
        lax.psum(gain_two_grad.astype(jnp.bfloat16), "expert").astype(jnp.float32),
    )
    gate_grad, up_grad, down_grad, gain_one_grad, gain_two_grad = (
        lax.psum(gate_grad.astype(jnp.bfloat16), "dp").astype(jnp.float32),
        lax.psum(up_grad.astype(jnp.bfloat16), "dp").astype(jnp.float32),
        lax.psum(down_grad.astype(jnp.bfloat16), "dp").astype(jnp.float32),
        lax.psum(gain_one_grad.astype(jnp.bfloat16), "dp").astype(jnp.float32),
        lax.psum(gain_two_grad.astype(jnp.bfloat16), "dp").astype(jnp.float32),
    )
    return (
        layer_outputs[None],
        input_grads[None],
        gain_one_grad[None],
        query_grad[None],
        key_grad[None],
        value_grad[None],
        out_grad[None],
        router_grad[None],
        gain_two_grad[None],
        gate_grad[None],
        up_grad[None],
        down_grad[None],
    )


def solution(mesh):
    placed = (
        P(None, ("dp", "expert"), None),
        P(None, ("dp", "expert"), None),
        P(None, "dp"),
        P("section", None, ("dp", "expert"), None),
        P("section", None),
        P("section", "dp", None),
        P("section", "dp", None),
        P("section", "dp", None),
        P("section", "dp", None),
        P("section", "dp", None),
        P("section", None),
        P("section", "expert", None, None),
        P("section", "expert", None, None),
        P("section", "expert", None, None),
    )
    return jax.shard_map(
        body,
        mesh=mesh,
        in_specs=placed,
        out_specs=(
            P("section", None, ("dp", "expert"), None),
            P("section", None, ("dp", "expert"), None),
            P("section", None),
            P("section", "dp", None),
            P("section", "dp", None),
            P("section", "dp", None),
            P("section", "dp", None),
            P("section", "dp", None),
            P("section", None),
            P("section", "expert", None, None),
            P("section", "expert", None, None),
            P("section", "expert", None, None),
        ),
        check_vma=False,
    )
```

profile of v0, /device:TPU:0, one launch (start us, length us, event | category | flops | bytes accessed | tf_op | source)
XLA Modules:
  0.0 2327.0 jit_solution(13561019970252358221)
XLA Ops:
  35.6 13.8 all-gather.10.cloned.1.call-done
  51.3 10.0 all_gather.34
  62.3 24.7 %all-gather.12.cloned.1.call-done = bf16[1,1536,512]{2,1,0:T(8,128)(2,1)} async-done(((bf16[1,384,512]{2,1,0:T(8,128)(2,1)}), bf16[1,1536,512]{2,1,0:T(8,128)(2,1)}) %all-gather.12.cloned.1.call-update) | async-done | bytes 1572880 | tf_op jit(solution)/shard_map/all_gather | solution.py:368
  89.6 10.2 all_gather.36
  100.0 76.9 %all-gather.14.cloned.1.call-done = bf16[1,1536,1536]{2,1,0:T(8,128)(2,1)} async-done(((bf16[1,384,1536]{2,1,0:T(8,128)(2,1)}), bf16[1,1536,1536]{2,1,0:T(8,128)(2,1)}) %all-gather.14.cloned.1.call-update) | async-done | bytes 4718608 | tf_op jit(solution)/shard_map/all_gather | solution.py:367
  176.9 6.6 copy.380
  192.2 74.0 %all-gather.16.cloned.1.call-done = bf16[1,1536,1536]{2,1,0:T(8,128)(2,1)} async-done(((bf16[1,384,1536]{2,1,0:T(8,128)(2,1)}), bf16[1,1536,1536]{2,1,0:T(8,128)(2,1)}) %all-gather.16.cloned.1.call-update) | async-done | bytes 4718608 | tf_op jit(solution)/shard_map/all_gather | solution.py:370
  276.7 58.1 %all_to_all.60 = bf16[4,384,1536]{2,1,0:T(8,128)(2,1)S(1)} all-to-all(bf16[4,384,1536]{2,1,0:T(8,128)(2,1)} %bitcast.961), channel_id=1, replica_groups=mesh['section'=2,'dp'=4,'expert'=4] {'expert'}, dimensions={0} | all-to-all | bytes 9437184 | tf_op jit(solution)/shard_map/all_to_all | solution.py:128
  356.1 13.1 all-gather.4
  370.8 37.3 %all-to-all-done.1 = bf16[4,384,1536]{2,1,0:T(8,128)(2,1)} async-done(((bf16[4,384,1536]{2,1,0:T(8,128)(2,1)}), bf16[4,384,1536]{2,1,0:T(8,128)(2,1)}, u32[]{:S(2)}, u32[]{:S(2)}) %all-to-all-start.1) | async-done | bytes 4718624 | tf_op jit(solution)/shard_map/all_to_all | solution.py:141
  408.1 10.3 gather_fusion.1
  433.7 11.5 all_gather.40
  448.3 9.9 all_gather.41
  486.1 9.0 scatter_custom_fusion.3
  495.2 36.8 %all-to-all-done.2 = bf16[4,384,1536]{2,1,0:T(8,128)(2,1)} async-done(((bf16[4,384,1536]{2,1,0:T(8,128)(2,1)}), bf16[4,384,1536]{2,1,0:T(8,128)(2,1)}, u32[]{:S(2)}, u32[]{:S(2)}) %all-to-all-start.2) | async-done | bytes 4718624 | tf_op jit(solution)/shard_map/all_to_all | solution.py:128
  537.1 8.0 fusion.64
  545.1 8.0 fusion.52
  553.1 36.4 %all-to-all-done.6 = bf16[4,384,1536]{2,1,0:T(8,128)(2,1)} async-done(((bf16[4,384,1536]{2,1,0:T(8,128)(2,1)}), bf16[4,384,1536]{2,1,0:T(8,128)(2,1)}, u32[]{:S(2)}, u32[]{:S(2)}) %all-to-all-start.6) | async-done | bytes 4718624 | tf_op jit(solution)/shard_map/all_to_all | solution.py:210
  589.5 13.4 fusion.144
  625.8 6.6 fusion.110
  637.2 31.4 %all-to-all-done.3 = bf16[4,384,1536]{2,1,0:T(8,128)(2,1)} async-done(((bf16[4,384,1536]{2,1,0:T(8,128)(2,1)}), bf16[4,384,1536]{2,1,0:T(8,128)(2,1)}, u32[]{:S(2)}, u32[]{:S(2)}) %all-to-all-start.3) | async-done | bytes 4718624 | tf_op jit(solution)/shard_map/all_to_all | solution.py:141
  688.1 10.2 gather_fusion.3
  706.4 19.8 all-to-all-done.7
  726.2 10.2 gather_fusion.6
  793.9 24.4 %reduce-scatter.36.cloned.1.call-done = bf16[128,512]{1,0:T(8,128)(2,1)} async-done(((bf16[512,512]{1,0:T(8,128)(2,1)}), bf16[128,512]{1,0:T(8,128)(2,1)}) %reduce-scatter.36.cloned.1.call-update) | async-done | bytes 131088
  823.1 10.6 all_gather.42
  836.7 10.8 all_gather.43
  882.0 8.8 scatter_custom_fusion.4
  890.8 32.9 %all-to-all-done.4 = bf16[4,384,1536]{2,1,0:T(8,128)(2,1)} async-done(((bf16[4,384,1536]{2,1,0:T(8,128)(2,1)}), bf16[4,384,1536]{2,1,0:T(8,128)(2,1)}, u32[]{:S(2)}, u32[]{:S(2)}) %all-to-all-start.4) | async-done | bytes 4718624 | tf_op jit(solution)/shard_map/all_to_all | solution.py:128
  928.6 8.0 fusion.62
  936.7 8.0 fusion.50
  944.7 36.4 %all-to-all-done.8 = bf16[4,384,1536]{2,1,0:T(8,128)(2,1)} async-done(((bf16[4,384,1536]{2,1,0:T(8,128)(2,1)}), bf16[4,384,1536]{2,1,0:T(8,128)(2,1)}, u32[]{:S(2)}, u32[]{:S(2)}) %all-to-all-start.8) | async-done | bytes 4718624 | tf_op jit(solution)/shard_map/all_to_all | solution.py:210
  981.1 13.4 fusion.143
  1000.1 6.6 fusion.113
  1024.5 44.5 %all-to-all-done.9 = bf16[4,384,1536]{2,1,0:T(8,128)(2,1)} async-done(((bf16[4,384,1536]{2,1,0:T(8,128)(2,1)}), bf16[4,384,1536]{2,1,0:T(8,128)(2,1)}, u32[]{:S(2)}, u32[]{:S(2)}) %all-to-all-start.9) | async-done | bytes 4718624 | tf_op jit(solution)/shard_map/all_to_all | solution.py:238
  1087.2 10.4 gather_fusion.7
  1102.4 24.2 %all-to-all-done.5 = bf16[4,384,1536]{2,1,0:T(8,128)(2,1)} async-done(((bf16[4,384,1536]{2,1,0:T(8,128)(2,1)}), bf16[4,384,1536]{2,1,0:T(8,128)(2,1)}, u32[]{:S(2)}, u32[]{:S(2)}) %all-to-all-start.5) | async-done | bytes 4718624 | tf_op jit(solution)/shard_map/all_to_all | solution.py:141
  1126.6 10.2 gather_fusion.5
  1182.6 9.4 reduce-scatter.38.cloned.1.call-done
  1197.5 22.4 reduce-scatter.40.cloned.1.call-done
  1229.9 8.8 scatter_custom_fusion.5
  1238.7 60.7 %all_to_all.61 = bf16[4,384,1536]{2,1,0:T(8,128)(2,1)} all-to-all(bf16[4,384,1536]{2,1,0:T(8,128)(2,1)} %bitcast.956), channel_id=1, replica_groups=mesh['section'=2,'dp'=4,'expert'=4] {'expert'}, dimensions={0} | all-to-all | bytes 9437184 | tf_op jit(solution)/shard_map/all_to_all | solution.py:210
  1299.4 11.0 fusion.142
  1310.5 8.6 fusion.56
  1352.3 32.4 %all-to-all-done.11 = bf16[4,384,1536]{2,1,0:T(8,128)(2,1)} async-done(((bf16[4,384,1536]{2,1,0:T(8,128)(2,1)}), bf16[4,384,1536]{2,1,0:T(8,128)(2,1)}, u32[]{:S(2)}, u32[]{:S(2)}) %all-to-all-start.11) | async-done | bytes 4718624 | tf_op jit(solution)/shard_map/all_to_all | solution.py:238
  1384.7 9.7 gather_fusion.8
  1429.4 12.3 reduce-scatter.42.cloned.1.call-done
  1449.9 19.4 reduce-scatter.44.cloned.1.call-done
  1500.0 9.4 fusion.200
  1509.5 8.5 fusion.199
  1518.1 7.7 fusion.101
  1526.0 6.4 fusion.202
  1538.9 7.5 fusion.98
  1548.0 13.0 fusion.119
  1561.1 11.9 fusion.120
  1573.0 13.3 fusion.121
  1587.4 42.6 %reduce-scatter.26.cloned.1.call-done = bf16[384,1536]{1,0:T(8,128)(2,1)} async-done(((bf16[1536,1536]{1,0:T(8,128)(2,1)}), bf16[384,1536]{1,0:T(8,128)(2,1)}) %reduce-scatter.26.cloned.1.call-update) | async-done | bytes 1179664 | tf_op jit(solution)/shard_map/reduce_scatter | solution.py:446
  1630.0 88.0 %reduce-scatter.32.cloned.1.call-done = bf16[384,1536]{1,0:T(8,128)(2,1)} async-done(((bf16[1536,1536]{1,0:T(8,128)(2,1)}), bf16[384,1536]{1,0:T(8,128)(2,1)}) %reduce-scatter.32.cloned.1.call-update) | async-done | bytes 1179664 | tf_op jit(solution)/shard_map/reduce_scatter | solution.py:455
  1721.7 20.1 reduce-scatter.46.cloned.1.call-done
  1750.5 16.1 all-reduce.15
  1766.7 18.9 all-reduce.17
  1790.1 432.2 %all-reduce.24.cloned.1.call-done = (bf16[1,3,1536,512]{3,2,1,0:T(8,128)(2,1)}, bf16[1,3,1536,512]{3,2,1,0:T(8,128)(2,1)}, bf16[1,3,512,1536]{3,2,1,0:T(8,128)(2,1)}) async-done(((bf16[1,3,1536,512]{3,2,1,0:T(8,128)(2,1)}, bf16[1,3,1536,512]{3,2,1,0:T(8,128)(2,1)}, bf16[1,3,512,1536]{3,2,1,0:T(8,128)(2,1)}), (bf16[1,3,1536,512]{3,2,1,0:T(8,128)(2,1)}, bf16[1,3,1536,512]{3,2,1,0:T(8,128)(2,1)}, ...) | async-done | bytes 14155792 | tf_op jit(solution)/shard_map/psum | solution.py:472
  2222.3 7.6 broadcast_in_dim.153
  2240.0 72.5 %all-reduce.22.cloned.1.call-done = (bf16[1,384,1536]{2,1,0:T(8,128)(2,1)}, bf16[1,384,512]{2,1,0:T(8,128)(2,1)}, bf16[1,384,512]{2,1,0:T(8,128)(2,1)}, bf16[1,384,1536]{2,1,0:T(8,128)(2,1)}) async-done(((bf16[1,384,1536]{2,1,0:T(8,128)(2,1)}, bf16[1,384,512]{2,1,0:T(8,128)(2,1)}, bf16[1,384,512]{2,1,0:T(8,128)(2,1)}, bf16[1,384,1536]{2,1,0:T(8,128)(2,1)}), (bf16[1,384,1536]{2,1,0:T(8,128)(2,1)}, ...) | async-done | bytes 3145744 | tf_op jit(solution)/shard_map/psum | solution.py:463
  (787 shorter events, 543.4 us)
Async XLA Ops:
  7.2 42.3 %all-gather.10.cloned.1.call-start = ((), (), s32[]{:S(2)}) async-start(), calls=%async_computation.27 | async-start | bytes 1966080 | tf_op jit(solution)/shard_map/all_gather | solution.py:369
  7.9 79.1 %all-gather.12.cloned.1.call-start = ((), (), s32[]{:S(2)}) async-start(), calls=%async_computation.28 | async-start | bytes 1966080 | tf_op jit(solution)/shard_map/all_gather | solution.py:368
  8.7 168.2 %all-gather.14.cloned.1.call-start = ((), (), s32[]{:S(2)}) async-start(), calls=%async_computation.29 | async-start | bytes 5898240 | tf_op jit(solution)/shard_map/all_gather | solution.py:367
  9.4 256.8 %all-gather.16.cloned.1.call-start = ((), (), s32[]{:S(2)}) async-start(), calls=%async_computation.30 | async-start | bytes 5898240 | tf_op jit(solution)/shard_map/all_gather | solution.py:370
  12.2 76.5 %copy-start.121 = (s32[1,1,128,8]{2,3,1,0:T(8,128)}, s32[1,1,128,8]{2,3,1,0:T(8,128)S(1)}, u32[]{:S(2)}) copy-start(s32[1,1,128,8]{2,3,1,0:T(8,128)S(1)} %get-tuple-element.191) | copy-start | bytes 12292
  12.2 76.5 %copy-start.123 = (s32[1,1,128,8]{2,3,1,0:T(8,128)}, s32[1,1,128,8]{2,3,1,0:T(8,128)S(1)}, u32[]{:S(2)}) copy-start(s32[1,1,128,8]{2,3,1,0:T(8,128)S(1)} %get-tuple-element.189) | copy-start | bytes 12292
  27.4 62.0 %copy-start.164 = (s32[1024]{0:T(1024)}, s32[1024]{0:T(1024)S(1)}, u32[]{:S(2)}) copy-start(s32[1024]{0:T(1024)S(1)} %add_select_fusion) | copy-start | bytes 12292
  34.2 149.3 %copy-start.138 = (f32[128]{0:T(128)}, f32[128]{0:T(128)S(1)}, u32[]{:S(2)}) copy-start(f32[128]{0:T(128)S(1)} %add_rsqrt_fusion.5) | copy-start | bytes 1540
  34.3 1160.3 %copy-start.73 = (f32[128,32]{0,1:T(8,128)}, f32[128,32]{0,1:T(8,128)S(1)}, u32[]{:S(2)}) copy-start(f32[128,32]{0,1:T(8,128)S(1)} %get-tuple-element.204) | copy-start | bytes 49156
  34.3 1160.3 %copy-start.75 = (f32[128,32]{0,1:T(8,128)}, f32[128,32]{0,1:T(8,128)S(1)}, u32[]{:S(2)}) copy-start(f32[128,32]{0,1:T(8,128)S(1)} %get-tuple-element.205) | copy-start | bytes 49156
  61.3 38.7 %copy-start.44 = (bf16[512,512]{1,0:T(8,128)(2,1)}, bf16[512,512]{1,0:T(8,128)(2,1)S(1)}, u32[]{:S(2)}) copy-start(bf16[512,512]{1,0:T(8,128)(2,1)S(1)} %all_gather.34) | copy-start | bytes 1572868
  99.7 83.7 %copy-start.45 = (bf16[512,512]{1,0:T(8,128)(2,1)}, bf16[512,512]{1,0:T(8,128)(2,1)S(1)}, u32[]{:S(2)}) copy-start(bf16[512,512]{1,0:T(8,128)(2,1)S(1)} %all_gather.36) | copy-start | bytes 1572868
  192.2 77.2 %copy-start.89 = (bf16[8,64,3,128]{3,1,2,0:T(8,128)(2,1)}, bf16[8,64,3,128]{3,1,2,0:T(8,128)(2,1)S(1)}, u32[]{:S(2)}) copy-start(bf16[8,64,3,128]{3,1,2,0:T(8,128)(2,1)S(1)} %fusion.257) | copy-start | bytes 1179652
  192.2 78.3 %copy-start.145 = (s32[2048]{0:T(1024)S(1)}, s32[2048]{0:T(1024)}, u32[]{:S(2)}) copy-start(s32[2048]{0:T(1024)} %pad_clamp_fusion.2) | copy-start | bytes 24580
  270.4 98.8 %copy-start.31 = (bf16[128,1536]{1,0:T(8,128)(2,1)}, bf16[128,1536]{1,0:T(8,128)(2,1)S(1)}, u32[]{:S(2)}) copy-start(bf16[128,1536]{1,0:T(8,128)(2,1)S(1)} %multiply_convert_fusion.2) | copy-start | bytes 1179652
  276.7 64.4 %slice-start.6 = ((s8[4718592]{0:T(1024)(128)(4,1)}), s8[4194304]{0:T(1024)(128)(4,1)S(1)}, s32[]{:S(2)}) async-start(s8[4718592]{0:T(1024)(128)(4,1)} %bitcast.943), calls=%async_computation.46 | async-start | bytes 8388608
  351.0 57.1 %all-to-all-start.1 = ((bf16[4,384,1536]{2,1,0:T(8,128)(2,1)}), bf16[4,384,1536]{2,1,0:T(8,128)(2,1)}, u32[]{:S(2)}, u32[]{:S(2)}) async-start(bf16[4,384,1536]{2,1,0:T(8,128)(2,1)} %bitcast.951), calls=%async_computation.1 | async-start | bytes 9437184 | tf_op jit(solution)/shard_map/all_to_all | solution.py:141
  369.3 771.5 %copy-start.77 = (bf16[1,1536,12]{1,2,0:T(8,128)(2,1)}, bf16[1,1536,12]{1,2,0:T(8,128)(2,1)S(1)}, u32[]{:S(2)}) copy-start(bf16[1,1536,12]{1,2,0:T(8,128)(2,1)S(1)} %all-gather.4) | copy-start | bytes 110596
  423.3 37.0 %copy-start.87 = (bf16[128,1536]{1,0:T(8,128)(2,1)}, bf16[128,1536]{1,0:T(8,128)(2,1)S(1)}, u32[]{:S(2)}) copy-start(bf16[128,1536]{1,0:T(8,128)(2,1)S(1)} %add.601) | copy-start | bytes 1179652
  423.3 6.4 collective-permute-start
  431.7 442.6 %copy-start.1 = (bf16[128,1536]{1,0:T(8,128)(2,1)}, bf16[128,1536]{1,0:T(8,128)(2,1)S(1)}, u32[]{:S(2)}) copy-start(bf16[128,1536]{1,0:T(8,128)(2,1)S(1)} %get-tuple-element.137) | copy-start | bytes 1179652
  431.7 32.9 %copy-start.129 = (f32[128]{0:T(128)}, f32[128]{0:T(128)S(1)}, u32[]{:S(2)}) copy-start(f32[128]{0:T(128)S(1)} %add_rsqrt_fusion.3) | copy-start | bytes 1540
  464.8 297.1 %copy-start.18 = (bf16[128,24,64]{0,2,1:T(8,128)(2,1)}, bf16[128,24,64]{0,2,1:T(8,128)(2,1)S(1)}, u32[]{:S(2)}) copy-start(bf16[128,24,64]{0,2,1:T(8,128)(2,1)S(1)} %pad_maximum_fusion.2) | copy-start | bytes 1179652
  465.9 217.3 %copy-start.110 = (f32[8,3,128]{2,1,0:T(4,128)}, f32[8,3,128]{2,1,0:T(4,128)S(1)}, u32[]{:S(2)}) copy-start(f32[8,3,128]{2,1,0:T(4,128)S(1)} %get-tuple-element.218) | copy-start | bytes 36868
  467.3 216.0 %copy-start.115 = (f32[8,3,128]{2,1,0:T(4,128)}, f32[8,3,128]{2,1,0:T(4,128)S(1)}, u32[]{:S(2)}) copy-start(f32[8,3,128]{2,1,0:T(4,128)S(1)} %fusion.30) | copy-start | bytes 36868
  478.5 53.4 %all-to-all-start.2 = ((bf16[4,384,1536]{2,1,0:T(8,128)(2,1)}), bf16[4,384,1536]{2,1,0:T(8,128)(2,1)}, u32[]{:S(2)}, u32[]{:S(2)}) async-start(bf16[4,384,1536]{2,1,0:T(8,128)(2,1)} %bitcast.960), calls=%async_computation.2 | async-start | bytes 9437184 | tf_op jit(solution)/shard_map/all_to_all | solution.py:128
  485.9 188.8 %copy-start.136 = (f32[128,8]{0,1:T(8,128)}, f32[128,8]{0,1:T(8,128)S(1)}, u32[]{:S(2)}) copy-start(f32[128,8]{0,1:T(8,128)S(1)} %get-tuple-element.200) | copy-start | bytes 12292
  532.0 57.5 %all-to-all-start.6 = ((bf16[4,384,1536]{2,1,0:T(8,128)(2,1)}), bf16[4,384,1536]{2,1,0:T(8,128)(2,1)}, u32[]{:S(2)}, u32[]{:S(2)}) async-start(bf16[4,384,1536]{2,1,0:T(8,128)(2,1)} %bitcast.953), calls=%async_computation.6 | async-start | bytes 9437184 | tf_op jit(solution)/shard_map/all_to_all | solution.py:210
  611.2 57.5 %all-to-all-start.3 = ((bf16[4,384,1536]{2,1,0:T(8,128)(2,1)}), bf16[4,384,1536]{2,1,0:T(8,128)(2,1)}, u32[]{:S(2)}, u32[]{:S(2)}) async-start(bf16[4,384,1536]{2,1,0:T(8,128)(2,1)} %bitcast.952), calls=%async_computation.3 | async-start | bytes 9437184 | tf_op jit(solution)/shard_map/all_to_all | solution.py:141
  668.7 57.6 %all-to-all-start.7 = ((bf16[4,384,1536]{2,1,0:T(8,128)(2,1)}), bf16[4,384,1536]{2,1,0:T(8,128)(2,1)}, u32[]{:S(2)}, u32[]{:S(2)}) async-start(bf16[4,384,1536]{2,1,0:T(8,128)(2,1)} %bitcast.948), calls=%async_computation.7 | async-start | bytes 9437184 | tf_op jit(solution)/shard_map/all_to_all | solution.py:238
  673.8 116.3 %reduce-scatter.34.cloned.1.call-start = ((), (), s32[]{:S(2)}) async-start(), calls=%async_computation.31 | async-start | bytes 655360
  704.4 89.6 %collective-permute-start.1 = (bf16[128,1536]{1,0:T(8,128)(2,1)}, bf16[128,1536]{1,0:T(8,128)(2,1)}, u32[]{:S(2)}, u32[]{:S(2)}) collective-permute-start(bf16[128,1536]{1,0:T(8,128)(2,1)} %get-tuple-element.117), channel_id=1, source_target_pairs={{0,16},{1,17},{2,18},{3,19},{4,20},{5,21},{6,22},{7,23},{8,24},{9,... | collective-permute-start | bytes 1179656 | tf_op jit(solution)/shard_map/ppermute | solution.py:19
  767.5 50.8 %reduce-scatter.36.cloned.1.call-start = ((), (), s32[]{:S(2)}) async-start(), calls=%async_computation.32 | async-start | bytes 655360
  780.0 38.4 %copy-start.171 = (f32[128]{0:T(128)S(1)}, f32[128]{0:T(128)}, u32[]{:S(2)}) copy-start(f32[128]{0:T(128)} %fusion.373) | copy-start | bytes 1540
  868.9 54.7 %all-to-all-start.4 = ((bf16[4,384,1536]{2,1,0:T(8,128)(2,1)}), bf16[4,384,1536]{2,1,0:T(8,128)(2,1)}, u32[]{:S(2)}, u32[]{:S(2)}) async-start(bf16[4,384,1536]{2,1,0:T(8,128)(2,1)} %bitcast.959), calls=%async_computation.4 | async-start | bytes 9437184 | tf_op jit(solution)/shard_map/all_to_all | solution.py:128
  877.0 3.7 collective-permute-start.2
  878.7 261.3 %copy-start.127 = (f32[128,8]{0,1:T(8,128)}, f32[128,8]{0,1:T(8,128)S(1)}, u32[]{:S(2)}) copy-start(f32[128,8]{0,1:T(8,128)S(1)} %get-tuple-element.113) | copy-start | bytes 12292
  878.8 261.3 %copy-start.162 = (f32[128]{0:T(128)}, f32[128]{0:T(128)S(1)}, u32[]{:S(2)}) copy-start(f32[128]{0:T(128)S(1)} %get-tuple-element.112) | copy-start | bytes 1540
  881.9 41.7 %copy-start.27 = (f32[128,1536]{1,0:T(8,128)}, f32[128,1536]{1,0:T(8,128)S(1)}, u32[]{:S(2)}) copy-start(f32[128,1536]{1,0:T(8,128)S(1)} %convert_select_fusion.3) | copy-start | bytes 2359300
  923.6 57.4 %all-to-all-start.8 = ((bf16[4,384,1536]{2,1,0:T(8,128)(2,1)}), bf16[4,384,1536]{2,1,0:T(8,128)(2,1)}, u32[]{:S(2)}, u32[]{:S(2)}) async-start(bf16[4,384,1536]{2,1,0:T(8,128)(2,1)} %bitcast.954), calls=%async_computation.8 | async-start | bytes 9437184 | tf_op jit(solution)/shard_map/all_to_all | solution.py:210
  1011.6 57.4 %all-to-all-start.9 = ((bf16[4,384,1536]{2,1,0:T(8,128)(2,1)}), bf16[4,384,1536]{2,1,0:T(8,128)(2,1)}, u32[]{:S(2)}, u32[]{:S(2)}) async-start(bf16[4,384,1536]{2,1,0:T(8,128)(2,1)} %bitcast.955), calls=%async_computation.9 | async-start | bytes 9437184 | tf_op jit(solution)/shard_map/all_to_all | solution.py:238
  1069.0 57.6 %all-to-all-start.5 = ((bf16[4,384,1536]{2,1,0:T(8,128)(2,1)}), bf16[4,384,1536]{2,1,0:T(8,128)(2,1)}, u32[]{:S(2)}, u32[]{:S(2)}) async-start(bf16[4,384,1536]{2,1,0:T(8,128)(2,1)} %bitcast.949), calls=%async_computation.5 | async-start | bytes 9437184 | tf_op jit(solution)/shard_map/all_to_all | solution.py:141
  1074.2 117.8 %reduce-scatter.38.cloned.1.call-start = ((), (), s32[]{:S(2)}) async-start(), calls=%async_computation.33 | async-start | bytes 655360
  1167.1 52.8 %reduce-scatter.40.cloned.1.call-start = ((), (), s32[]{:S(2)}) async-start(), calls=%async_computation.34 | async-start | bytes 655360
  1177.5 42.4 %copy-start.6 = (bf16[2,128,1536]{2,1,0:T(8,128)(2,1)S(1)}, bf16[2,128,1536]{2,1,0:T(8,128)(2,1)}, u32[]{:S(2)}) copy-start(bf16[2,128,1536]{2,1,0:T(8,128)(2,1)} %param.14) | copy-start | bytes 2359300
  1226.2 3.6 collective-permute-start.3
  1229.8 69.6 %copy-start.85 = (bf16[128,1536]{1,0:T(8,128)(2,1)}, bf16[128,1536]{1,0:T(8,128)(2,1)S(1)}, u32[]{:S(2)}) copy-start(bf16[128,1536]{1,0:T(8,128)(2,1)S(1)} %collective-permute-done.3) | copy-start | bytes 1179652
  1229.9 69.5 %copy-start.50 = (f32[128,1536]{1,0:T(8,128)}, f32[128,1536]{1,0:T(8,128)S(1)}, u32[]{:S(2)}) copy-start(f32[128,1536]{1,0:T(8,128)S(1)} %convert_select_fusion.4) | copy-start | bytes 2359300
  1238.7 80.4 %slice-start.8 = ((s8[4718592]{0:T(1024)(128)(4,1)}), s8[4194304]{0:T(1024)(128)(4,1)S(1)}, s32[]{:S(2)}) async-start(s8[4718592]{0:T(1024)(128)(4,1)} %bitcast.945), calls=%async_computation.48 | async-start | bytes 8388608
  1327.3 57.4 %all-to-all-start.11 = ((bf16[4,384,1536]{2,1,0:T(8,128)(2,1)}), bf16[4,384,1536]{2,1,0:T(8,128)(2,1)}, u32[]{:S(2)}, u32[]{:S(2)}) async-start(bf16[4,384,1536]{2,1,0:T(8,128)(2,1)} %bitcast.950), calls=%async_computation.11 | async-start | bytes 9437184 | tf_op jit(solution)/shard_map/all_to_all | solution.py:238
  1332.3 109.4 %reduce-scatter.42.cloned.1.call-start = ((), (), s32[]{:S(2)}) async-start(), calls=%async_computation.35 | async-start | bytes 655360
  1416.7 52.6 %reduce-scatter.44.cloned.1.call-start = ((), (), s32[]{:S(2)}) async-start(), calls=%async_computation.36 | async-start | bytes 655360
  1425.0 162.3 %reduce-scatter.28.cloned.1.call-start = ((), (), s32[]{:S(2)}) async-start(), calls=%async_computation.24 | async-start | bytes 1966080 | tf_op jit(solution)/shard_map/reduce_scatter | solution.py:449
  1446.8 140.6 %reduce-scatter.30.cloned.1.call-start = ((), (), s32[]{:S(2)}) async-start(), calls=%async_computation.25 | async-start | bytes 1966080 | tf_op jit(solution)/shard_map/reduce_scatter | solution.py:452
  1473.2 156.8 %reduce-scatter.26.cloned.1.call-start = ((), (), s32[]{:S(2)}) async-start(), calls=%async_computation.23 | async-start | bytes 5898240 | tf_op jit(solution)/shard_map/reduce_scatter | solution.py:446
  1481.4 236.6 %reduce-scatter.32.cloned.1.call-start = ((), (), s32[]{:S(2)}) async-start(), calls=%async_computation.26 | async-start | bytes 5898240 | tf_op jit(solution)/shard_map/reduce_scatter | solution.py:455
  1499.8 242.0 %reduce-scatter.46.cloned.1.call-start = ((), (), s32[]{:S(2)}) async-start(), calls=%async_computation.37 | async-start | bytes 491520
  1547.8 674.5 %all-reduce.24.cloned.1.call-start = ((), (), s32[]{:S(2)}) async-start(), calls=%async_computation.39 | async-start | bytes 28311552 | tf_op jit(solution)/shard_map/psum | solution.py:472
  1586.3 157.1 %copy-start.142 = (f32[1536]{0:T(1024)S(1)}, f32[1536]{0:T(1024)}, u32[]{:S(2)}) copy-start(f32[1536]{0:T(1024)} %get-tuple-element.82) | copy-start | bytes 18436
  1586.3 158.5 %copy-start.72 = (bf16[128,24,64]{0,2,1:T(8,128)(2,1)S(1)}, bf16[128,24,64]{0,2,1:T(8,128)(2,1)}, u32[]{:S(2)}) copy-start(bf16[128,24,64]{0,2,1:T(8,128)(2,1)} %copy-done.71) | copy-start | bytes 1179652
  1586.3 726.1 %all-reduce.22.cloned.1.call-start = ((), (), s32[]{:S(2)}) async-start(), calls=%async_computation.38 | async-start | bytes 6291456 | tf_op jit(solution)/shard_map/psum | solution.py:463
  1748.9 38.5 %copy-start.175 = (f32[128]{0:T(128)S(1)}, f32[128]{0:T(128)}, u32[]{:S(2)}) copy-start(f32[128]{0:T(128)} %get-tuple-element.89) | copy-start | bytes 1540
  1749.0 38.5 %copy-start.166 = (f32[128]{0:T(128)S(1)}, f32[128]{0:T(128)}, u32[]{:S(2)}) copy-start(f32[128]{0:T(128)} %fusion.377) | copy-start | bytes 1540
  1749.7 37.7 %copy-start.48 = (f32[128,1536]{1,0:T(8,128)S(1)}, f32[128,1536]{1,0:T(8,128)}, u32[]{:S(2)}) copy-start(f32[128,1536]{1,0:T(8,128)} %copy-done.47) | copy-start | bytes 2359300
  (160 other events, 1183.5 us)
Sparse Core Ops, SparseCore 0:
  9.6 39.8 all-gather.9
  51.0 35.9 all-gather.11
  88.6 88.2 all-gather.13
  178.3 87.8 all-gather.15
  767.7 22.3 reduce-scatter.33
  793.6 24.7 reduce-scatter.35
  1167.2 24.7 reduce-scatter.37
  1195.1 24.7 reduce-scatter.39
  1416.8 24.7 reduce-scatter.41
  1444.6 24.7 reduce-scatter.43
  1471.7 35.2 reduce-scatter.27
  1509.2 34.2 reduce-scatter.29
  1545.7 84.2 reduce-scatter.25
  1632.2 85.7 reduce-scatter.31
  1720.7 21.0 reduce-scatter.45
  1745.3 476.9 all-reduce.23
  2225.9 86.5 all-reduce.21
where the time goes:
time: 2340 us; the launch traced here: 2330 us
  waiting for transfers between devices  1280 us (55%)
  matrix products  394 us (17%)
  blocking collectives  230 us (10%)
  local copies, waits for them, and re-layouts  186 us (8%)
  other arithmetic  164 us (7%)
  starting transfers between devices  59.2 us (3%)
    psum x1, waiting for transfers between devices, body(): lax.psum(gate_grad.astype(jnp.bfloat16), 'dp').astype(jnp.float32)  432 us
    unnamed x24, waiting for transfers between devices  116 us
    all_to_all x3, waiting for transfers between devices, backward_layer(): lax.all_to_all(input_grad.reshape(groups, local_count * rows_here, model_...  96.7 us
    all_to_all x3, waiting for transfers between devices, forward_layer(): lax.all_to_all(results.reshape(groups, local_count * rows_here, model_wid...  92.9 us
    reduce_scatter x1, waiting for transfers between devices, body(): lax.psum_scatter(out_grad.astype(jnp.bfloat16), 'dp', scatter_dimension=0...  88 us
    all_gather x1, waiting for transfers between devices, body(): lax.all_gather(query_weight[0], 'dp', axis=0, tiled=True)  76.9 us
    all_gather x1, waiting for transfers between devices, body(): lax.all_gather(output_weight[0], 'dp', axis=0, tiled=True)  74 us
    all_to_all x2, waiting for transfers between devices, backward_layer(): lax.all_to_all(slots_back.reshape(groups, local_count * rows_here, model_...  72.7 us
  transfers between devices with their start and end apart: 31, of which 27 were waited for; matrix products, arithmetic and copies ran while one was open for 20% of the time, Pallas kernels for 0%

commit v1 on v0

v1 whole, which is shorter than its diff:
```python
import functools

import jax
import jax.numpy as jnp
from jax import lax
from jax.experimental import pallas as pl
from jax.experimental.pallas import tpu as pltpu
from jax.sharding import PartitionSpec as P

H = 24
KVH = 8
HD = 64
GROUP = H // KVH
HALF = HD // 2

EPS = 1e-06
THETA = 10000.0
BIG = 1e30
LANES = 128
LOW = 64
SCALE = HD ** (-0.5)
VMEM = 60 * 1024 * 1024

F32 = jnp.float32
BF16 = jnp.bfloat16


def params(*semantics):
    return pltpu.CompilerParams(vmem_limit_bytes=VMEM, dimension_semantics=semantics or None)


def cost(flops, nbytes):
    return pl.CostEstimate(flops=int(flops), bytes_accessed=int(nbytes), transcendentals=0)


def dot(left, right, contract):
    return lax.dot_general(left, right, (contract, ((), ())), preferred_element_type=F32)


def shape(dims, dtype):
    return jax.ShapeDtypeStruct(dims, dtype)


def whole():
    return pl.BlockSpec(memory_space=pltpu.VMEM)


def shift(block, axis, distance, sections=None):
    count = lax.axis_size(axis)
    if sections is None:
        return lax.ppermute(block, axis, [(i, (i + distance) % count) for i in range(count)])
    route = [
        (section * count + i, section * count + (i + distance) % count)
        for section in sections
        for i in range(count)
    ]
    return lax.ppermute(block, ("section", axis), route)


def from_behind(block, distance):
    devices = range(lax.axis_size("section"))
    route = [(i - distance, i) for i in devices if i - distance in devices]
    return lax.ppermute(block, "section", route)


def spread(block, sections=None, axis="expert"):
    return [block] + [
        shift(block, axis, distance, sections) for distance in range(1, lax.axis_size(axis))
    ]


def partner(me, distance):
    other = me
    bit = 1
    while bit <= distance:
        if distance & bit:
            other = other + bit - 2 * bit * (me // bit % 2)
        bit *= 2
    return other


def plane_peers(blocks):
    me = lax.axis_index("expert")
    here = (lax.axis_index("section"), lax.axis_index("dp"))
    return [here + (partner(me, d),) for d in range(1, blocks)]


def line_peers(members):
    place = lax.axis_index("dp")
    return [
        (lax.axis_index("section"), lax.rem(place + k, members), lax.axis_index("expert"))
        for k in range(1, members)
    ]


def greet(peers):
    barrier = pltpu.get_barrier_semaphore()
    for peer in peers:
        pl.semaphore_signal(barrier, inc=1, device_id=peer, device_id_type=pl.DeviceIdType.MESH)
    pl.semaphore_wait(barrier, len(peers))


def send(source, target, send_sem, recv_sem, peer):
    return pltpu.make_async_remote_copy(
        src_ref=source,
        dst_ref=target,
        send_sem=send_sem,
        recv_sem=recv_sem,
        device_id=peer,
        device_id_type=pl.DeviceIdType.MESH,
    )


def in_section(section):
    return pl.when(lax.axis_index("section") == section)


def in_sections(sections):
    if len(sections) == 1:
        return in_section(sections[0])
    return lambda run: run()


def relay_sems(blocks, members):
    line = (2, members - 1)
    plane = (members - 1, blocks - 2)
    return [pltpu.SemaphoreType.DMA(dims) for dims in (line, line, plane, plane, (1,))]


class Relay:
    def __init__(self, near, dest, sems):
        self.near, self.dest = near, dest
        self.members, self.blocks = dest.shape[:2]
        self.line_send, self.line_recv, self.plane_send, self.plane_recv, self.near_sem = sems

    def line(self, which, k):
        slot = which * (self.blocks - 1)
        return send(
            self.near.at[slot],
            self.dest.at[k, slot],
            self.line_send.at[which, k - 1],
            self.line_recv.at[which, k - 1],
            line_peers(self.members)[k - 1],
        )

    def plane(self, k, d):
        return send(
            self.dest.at[k, 0],
            self.dest.at[k, d],
            self.plane_send.at[k - 1, d - 1],
            self.plane_recv.at[k - 1, d - 1],
            plane_peers(self.blocks)[d - 1],
        )

    def start(self, which):
        for k in range(1, self.members):
            self.line(which, k).start()

    def keep(self):
        return pltpu.make_async_copy(self.near, self.dest.at[0], self.near_sem.at[0])

    def forward(self):
        for k in range(1, self.members):
            self.line(0, k).wait_recv()
            for d in range(1, self.blocks - 1):
                self.plane(k, d).start()

    def finish(self):
        for k in range(1, self.members):
            self.line(1, k).wait_recv()
            for which in range(2):
                self.line(which, k).wait_send()
            for d in range(1, self.blocks - 1):
                self.plane(k, d).wait()
        self.keep().wait()


def gather_kernel(section, chained, *refs):
    q_ref, k_ref, v_ref, o_ref, router_ref = refs[:5]
    refs = refs[9:] if chained else refs[5:]
    inner, out, router, local_sem, line_sem, plane_sem, router_sem, own_sem = refs
    blocks = inner.shape[0]
    depth = q_ref.shape[0]
    members = inner.shape[1] // depth
    me = lax.axis_index("expert")
    place = lax.axis_index("dp")

    def rows(member):
        return pl.ds(pl.multiple_of(member * depth, depth), depth)

    def local(e):
        copies = []
        at = 0
        for source, target, start in (
            (q_ref, inner, 0),
            (k_ref, inner, q_ref.shape[1] // blocks),
            (v_ref, inner, (q_ref.shape[1] + k_ref.shape[1]) // blocks),
            (o_ref, out, 0),
        ):
            part = source.shape[1] // blocks
            copies.append(
                pltpu.make_async_copy(
                    source.at[:, pl.ds(pl.multiple_of(e * part, LANES), part)],
                    target.at[e, rows(place), pl.ds(start, part)],
                    local_sem.at[at],
                )
            )
            at += 1
        return copies

    @in_section(section)
    def _():
        diagonal = partner(me, blocks - 1)
        for copy in local(me):
            copy.start()
        mine = pltpu.make_async_copy(router_ref, router.at[rows(place)], own_sem.at[0])
        mine.start()
        greet(plane_peers(blocks) + line_peers(members))
        for copy in local(me):
            copy.wait()

        def line(which, k):
            target, column = ((inner, me), (out, me), (out, diagonal))[which]
            piece = target.at[column, rows(place)]
            return send(
                piece,
                piece,
                line_sem.at[0, which, k - 1],
                line_sem.at[1, which, k - 1],
                line_peers(members)[k - 1],
            )

        def plane(which, k, d):
            target = (inner, out)[which]
            piece = target.at[me, rows(lax.rem(place + members - k, members))]
            return send(
                piece,
                piece,
                plane_sem.at[0, which, k - 1, d - 1],
                plane_sem.at[1, which, k - 1, d - 1],
                plane_peers(blocks)[d - 1],
            )

        def narrow(k):
            piece = router.at[rows(place)]
            return send(
                piece, piece, router_sem.at[0, k - 1], router_sem.at[1, k - 1], line_peers(members)[k - 1]
            )

        for which in range(2):
            for k in range(1, members):
                line(which, k).start()
        for d in range(1, blocks):
            for copy in local(partner(me, d)):
                copy.start()
            for copy in local(partner(me, d)):
                copy.wait()
        mine.wait()
        for k in range(1, members):
            line(2, k).start()
        for k in range(1, members):
            narrow(k).start()
        reach = (blocks, blocks - 1)
        for which in range(2):
            for k in range(1, members):
                line(which, k).wait_recv()
                for d in range(1, reach[which]):
                    plane(which, k, d).start()
        for k in range(1, members):
            line(2, k).wait_recv()
            narrow(k).wait()
            for which in range(3):
                line(which, k).wait_send()
            for which in range(2):
                for d in range(1, reach[which]):
                    plane(which, k, d).wait()


def gather_weights(section, number, sources, before=None, after=None):
    q, k, v, o, router = sources
    blocks = lax.axis_size("expert")
    members = lax.axis_size("dp")
    depth = q.shape[0] * members
    wide = (q.shape[1] + k.shape[1] + v.shape[1]) // blocks
    shapes = [
        shape((blocks, depth, wide), BF16),
        shape((blocks, depth, o.shape[1] // blocks), BF16),
        shape((depth, LANES), BF16),
    ]
    chained = before is not None
    return pl.pallas_call(
        functools.partial(gather_kernel, section, chained),
        in_specs=[pl.BlockSpec(memory_space=pl.ANY)] * (9 if chained else 5),
        out_specs=[pl.BlockSpec(memory_space=pl.ANY)] * 3,
        out_shape=shapes,
        scratch_shapes=[
            pltpu.SemaphoreType.DMA((4,)),
            pltpu.SemaphoreType.DMA((2, 3, members - 1)),
            pltpu.SemaphoreType.DMA((2, 2, members - 1, blocks - 1)),
            pltpu.SemaphoreType.DMA((2, members - 1)),
            pltpu.SemaphoreType.DMA((1,)),
        ],
        input_output_aliases={5: 0, 6: 1, 7: 2} if chained else {},
        compiler_params=pltpu.CompilerParams(collective_id=number, has_side_effects=True),
        name="gather_weights",
    )(*sources, *((*before, after) if chained else ()))


def group_of(ref, group):
    base = pl.multiple_of(group * GROUP * HD, HD)
    return jnp.concatenate(
        [ref[pl.ds(base + head * HD, HD), :] for head in range(GROUP)], axis=1
    )


def keys_of(ref, which, group):
    base = pl.multiple_of(group * HD, HD)
    return jnp.concatenate(
        [ref[block, which, pl.ds(base, HD), :] for block in range(ref.shape[0])], axis=1
    )


def turn_heads(turned, cosine, sine, target, at, count, sign):
    for head in range(0, count, HD):
        leading = turned[head : head + HALF]
        trailing = turned[head + HALF : head + HD]
        target[at + head : at + head + HALF] = (leading * cosine - trailing * sine * sign).astype(
            BF16
        )
        target[at + head + HALF : at + head + HD] = (
            trailing * cosine + leading * sine * sign
        ).astype(BF16)


def enter(sections, relays, blocks):
    for section in range(lax.axis_size("section")):
        peers = []
        own = [relay for at, relay in relays if at == section]
        if section in sections or own:
            peers = plane_peers(blocks)
        if own:
            peers = peers + line_peers(own[0].members)
        if peers:
            in_section(section)(lambda peers=peers: greet(peers))


def open_relay(relay):
    relay.keep().start()
    relay.start(0)
    relay.start(1)


def forward_kernel(sections, tasks, fresh, reused, groups_of_blocks, *refs):
    sources = [refs[14 + i] for i in range(len(tasks))]
    inputs = refs[:14]
    at = 14 + len(tasks) + reused
    outputs = refs[at : at + 8]
    dests = refs[at + 8 : at + 8 + fresh + reused]
    at = at + 8 + fresh + reused
    scratch = refs[at : at + 23]
    relay_refs = refs[at + 23 :]
    relays = [
        (section, Relay(sources[i], dests[dest], relay_refs[5 * i : 5 * i + 5]))
        for i, (section, dest) in enumerate(tasks)
    ]
    (
    entry_ref,
    gain_one_ref,
    cos_ref,
    sin_ref,
    bias_ref,
    gain_two_ref,
    router_ref,
    chosen_ref,
    pick_ref,
    inner_hbm,
    out_hbm,
    gate_hbm,
    up_hbm,
    down_hbm,
    ) = inputs
    (
    normed_out,
    q_out,
    kv_out,
    att_out,
    lse_out,
    middle_out,
    payload_out,
    output_out,
    ) = outputs
    (
    inner,
    out,
    gates_w,
    ups_w,
    downs_w,
    normed,
    query,
    kv,
    att,
    lse,
    middle,
    payload,
    sent,
    back,
    own,
    result,
    inner_sem,
    out_sem,
    expert_sem,
    kv_sem,
    payload_sem,
    back_sem,
    save_sem,
    ) = scratch
    blocks = kv.shape[0]
    rows, width = entry_ref.shape
    local, _, hidden_width = gates_w.shape
    queries = query.shape[0] // blocks
    keys = kv.shape[2] // blocks
    part = width // blocks

    enter(sections, relays, blocks)
    for section, relay in relays:
        in_section(section)(lambda relay=relay: open_relay(relay))

    @in_sections(sections)
    def _():
        peers = plane_peers(blocks)
        inner_copies = [
            pltpu.make_async_copy(inner_hbm.at[e], inner.at[e], inner_sem.at[e])
            for e in range(blocks)
        ]
        out_copy = pltpu.make_async_copy(out_hbm, out, out_sem)
        expert_copies = []
        for e in range(local):
            band = pl.ds(e * hidden_width, hidden_width)
            expert_copies.append(
                (
                    pltpu.make_async_copy(gate_hbm.at[e], gates_w.at[e], expert_sem.at[e, 0]),
                    pltpu.make_async_copy(up_hbm.at[e], ups_w.at[e], expert_sem.at[e, 1]),
                    pltpu.make_async_copy(down_hbm.at[e], downs_w.at[band], expert_sem.at[e, 2]),
                )
            )
        for copy in inner_copies:
            copy.start()
        out_copy.start()
        for copies in expert_copies:
            for copy in copies:
                copy.start()

        saves = []

        def save(source, target):
            copy = pltpu.make_async_copy(source, target, save_sem.at[len(saves)])
            copy.start()
            saves.append(copy)

        values = entry_ref[...].astype(F32)
        scale = lax.rsqrt(jnp.mean(values * values, axis=-1, keepdims=True) + EPS)
        normed[...] = (values * scale * gain_one_ref[...]).astype(BF16)
        save(normed, normed_out)
        cosine = cos_ref[...]
        sine = sin_ref[...]
        for e in range(blocks):
            inner_copies[e].wait()
            turned = dot(normed[...], inner[e, :, queries:], ((1,), (0,))).T
            turn_heads(turned[:keys], cosine, sine, kv.at[0, 0], e * keys, keys, 1.0)
            kv[0, 1, e * keys : (e + 1) * keys] = turned[keys:].astype(BF16)
        kv_copies = [
            send(kv.at[0], kv.at[d], kv_sem.at[0, d - 1], kv_sem.at[1, d - 1], peers[d - 1])
            for d in range(1, blocks)
        ]
        for copy in kv_copies:
            copy.start()
        for e in range(blocks):
            turned = dot(normed[...], inner[e, :, :queries], ((1,), (0,))).T
            turn_heads(turned, cosine, sine, query, e * queries, queries, 1.0)
        save(query, q_out)
        bias = jnp.concatenate([bias_ref[...]] * GROUP, axis=1)
        for copy in kv_copies:
            copy.wait()
        save(kv, kv_out)

        def one(group, carry):
            query_group = group_of(query, group)
            scores = dot(keys_of(kv, 0, group), query_group, ((0,), (0,))) * SCALE + bias
            highest = jnp.max(scores, axis=0, keepdims=True)
            powers = jnp.exp(scores - highest)
            totals = jnp.sum(powers, axis=0, keepdims=True)
            lse[group] = highest + jnp.log(totals)
            probabilities = (powers * (1.0 / totals)).astype(BF16)
            mixed = dot(keys_of(kv, 1, group), probabilities, ((1,), (0,))).astype(BF16)
            for head in range(GROUP):
                base = pl.multiple_of(group * GROUP * HD + head * HD, HD)
                att[pl.ds(base, HD), :] = mixed[:, head * rows : (head + 1) * rows]
            return carry

        lax.fori_loop(0, kv.shape[2] // HD, one, 0)
        for section, relay in relays:
            if section in sections:
                in_section(section)(relay.forward)
        save(att, att_out)
        save(lse, lse_out)
        attended = att[...].T
        out_copy.wait()
        for e in range(blocks):
            columns = slice(e * part, (e + 1) * part)
            middle[:, columns] = entry_ref[:, columns].astype(F32) + dot(
                attended, out[e], ((1,), (0,))
            )
        save(middle, middle_out)
        held = middle[...]
        scale = lax.rsqrt(jnp.mean(held * held, axis=-1, keepdims=True) + EPS)
        normed_two = (held * scale * gain_two_ref[...]).astype(BF16)
        payload[0, :, :width] = normed_two
        logits = dot(normed_two, router_ref[...], ((1,), (0,))) + chosen_ref[...]
        highest = jnp.max(logits, axis=-1, keepdims=True)
        powers = jnp.exp(logits - highest)
        shares = powers / jnp.sum(powers, axis=-1, keepdims=True)
        high = shares.astype(BF16).astype(F32)
        payload[0, :, width:] = (high + pltpu.roll(shares - high, LOW, 1)).astype(BF16)
        payload_copies = [
            send(
                payload.at[0],
                payload.at[d],
                payload_sem.at[0, d - 1],
                payload_sem.at[1, d - 1],
                peers[d - 1],
            )
            for d in range(1, blocks)
        ]
        for copy in payload_copies:
            copy.start()
        back_copies = [
            send(sent.at[d - 1], back.at[d - 1], back_sem.at[0, d - 1], back_sem.at[1, d - 1], peers[d - 1])
            for d in range(1, blocks)
        ]
        for at, members in enumerate(groups_of_blocks):
            for d in members:
                if d:
                    payload_copies[d - 1].wait_recv()
            stacked = jnp.concatenate([payload[d] for d in members], axis=0)
            lanes = stacked[:, width:].astype(F32)
            pieces = []
            for e in range(local):
                if at == 0:
                    for copy in expert_copies[e]:
                        copy.wait()
                gate = dot(stacked[:, :width], gates_w[e], ((1,), (0,)))
                up = dot(stacked[:, :width], ups_w[e], ((1,), (0,)))
                share = jnp.sum(lanes * pick_ref[e], axis=-1, keepdims=True)
                pieces.append((gate / (1.0 + jnp.exp(-gate)) * up * share).astype(BF16))
            total = dot(jnp.concatenate(pieces, axis=1), downs_w[...], ((1,), (0,)))
            for place, d in enumerate(members):
                piece = total[place * rows : (place + 1) * rows]
                if d:
                    sent[d - 1] = piece.astype(BF16)
                    back_copies[d - 1].start()
                else:
                    own[...] = middle[...] + piece
        save(payload, payload_out)
        total = own[...]
        for d in range(1, blocks):
            back_copies[d - 1].wait_recv()
            total = total + back[d - 1].astype(F32)
        result[...] = total.astype(BF16)
        save(result, output_out)
        for d in range(1, blocks):
            payload_copies[d - 1].wait_send()
            back_copies[d - 1].wait_send()
        for copy in saves:
            copy.wait()

    for section, relay in relays:
        if section not in sections:
            in_section(section)(relay.forward)
        in_section(section)(relay.finish)


def forward_layer(
    sections,
    number,
    entry,
    gain_one,
    cosine,
    sine,
    bias,
    gain_two,
    router,
    chosen,
    pick,
    weights,
    tasks=(),
    fresh=0,
    reused=(),
):
    inner, out, gate_all, up_all, down_all = weights
    rows, width = entry.shape
    blocks = inner.shape[0]
    members = lax.axis_size("dp")
    local, _, hidden = gate_all.shape
    keys = KVH * HD
    flops = 2 * rows * width * (H + 2 * KVH) * HD + 4 * rows * rows * blocks * H * HD
    flops += 2 * rows * H * HD * width + 6 * rows * blocks * local * width * hidden
    groups_of_blocks = [[0], list(range(1, blocks - 1)), [blocks - 1]]
    pair = (2, blocks - 1)
    anywhere = pl.BlockSpec(memory_space=pl.ANY)
    first_reused = 14 + len(tasks)
    results = pl.pallas_call(
        functools.partial(
            forward_kernel,
            sections,
            [(section, dest) for section, _, dest in tasks],
            fresh,
            len(reused),
            groups_of_blocks,
        ),
        in_specs=[whole()] * 9 + [anywhere] * (5 + len(tasks) + len(reused)),
        out_specs=[anywhere] * (8 + len(reused) + fresh),
        out_shape=[
            shape((rows, width), BF16),
            shape((H * HD, rows), BF16),
            shape((blocks, 2, keys, rows), BF16),
            shape((H * HD, rows), BF16),
            shape((KVH, 1, GROUP * rows), F32),
            shape((rows, width), F32),
            shape((blocks, rows, width + LANES), BF16),
            shape((rows, width), BF16),
        ]
        + [shape((members, blocks, rows, width + LANES), BF16)] * (len(reused) + fresh),
        scratch_shapes=[
            pltpu.VMEM(inner.shape, BF16),
            pltpu.VMEM(out.shape, BF16),
            pltpu.VMEM(gate_all.shape, BF16),
            pltpu.VMEM(up_all.shape, BF16),
            pltpu.VMEM((local * hidden, width), BF16),
            pltpu.VMEM((rows, width), BF16),
            pltpu.VMEM((H * HD, rows), BF16),
            pltpu.VMEM((blocks, 2, keys, rows), BF16),
            pltpu.VMEM((H * HD, rows), BF16),
            pltpu.VMEM((KVH, 1, GROUP * rows), F32),
            pltpu.VMEM((rows, width), F32),
            pltpu.VMEM((blocks, rows, width + LANES), BF16),
            pltpu.VMEM((blocks - 1, rows, width), BF16),
            pltpu.VMEM((blocks - 1, rows, width), BF16),
            pltpu.VMEM((rows, width), F32),
            pltpu.VMEM((rows, width), BF16),
            pltpu.SemaphoreType.DMA((blocks,)),
            pltpu.SemaphoreType.DMA(()),
            pltpu.SemaphoreType.DMA((local, 3)),
            pltpu.SemaphoreType.DMA(pair),
            pltpu.SemaphoreType.DMA(pair),
            pltpu.SemaphoreType.DMA(pair),
            pltpu.SemaphoreType.DMA((8,)),
        ]
        + relay_sems(blocks, members) * len(tasks),
        input_output_aliases={first_reused + i: 8 + i for i in range(len(reused))},
        compiler_params=pltpu.CompilerParams(
            vmem_limit_bytes=VMEM, collective_id=number, has_side_effects=True
        ),
        cost_estimate=cost(flops, 3e7),
        name="forward_layer",
    )(
        entry,
        gain_one,
        cosine,
        sine,
        bias,
        gain_two,
        router,
        chosen,
        pick,
        inner,
        out,
        gate_all,
        up_all,
        down_all,
        *[payloads for _, payloads, _ in tasks],
        *reused,
    )
    return results[:8], results[8:]


def activation(gate, up, hidden_grad):
    sigmoid = 1.0 / (1.0 + jnp.exp(-gate))
    silu = gate * sigmoid
    slope = sigmoid * (1.0 + gate * (1.0 - sigmoid))
    return silu * up, hidden_grad * up * slope, hidden_grad * silu


def norm_back(values, gain, grad):
    width = values.shape[1]
    scale = lax.rsqrt(jnp.mean(values * values, axis=-1, keepdims=True) + EPS)
    scaled = grad * gain
    inner = jnp.sum(values * scaled, axis=-1, keepdims=True) * (1.0 / width)
    part = scale * scaled - values * (scale * scale * scale * inner)
    return part, jnp.sum(grad * values * scale, axis=0, keepdims=True)


HELD = 7


def backward_kernel(sections, holders, tasks, grad_dests, fresh, reused, groups_of_blocks, *refs):
    refs = list(refs)

    def take(count):
        taken = refs[:count]
        del refs[:count]
        return taken

    g_ref, gain_one_ref, gain_two_ref, router_ref, cos_ref, sin_ref, pick_ref, mark_ref = take(8)
    inner_hbm, out_hbm, gate_hbm, up_hbm, down_hbm = take(5)
    sets = [take(HELD) for _ in holders]
    sources = take(len(tasks))
    take(reused)
    outputs = take(7)
    dests = take(fresh + reused)
    gates_w, ups_w, downs_w, out, inner = take(5)
    held = take(HELD)
    entry, bias_v, query, kv, lse, middle, payload = held
    grads, gate_v, up_v, own, sent, back = take(6)
    branch, logit, middle_grad, datt = take(4)
    own_kv, sent_kv, back_kv, turned, entry_grad, entry_low, gain_one_v, gain_two_v = take(8)
    expert_sem, out_sem, inner_sem, held_sem, grads_sem, back_sem, kv_sem, save_sem = take(8)
    relays = [
        (section, Relay(sources[i], dests[dest], take(5))) for i, (section, dest) in enumerate(tasks)
    ]
    grad_relays = [(section, Relay(grads, dests[dest], take(5))) for section, dest in grad_dests]

    blocks, rows, width = grads.shape
    local, _, hidden_width = gates_w.shape
    keys = kv.shape[2]
    part = width // blocks
    queries = H * HD // blocks
    own_keys = keys // blocks

    enter(sections, relays + grad_relays, blocks)
    for section, relay in relays:
        in_section(section)(lambda relay=relay: open_relay(relay))

    @in_sections(sections)
    def _():
        peers = plane_peers(blocks)
        expert_copies = []
        for e in range(local):
            band = pl.ds(e * hidden_width, hidden_width)
            expert_copies.append(
                (
                    pltpu.make_async_copy(gate_hbm.at[e], gates_w.at[e], expert_sem.at[e, 0]),
                    pltpu.make_async_copy(up_hbm.at[e], ups_w.at[e], expert_sem.at[e, 1]),
                    pltpu.make_async_copy(down_hbm.at[e], downs_w.at[band], expert_sem.at[e, 2]),
                )
            )
        out_copy = pltpu.make_async_copy(out_hbm, out, out_sem)
        inner_copy = pltpu.make_async_copy(inner_hbm, inner, inner_sem)
        grads[0] = g_ref[...]
        grads_copies = [
            send(
                grads.at[0],
                grads.at[d],
                grads_sem.at[0, d - 1],
                grads_sem.at[1, d - 1],
                peers[d - 1],
            )
            for d in range(1, blocks)
        ]
        for copy in grads_copies:
            copy.start()

        def fetch(at, index):
            return pltpu.make_async_copy(sets[at][index], held[index], held_sem.at[index])

        order = (HELD - 1,) + tuple(range(HELD - 1))
        for at, section in enumerate(holders):

            @in_section(section)
            def _(at=at):
                fetch(at, HELD - 1).start()

        for copy in expert_copies[0]:
            copy.start()
        for at, section in enumerate(holders):

            @in_section(section)
            def _(at=at):
                for index in order[1:]:
                    fetch(at, index).start()

        for copies in expert_copies[1:]:
            for copy in copies:
                copy.start()
        out_copy.start()
        inner_copy.start()
        for section, relay in grad_relays:
            in_section(section)(lambda relay=relay: relay.start(0))

        saves = []

        def save(source, target):
            copy = pltpu.make_async_copy(source, target, save_sem.at[len(saves)])
            copy.start()
            saves.append(copy)

        fetch(0, HELD - 1).wait()
        stacked = payload[...].reshape(blocks * rows, width + LANES)
        for e in range(local):
            for copy in expert_copies[e]:
                copy.wait()
            gate_v[e] = dot(stacked[:, :width], gates_w[e], ((1,), (0,)))
            up_v[e] = dot(stacked[:, :width], ups_w[e], ((1,), (0,)))
        back_copies = [
            send(
                sent.at[d - 1],
                back.at[d - 1],
                back_sem.at[0, d - 1],
                back_sem.at[1, d - 1],
                peers[d - 1],
            )
            for d in range(1, blocks)
        ]
        for members in groups_of_blocks:
            for d in members:
                if d:
                    grads_copies[d - 1].wait_recv()
            if blocks - 1 in members:
                for section, relay in grad_relays:

                    @in_section(section)
                    def _(relay=relay):
                        relay.start(1)
                        relay.keep().start()

            held_rows = slice(members[0] * rows, (members[-1] + 1) * rows)
            grad = jnp.concatenate([grads[d] for d in members], axis=0)
            lanes = jnp.concatenate([payload[d, :, width:] for d in members], axis=0).astype(F32)
            hidden_grad = dot(grad, downs_w[...], ((1,), (1,)))
            total = jnp.zeros((rows * len(members), width), F32)
            share = jnp.zeros((rows * len(members), LANES), F32)
            for e in range(local):
                columns = slice(e * hidden_width, (e + 1) * hidden_width)
                raw = hidden_grad[:, columns]
                hidden, gate_part, up_part = activation(gate_v[e, held_rows], up_v[e, held_rows], raw)
                hidden = hidden.astype(BF16).astype(F32)
                share = share + jnp.sum(hidden * raw, axis=-1, keepdims=True) * mark_ref[e]
                weight = jnp.sum(lanes * pick_ref[e], axis=-1, keepdims=True)
                total = total + dot((gate_part * weight).astype(BF16), gates_w[e], ((1,), (1,)))
                total = total + dot((up_part * weight).astype(BF16), ups_w[e], ((1,), (1,)))
            high = share.astype(BF16).astype(F32)
            both = high + pltpu.roll(share - high, LOW, 1)
            for place, d in enumerate(members):
                band = slice(place * rows, (place + 1) * rows)
                if d:
                    sent[d - 1, :, :width] = total[band].astype(BF16)
                    sent[d - 1, :, width:] = both[band].astype(BF16)
                    back_copies[d - 1].start()
                else:
                    own[:, :width] = total[band]
                    own[:, width:] = share[band]
        for at, section in enumerate(holders):
            if at == 0:
                for index in order[1:]:
                    fetch(0, index).wait()
        for section, relay in grad_relays + [item for item in relays if item[0] in sections]:
            in_section(section)(relay.forward)

        total = own[:, :width]
        share = own[:, width:]
        for d in range(1, blocks):
            back_copies[d - 1].wait_recv()
            total = total + back[d - 1, :, :width].astype(F32)
            share = share + back[d - 1, :, width:].astype(F32)
        first = lax.broadcasted_iota(jnp.int32, (1, LANES), 1) < LOW
        shares = payload[0, :, width:].astype(F32)
        shares = jnp.where(first, shares + pltpu.roll(shares, LOW, 1), 0.0)
        share = jnp.where(first, share + pltpu.roll(share, LOW, 1), 0.0)
        weighted = shares * share
        logit_grad = (weighted - shares * jnp.sum(weighted, axis=-1, keepdims=True)).astype(BF16)
        logit[...] = logit_grad
        total = total + dot(logit_grad, router_ref[...], ((1,), (1,)))
        piece, gain_two_v[...] = norm_back(middle[...], gain_two_ref[...], total)
        middle_grad[...] = g_ref[...].astype(F32) + piece
        branch[...] = middle_grad[...].astype(BF16)
        save(logit, outputs[4])
        save(branch, outputs[3])
        save(gain_two_v, outputs[6])
        out_copy.wait()
        total = jnp.zeros(datt.shape, F32)
        for e in range(blocks):
            total = total + dot(out[e], branch[:, e * part : (e + 1) * part], ((1,), (1,)))
        datt[...] = total.astype(BF16)

        bias = jnp.concatenate([bias_v[...]] * GROUP, axis=1)
        cosine = cos_ref[...]
        sine = sin_ref[...]
        per_block = queries // (GROUP * HD)

        def one(group, carry):
            query_group = group_of(query, group)
            key_group = keys_of(kv, 0, group)
            grad_group = group_of(datt, group)
            scores = dot(key_group, query_group, ((0,), (0,))) * SCALE + bias
            probabilities = jnp.exp(scores - lse[group])
            probability_grad = dot(keys_of(kv, 1, group), grad_group, ((0,), (0,)))
            centre = jnp.sum(probabilities * probability_grad, axis=0, keepdims=True)
            score_grad = (probabilities * (probability_grad - centre)).astype(BF16)
            query_part = dot(key_group, score_grad, ((1,), (0,))) * SCALE
            e = lax.div(group, per_block)
            base = lax.rem(group, per_block) * (GROUP * HD)
            for head in range(GROUP):
                start = pl.multiple_of(base + head * HD, HALF)
                leading = query_part[:HALF, head * rows : (head + 1) * rows]
                trailing = query_part[HALF:, head * rows : (head + 1) * rows]
                turned[e, pl.ds(start, HALF), :] = (leading * cosine + trailing * sine).astype(BF16)
                turned[e, pl.ds(start + HALF, HALF), :] = (
                    trailing * cosine - leading * sine
                ).astype(BF16)
            key_part = dot(query_group, score_grad, ((1,), (1,))) * SCALE
            value_part = dot(grad_group, probabilities.astype(BF16), ((1,), (1,)))
            base = pl.multiple_of(group * HD, HD)
            for which, piece in ((0, key_part), (1, value_part)):
                own_kv[which, pl.ds(base, HD), :] = piece[:, :rows]
                for d in range(1, blocks):
                    sent_kv[d - 1, which, pl.ds(base, HD), :] = piece[
                        :, d * rows : (d + 1) * rows
                    ].astype(BF16)
            return carry

        heads = keys // HD
        kv_copies = []
        for half in range(2):
            lax.fori_loop(half * heads // 2, (half + 1) * heads // 2, one, 0)
            band = pl.ds(half * keys // 2, keys // 2)
            for d in range(1, blocks):
                copy = send(
                    sent_kv.at[d - 1, :, band],
                    back_kv.at[d - 1, :, band],
                    kv_sem.at[0, half, d - 1],
                    kv_sem.at[1, half, d - 1],
                    peers[d - 1],
                )
                copy.start()
                kv_copies.append(copy)

        inner_copy.wait()
        total = jnp.zeros((rows, width), F32)
        for e in range(blocks):
            total = total + dot(turned[e, :queries], inner[e, :, :queries], ((0,), (1,)))
        for copy in kv_copies:
            copy.wait_recv()
        pair = own_kv[...]
        for d in range(1, blocks):
            pair = pair + back_kv[d - 1].astype(F32)
        for e in range(blocks):
            band = slice(e * own_keys, (e + 1) * own_keys)
            turn_heads(pair[0, band], cosine, sine, turned.at[e], queries, own_keys, -1.0)
            turned[e, queries + own_keys :] = pair[1, band].astype(BF16)
        save(turned, outputs[2])
        for e in range(blocks):
            total = total + dot(turned[e, queries:], inner[e, :, queries:], ((0,), (1,)))
        piece, gain_one_v[...] = norm_back(entry[...].astype(F32), gain_one_ref[...], total)
        result = middle_grad[...] + piece
        entry_grad[...] = result
        entry_low[...] = result.astype(BF16)
        save(entry_low, outputs[1])
        save(entry_grad, outputs[0])
        save(gain_one_v, outputs[5])
        for d in range(1, blocks):
            grads_copies[d - 1].wait_send()
            back_copies[d - 1].wait_send()
        for copy in kv_copies:
            copy.wait_send()
        for copy in saves:
            copy.wait()

    for section, relay in relays:
        if section not in sections:
            in_section(section)(relay.forward)
    for section, relay in relays + grad_relays:
        in_section(section)(relay.finish)


def backward_layer(
    sections,
    number,
    grad,
    sets,
    gain_one,
    gain_two,
    router,
    cosine,
    sine,
    pick,
    mark,
    weights,
    tasks=(),
    grad_dests=(),
    fresh=(),
    reused=(),
):
    inner, out, gate_all, up_all, down_all = weights
    rows, width = grad.shape
    blocks = inner.shape[0]
    members = lax.axis_size("dp")
    local, _, hidden = gate_all.shape
    keys = KVH * HD
    length = rows * blocks
    flops = 4 * rows * width * (H + 2 * KVH) * HD + 10 * rows * length * H * HD
    flops += 2 * rows * H * HD * width + 10 * length * local * width * hidden
    groups_of_blocks = [[0], list(range(1, blocks - 1)), [blocks - 1]]
    pair = (2, blocks - 1)
    anywhere = pl.BlockSpec(memory_space=pl.ANY)
    first_reused = 13 + HELD * len(sets) + len(tasks)
    held = sets[0][1]
    results = pl.pallas_call(
        functools.partial(
            backward_kernel,
            sections,
            [section for section, _ in sets],
            [(section, dest) for section, _, dest in tasks],
            grad_dests,
            len(fresh),
            len(reused),
            groups_of_blocks,
        ),
        in_specs=[whole()] * 8
        + [anywhere] * (5 + HELD * len(sets) + len(tasks) + len(reused)),
        out_specs=[anywhere] * (7 + len(reused) + len(fresh)),
        out_shape=[
            shape((rows, width), F32),
            shape((rows, width), BF16),
            shape((blocks, inner.shape[2], rows), BF16),
            shape((rows, width), BF16),
            shape((rows, LANES), BF16),
            shape((1, width), F32),
            shape((1, width), F32),
        ]
        + [shape(dest.shape, BF16) for dest in reused]
        + [shape((members, blocks, rows, columns), BF16) for columns in fresh],
        scratch_shapes=[
            pltpu.VMEM(gate_all.shape, BF16),
            pltpu.VMEM(up_all.shape, BF16),
            pltpu.VMEM((local * hidden, width), BF16),
            pltpu.VMEM(out.shape, BF16),
            pltpu.VMEM(inner.shape, BF16),
        ]
        + [pltpu.VMEM(array.shape, array.dtype) for array in held]
        + [
            pltpu.VMEM((blocks, rows, width), BF16),
            pltpu.VMEM((local, length, hidden), F32),
            pltpu.VMEM((local, length, hidden), F32),
            pltpu.VMEM((rows, width + LANES), F32),
            pltpu.VMEM((blocks - 1, rows, width + LANES), BF16),
            pltpu.VMEM((blocks - 1, rows, width + LANES), BF16),
            pltpu.VMEM((rows, width), BF16),
            pltpu.VMEM((rows, LANES), BF16),
            pltpu.VMEM((rows, width), F32),
            pltpu.VMEM((H * HD, rows), BF16),
            pltpu.VMEM((2, keys, rows), F32),
            pltpu.VMEM((blocks - 1, 2, keys, rows), BF16),
            pltpu.VMEM((blocks - 1, 2, keys, rows), BF16),
            pltpu.VMEM((blocks, inner.shape[2], rows), BF16),
            pltpu.VMEM((rows, width), F32),
            pltpu.VMEM((rows, width), BF16),
            pltpu.VMEM((1, width), F32),
            pltpu.VMEM((1, width), F32),
            pltpu.SemaphoreType.DMA((local, 3)),
            pltpu.SemaphoreType.DMA(()),
            pltpu.SemaphoreType.DMA(()),
            pltpu.SemaphoreType.DMA((HELD,)),
            pltpu.SemaphoreType.DMA(pair),
            pltpu.SemaphoreType.DMA(pair),
            pltpu.SemaphoreType.DMA((2, 2, blocks - 1)),
            pltpu.SemaphoreType.DMA((7,)),
        ]
        + relay_sems(blocks, members) * (len(tasks) + len(grad_dests)),
        input_output_aliases={first_reused + i: 7 + i for i in range(len(reused))},
        compiler_params=pltpu.CompilerParams(
            vmem_limit_bytes=VMEM, collective_id=number, has_side_effects=True
        ),
        cost_estimate=cost(flops, 4e7),
        name="backward_layer",
    )(
        grad,
        gain_one,
        gain_two,
        router,
        cosine,
        sine,
        pick,
        mark,
        inner,
        out,
        gate_all,
        up_all,
        down_all,
        *[array for _, arrays in sets for array in arrays],
        *[payloads for _, payloads, _ in tasks],
        *reused,
    )
    return results[:7], results[7:]


def expert_weights_kernel(batches, *refs):
    token_refs = refs[:batches]
    grad_refs = refs[batches : 2 * batches]
    pick_ref, gate_ref, up_ref, down_ref, dgate_ref, dup_ref, ddown_ref = refs[2 * batches :]
    tile = pl.program_id(1)
    tiles = pl.num_programs(1) // batches
    width = grad_refs[0].shape[1]

    @pl.when(tile == 0)
    def _():
        for out in (dgate_ref, dup_ref, ddown_ref):
            out[...] = jnp.zeros_like(out)

    for batch in range(batches):

        @pl.when(tile // tiles == batch)
        def _(x_ref=token_refs[batch], g_ref=grad_refs[batch]):
            entry = x_ref[:, :width]
            grad = g_ref[...]
            weight = jnp.sum(x_ref[:, width:].astype(F32) * pick_ref[0], axis=-1, keepdims=True)
            gate = dot(entry, gate_ref[0], ((1,), (0,)))
            up = dot(entry, up_ref[0], ((1,), (0,)))
            hidden_grad = dot(grad, down_ref[0], ((1,), (1,)))
            hidden, gate_part, up_part = activation(gate, up, hidden_grad * weight)
            dgate_ref[0] += dot(entry, gate_part.astype(BF16), ((0,), (0,)))
            dup_ref[0] += dot(entry, up_part.astype(BF16), ((0,), (0,)))
            ddown_ref[0] += dot((hidden * weight).astype(BF16), grad, ((0,), (0,)))


def expert_weights(tokens, grads, pick, gate_all, up_all, down_all, tile=512):
    local, width, hidden = gate_all.shape
    batches = len(tokens)
    total = tokens[0].shape[0]
    tile = min(tile, total)
    tiles = total // tile
    columns = pl.BlockSpec((1, width, hidden), lambda e, t: (e, 0, 0))
    bands = pl.BlockSpec((1, hidden, width), lambda e, t: (e, 0, 0))

    def rows(batch, lanes):
        return pl.BlockSpec(
            (tile, lanes), lambda e, t: (jnp.clip(t - batch * tiles, 0, tiles - 1), 0)
        )

    return pl.pallas_call(
        functools.partial(expert_weights_kernel, batches),
        grid=(local, batches * tiles),
        in_specs=[rows(batch, width + LANES) for batch in range(batches)]
        + [rows(batch, width) for batch in range(batches)]
        + [pl.BlockSpec((1, 1, LANES), lambda e, t: (e, 0, 0)), columns, columns, bands],
        out_specs=[columns, columns, bands],
        out_shape=[
            shape((local, width, hidden), F32),
            shape((local, width, hidden), F32),
            shape((local, hidden, width), F32),
        ],
        compiler_params=params("arbitrary", "arbitrary"),
        cost_estimate=cost(
            2 * total * batches * local * 6 * width * hidden,
            local * 3 * width * hidden * 6 + total * batches * local * width * 4,
        ),
        name="expert_weights",
    )(*tokens, *grads, pick, gate_all, up_all, down_all)


def pad_lanes(block):
    return jnp.pad(block, ((0, 0), (0, LANES - block.shape[1])))


def scatter_sum(blocks_of, axis):
    count = lax.axis_size(axis)
    me = lax.axis_index(axis)
    total = blocks_of(me).astype(F32)
    for distance in range(1, count):
        total = total + shift(blocks_of((me + distance) % count), axis, distance).astype(F32)
    return total


def body(
    layer_input,
    output_cotangent,
    documents,
    expert_routes,
    attention_gain,
    query_weight,
    key_weight,
    value_weight,
    output_weight,
    router_weight,
    mixture_gain,
    expert_gate,
    expert_up,
    expert_down,
):
    batches, rows, width = layer_input.shape
    groups = lax.axis_size("expert")
    members = lax.axis_size("dp")
    local = expert_gate.shape[1]
    experts_all = local * groups
    me = lax.axis_index("expert")
    first = lax.axis_index("section") == 0

    def choose(upper, lower):
        return jax.tree.map(lambda a, b: jnp.where(first, a, b), upper, lower)

    places = (me * rows + jnp.arange(rows, dtype=jnp.int32)).astype(F32)
    inverse = THETA ** (-jnp.arange(HALF, dtype=F32) * 2.0 / HD)
    angles = inverse[:, None] * places[None, :]
    cosine = jnp.cos(angles)
    sine = jnp.sin(angles)
    number = me * local + jnp.arange(local, dtype=jnp.int32)
    lanes = jnp.arange(LANES, dtype=jnp.int32)
    mark = (lanes[None, :] == number[:, None]).astype(F32)[:, None, :]
    pick = mark + (lanes[None, :] == number[:, None] + LOW).astype(F32)[:, None, :]

    def bias_of(batch):
        labels = documents[batch]
        own = lax.dynamic_slice_in_dim(labels, me * rows, rows)
        pieces = []
        for distance in range(groups):
            source = me ^ distance
            theirs = lax.dynamic_slice_in_dim(labels, source * rows, rows)
            order = source * rows + jnp.arange(rows, dtype=jnp.int32)
            allowed = (theirs[:, None] == own[None, :]) & (
                order[:, None] <= (me * rows + jnp.arange(rows, dtype=jnp.int32))[None, :]
            )
            pieces.append(jnp.where(allowed, 0.0, -BIG))
        return jnp.concatenate(pieces, axis=0)

    def chosen_of(batch):
        named = (expert_routes[0, batch][:, :, None] == lanes[None, None, :]).any(axis=1)
        return jnp.where(named, 0.0, -BIG)

    biases = [bias_of(batch) for batch in range(batches)]
    chosens = [chosen_of(batch) for batch in range(batches)]

    sources = (
        query_weight[0],
        key_weight[0],
        value_weight[0],
        output_weight[0],
        pad_lanes(router_weight[0]),
    )
    gathered = gather_weights(0, 0, sources)
    done = from_behind(gathered[2][:8], 1)
    inner, out, router = gather_weights(1, 1, sources, gathered, done)
    gain_one = attention_gain
    gain_two = mixture_gain
    gate_all, up_all, down_all = (expert_gate[0], expert_up[0], expert_down[0])
    weights = (inner, out, gate_all, up_all, down_all)

    def active(moment):
        return [s for s in range(2) if 0 <= moment - s < batches]

    payload_all = [None] * batches
    grads_all = [None] * batches
    stored = []
    produced = []
    inbound = jnp.zeros((rows, width), BF16)

    def plan_tasks(moment):
        tasks, reused, fresh = [], [], []
        for section in active(moment - 1):
            batch = moment - 1 - section
            (fresh if payload_all[batch] is None else reused).append((section, batch))
        for at, (section, batch) in enumerate(reused + fresh):
            tasks.append((section, stored[moment - 1]["payloads"], at))
        return tasks, [batch for _, batch in reused], [batch for _, batch in fresh]

    for moment in range(batches + 1):
        sections = active(moment)
        early = min(moment, batches - 1)
        late = max(moment - 1, 0)
        if sections == [0]:
            entry, bias, chosen = layer_input[early], biases[early], chosens[early]
        elif sections == [1]:
            entry, bias, chosen = inbound, biases[late], chosens[late]
        else:
            entry, bias, chosen = choose(
                (layer_input[early], biases[early], chosens[early]),
                (inbound, biases[late], chosens[late]),
            )
        tasks, reused, fresh = plan_tasks(moment)
        results, dests = forward_layer(
            sections,
            2 + moment,
            entry,
            gain_one,
            cosine,
            sine,
            bias,
            gain_two,
            router,
            chosen,
            pick,
            weights,
            tasks,
            len(fresh),
            [payload_all[batch] for batch in reused],
        )
        for batch, dest in zip(reused + fresh, dests):
            payload_all[batch] = dest
        normed, queries, kv, attended, lse, middle, payloads, output = results
        produced.append(output)
        if moment < batches:
            inbound = from_behind(output, 1)
        stored.append(
            dict(
                held=(entry, bias, queries, kv, lse, middle, payloads),
                normed=normed,
                attended=attended,
                payloads=payloads,
            )
        )

    received = None
    moments = []
    for moment in range(batches + 1):
        sections = [s for s in range(2) if 0 <= moment - (1 - s) < batches]
        if received is None:
            grad = output_cotangent[moment]
        else:
            grad = received if moment == batches else choose(received, output_cotangent[moment])
        sets = [
            (s, stored[moment - 1 if s == 0 else moment + 1]["held"]) for s in sections
        ]
        tasks, reused, fresh = plan_tasks(batches + 1) if moment == 0 else ([], [], [])
        wanted = [(s, moment - (1 - s)) for s in sections]
        old = [(s, batch) for s, batch in wanted if grads_all[batch] is not None]
        new = [(s, batch) for s, batch in wanted if grads_all[batch] is None]
        grad_dests = []
        for at, (s, batch) in enumerate(old):
            grad_dests.append((s, len(reused) + at))
        for at, (s, batch) in enumerate(new):
            grad_dests.append((s, len(reused) + len(old) + len(fresh) + at))
        results, dests = backward_layer(
            sections,
            3 + batches + moment,
            grad,
            sets,
            gain_one,
            gain_two,
            router,
            cosine,
            sine,
            pick,
            mark,
            weights,
            tasks,
            grad_dests,
            [width + LANES] * len(fresh) + [width] * len(new),
            [payload_all[batch] for batch in reused] + [grads_all[batch] for _, batch in old],
        )
        dests = list(dests)
        for batch in reused:
            payload_all[batch] = dests.pop(0)
        for _, batch in old:
            grads_all[batch] = dests.pop(0)
        for batch in fresh:
            payload_all[batch] = dests.pop(0)
        for _, batch in new:
            grads_all[batch] = dests.pop(0)
        entry_grad, sent, turned, branch, logit_grad, gain_one_part, gain_two_part = results
        moments.append((entry_grad, turned, branch, logit_grad, gain_one_part, gain_two_part))
        if moment < batches:
            received = from_behind(sent, -1)

    gate_grad, up_grad, down_grad = expert_weights(
        [block.reshape(-1, width + LANES) for block in payload_all],
        [block.reshape(-1, width) for block in grads_all],
        pick,
        gate_all,
        up_all,
        down_all,
    )

    kept = [
        choose(
            (stored[batch]["payloads"][0], stored[batch]["normed"], stored[batch]["attended"]),
            (
                stored[batch + 1]["payloads"][0],
                stored[batch + 1]["normed"],
                stored[batch + 1]["attended"],
            ),
        )
        for batch in range(batches)
    ]
    final = [choose(moments[batch + 1], moments[batch]) for batch in range(batches)]
    layer_outputs = jnp.stack(
        [choose(produced[batch], produced[batch + 1]) for batch in range(batches)]
    )
    input_grads = jnp.stack([part[0] for part in final])

    def stack(parts, axis):
        return jnp.concatenate(parts, axis=axis)

    normed_all = stack([kept[batch][1] for batch in range(batches)], 0)
    attended_all = stack([kept[batch][2] for batch in range(batches)], 1)
    turned_all = stack([part[1] for part in final], 2)
    branch_all = stack([part[2] for part in final], 0)
    part_width = width // groups
    inner_grad = jnp.einsum(
        "td,ect->edc", normed_all, turned_all, preferred_element_type=F32
    ).astype(BF16)
    out_grad = jnp.einsum(
        "ct,ted->ecd",
        attended_all,
        branch_all.reshape(-1, groups, part_width),
        preferred_element_type=F32,
    ).astype(BF16)

    def settle(blocks):
        mine = scatter_sum(
            lambda i: lax.dynamic_index_in_dim(blocks, i, 0, keepdims=False), "expert"
        ).astype(BF16)
        depth = mine.shape[0] // members
        shard = scatter_sum(
            lambda i: lax.dynamic_slice_in_dim(mine, i * depth, depth, 0), "dp"
        ).astype(BF16)
        everyone = jnp.zeros((groups,) + shard.shape, BF16)
        for distance, piece in enumerate(spread(shard)):
            everyone = lax.dynamic_update_index_in_dim(
                everyone, piece, (me - distance) % groups, 0
            )
        return everyone

    def join(block):
        return jnp.moveaxis(block, 0, 1).reshape(block.shape[1], -1).astype(F32)

    inner_grad = settle(inner_grad)
    out_grad = settle(out_grad)
    q_cols = H * HD // groups
    kv_cols = KVH * HD // groups
    query_grad = join(inner_grad[:, :, :q_cols])
    key_grad = join(inner_grad[:, :, q_cols : q_cols + kv_cols])
    value_grad = join(inner_grad[:, :, q_cols + kv_cols :])
    out_grad = join(out_grad)

    small = 0.0
    for batch in range(batches):
        router_part = jnp.einsum(
            "te,td->ed",
            final[batch][3][:, :experts_all],
            kept[batch][0][:, :width],
            preferred_element_type=F32,
        )
        small = small + jnp.concatenate([router_part, final[batch][4], final[batch][5]], axis=0)
    small = lax.psum(small, ("dp", "expert"))
    depth = width // members
    router_grad = lax.dynamic_slice_in_dim(
        small[:experts_all], lax.axis_index("dp") * depth, depth, 1
    ).T
    return (
        layer_outputs[None],
        input_grads[None],
        small[experts_all][None],
        query_grad[None],
        key_grad[None],
        value_grad[None],
        out_grad[None],
        router_grad[None],
        small[experts_all + 1][None],
        gate_grad[None],
        up_grad[None],
        down_grad[None],
    )


def solution(mesh):
    placed = (
        P(None, ("dp", "expert"), None),
        P(None, ("dp", "expert"), None),
        P(None, "dp"),
        P("section", None, ("dp", "expert"), None),
        P("section", None),
        P("section", "dp", None),
        P("section", "dp", None),
        P("section", "dp", None),
        P("section", "dp", None),
        P("section", "dp", None),
        P("section", None),
        P("section", "expert", None, None),
        P("section", "expert", None, None),
        P("section", "expert", None, None),
    )
    return jax.shard_map(
        body,
        mesh=mesh,
        in_specs=placed,
        out_specs=(
            P("section", None, ("dp", "expert"), None),
            P("section", None, ("dp", "expert"), None),
            P("section", None),
            P("section", "dp", None),
            P("section", "dp", None),
            P("section", "dp", None),
            P("section", "dp", None),
            P("section", "dp", None),
            P("section", None),
            P("section", "expert", None, None),
            P("section", "expert", None, None),
            P("section", "expert", None, None),
        ),
        check_vma=False,
    )
```

time: 2340 us -> 1090 us (0.47)
  waiting for transfers between devices: 1280 us -> 154 us
  Pallas kernels: 0 us -> 675 us
  matrix products: 394 us -> 5.54 us
  blocking collectives: 230 us -> 0 us
  other arithmetic: 164 us -> 26.1 us
  local copies, waits for them, and re-layouts: 186 us -> 63.1 us
  starting transfers between devices: 59.2 us -> 144 us
    pallas_call x0 -> x9, Pallas kernels: none -> 675 us  [the longest x3 208 us: forward_layer(): pl.pallas_call(functools.partial(forward_kernel, sections, [(section, des...]
    psum x2 -> x1, waiting for transfers between devices: 505 us -> 0.01 us  [body(): small = lax.psum(small, ('dp', 'expert'))]
    dot_general x93 -> x4, matrix products: 394 us -> 5.54 us  [the longest x1 2.21 us: body(): jnp.einsum('td,ect->edc', normed_all, turned_all, preferred_element_type=...]
    all_to_all x10 -> x0, waiting for transfers between devices: 332 us -> none  [the longest x3 96.7 us: backward_layer(): lax.all_to_all(input_grad.reshape(groups, local_count * rows_here, model_...]
    all_gather x4 -> x0, waiting for transfers between devices: 189 us -> none  [the longest x1 76.9 us: body(): lax.all_gather(query_weight[0], 'dp', axis=0, tiled=True)]
    ppermute x4 -> x23, waiting for transfers between devices: 3.86 us -> 154 us  [the longest x5 110 us: from_behind(): return lax.ppermute(block, 'section', route)]
    ppermute x4 -> x23, starting transfers between devices: 6.34 us -> 144 us  [the longest x5 100 us: from_behind(): return lax.ppermute(block, 'section', route)]
    reduce_scatter x4 -> x0, waiting for transfers between devices: 131 us -> none  [the longest x1 88 us: body(): lax.psum_scatter(out_grad.astype(jnp.bfloat16), 'dp', scatter_dimension=0...]
  transfers between devices with their start and end apart: 31 -> 24, of which waited for: 27 -> 10; matrix products, arithmetic and copies ran while one was open for 20% -> 5% of each run, Pallas kernels for 0% -> 13%
where the time goes in v1:
time: 1090 us; the launch traced here: 1080 us
  Pallas kernels  675 us (62%)
  waiting for transfers between devices  154 us (14%)
  starting transfers between devices  144 us (13%)
  local copies, waits for them, and re-layouts  63.1 us (6%)
  other arithmetic  26.1 us (2%)
  between operations  15 us (1%)
    pallas_call x3, Pallas kernels, forward_layer(): pl.pallas_call(functools.partial(forward_kernel, sections, [(section, des...  208 us
    pallas_call x3, Pallas kernels, backward_layer(): pl.pallas_call(functools.partial(backward_kernel, sections, [section for...  178 us
    pallas_call x2, Pallas kernels, gather_weights(): pl.pallas_call(functools.partial(gather_kernel, section, chained), in_spe...  149 us
    pallas_call x1, Pallas kernels, expert_weights(): pl.pallas_call(functools.partial(expert_weights_kernel, batches), grid=(l...  141 us
    ppermute x5, waiting for transfers between devices, from_behind(): return lax.ppermute(block, 'section', route)  110 us
    ppermute x5, starting transfers between devices, from_behind(): return lax.ppermute(block, 'section', route)  100 us
    ppermute x18, waiting for transfers between devices, shift(): lax.ppermute(block, axis, [(i, (i + distance) % count) for i in range(cou...  43.9 us
    ppermute x18, starting transfers between devices, shift(): lax.ppermute(block, axis, [(i, (i + distance) % count) for i in range(cou...  43.7 us
  transfers between devices with their start and end apart: 24, of which 10 were waited for; matrix products, arithmetic and copies ran while one was open for 5% of the time, Pallas kernels for 13%

profile of v1, /device:TPU:0, one launch (start us, length us, event | category | flops | bytes accessed | tf_op | source)
XLA Modules:
  0.0 1083.1 jit_solution(16014637212380802484)
XLA Ops:
  7.2 0.9 copy.42
  8.8 148.2 %gather_weights.2 = (bf16[4,1536,640]{2,1,0:T(8,128)(2,1)}, bf16[4,1536,384]{2,1,0:T(8,128)(2,1)}, bf16[1536,128]{1,0:T(8,128)(2,1)}) custom-call(bf16[384,1536]{1,0:T(8,128)(2,1)} %bitcast.160, bf16[384,512]{1,0:T(8,128)(2,1)} %bitcast.165, bf16[384,512]{1,0:T(8,128)(2,1)} %bitcast.167, bf16[384,1536]{1,0:T(8,128)(2,1)} %bitcast.162, ...), custom_call_target="tpu_custom_call" | custom-call | tf_op jit(solution)/shard_map/gather_weights/pallas_call | solution.py:291
  157.6 1.3 collective-permute-start
  162.8 0.9 pad_maximum_fusion.2
  164.9 50.2 %forward_layer.3 = (bf16[128,1536]{1,0:T(8,128)(2,1)}, bf16[1536,128]{1,0:T(8,128)(2,1)}, bf16[4,2,512,128]{3,2,1,0:T(8,128)(2,1)}, bf16[1536,128]{1,0:T(8,128)(...) custom-call(bf16[128,1536]{1,0:T(8,128)(2,1)} %slice_bitcast_fusion., ...), custom_call_target="tpu_custom_call" | custom-call | flops 9261023232 | bytes 30000000 | tf_op jit(solution)/shard_map/forward_layer/pallas_call | solution.py:611
  215.1 95.1 %collective-permute-start.1 = (bf16[128,1536]{1,0:T(8,128)(2,1)}, bf16[128,1536]{1,0:T(8,128)(2,1)S(1)}, u32[]{:S(2)}, u32[]{:S(2)}) collective-permute-start(bf16[128,1536]{1,0:T(8,128)(2,1)} %get-tuple-element.79), channel_id=1, source_target_pairs={{0,16},{1,17},{2,18},{3,19},{4,20},{5,21},{6,22},{7,23},{8,24},{9,... | collective-permute-start | bytes 1179656 | tf_op jit(solution)/shard_map/ppermute | solution.py:63
  311.7 0.8 bitcast_select_fusion.1.refs_0_.refs_13_
  312.5 83.5 %forward_layer.4 = (bf16[128,1536]{1,0:T(8,128)(2,1)}, bf16[1536,128]{1,0:T(8,128)(2,1)}, bf16[4,2,512,128]{3,2,1,0:T(8,128)(2,1)}, bf16[1536,128]{1,0:T(8,128)(...) custom-call(bf16[128,1536]{1,0:T(8,128)(2,1)} %bitcast_select_fusion, ...), custom_call_target="tpu_custom_call" | custom-call | flops 9261023232 | bytes 30000000 | tf_op jit(solution)/shard_map/forward_layer/pallas_call | solution.py:611
  396.0 1.3 collective-permute-start.2
  397.3 0.8 slice_bitcast_fusion.refs_0_
  399.6 73.9 %forward_layer.5 = (bf16[128,1536]{1,0:T(8,128)(2,1)}, bf16[1536,128]{1,0:T(8,128)(2,1)}, bf16[4,2,512,128]{3,2,1,0:T(8,128)(2,1)}, bf16[1536,128]{1,0:T(8,128)(...) custom-call(bf16[128,1536]{1,0:T(8,128)(2,1)} %copy-done.9, ...), custom_call_target="tpu_custom_call", output_to_operand_aliasing={{8}: (16, {})} | custom-call | flops 9261023232 | bytes 30000000 | tf_op jit(solution)/shard_map/forward_layer/pallas_call | solution.py:611
  473.6 1.3 select_bitcast_fusion.2
  474.9 11.2 %backward_layer.3 = (f32[128,1536]{1,0:T(8,128)}, bf16[128,1536]{1,0:T(8,128)(2,1)}, bf16[4,640,128]{2,1,0:T(8,128)(2,1)}, bf16[128,1536]{1,0:T(8,128)(2,1)}, bf...) custom-call(bf16[128,1536]{1,0:T(8,128)(2,1)} %slice_bitcast_fusion., ...), custom_call_target="tpu_custom_call", output_to_operand_aliasing={{7}: (21, {})} | custom-call | flops 15703474176 | bytes 40000000 | tf_op jit(solution)/shard_map/backward_layer/pallas_call | solution.py:1016
  486.2 1.4 collective-permute-start.3
  487.8 108.1 %collective-permute-done.3 = bf16[128,1536]{1,0:T(8,128)(2,1)S(1)} collective-permute-done((bf16[128,1536]{1,0:T(8,128)(2,1)}, bf16[128,1536]{1,0:T(8,128)(2,1)S(1)}, u32[]{:S(2)}, u32[]{:S(2)}) %collective-permute-start.3) | collective-permute-done | bytes 393248 | tf_op jit(solution)/shard_map/ppermute | solution.py:63
  595.9 0.8 bitcast_select_fusion.refs_0_
  596.7 85.2 %backward_layer.4 = (f32[128,1536]{1,0:T(8,128)}, bf16[128,1536]{1,0:T(8,128)(2,1)}, bf16[4,640,128]{2,1,0:T(8,128)(2,1)}, bf16[128,1536]{1,0:T(8,128)(2,1)}, bf...) custom-call(bf16[128,1536]{1,0:T(8,128)(2,1)} %bitcast_select_fusion, ...), custom_call_target="tpu_custom_call", output_to_operand_aliasing={{7}: (27, {})} | custom-call | flops 15703474176 | bytes 40000000 | tf_op jit(solution)/shard_map/backward_layer/pallas_call | solution.py:1016
  682.0 1.3 collective-permute-start.4
  683.3 0.9 maximum_bitcast_fusion.1
  684.2 1.0 fusion.17
  686.6 81.2 %backward_layer.5 = (f32[128,1536]{1,0:T(8,128)}, bf16[128,1536]{1,0:T(8,128)(2,1)}, bf16[4,640,128]{2,1,0:T(8,128)(2,1)}, bf16[128,1536]{1,0:T(8,128)(2,1)}, bf...) custom-call(bf16[128,1536]{1,0:T(8,128)(2,1)} %copy-done.29, ...), custom_call_target="tpu_custom_call", output_to_operand_aliasing={{7}: (20, {})} | custom-call | flops 15703474176 | bytes 40000000 | tf_op jit(solution)/shard_map/backward_layer/pallas_call | solution.py:1016
  767.8 1.0 fusion.15
  771.0 1.4 broadcast_select_fusion.1
  772.4 2.2 convolution_convert_fusion
  774.6 2.6 dynamic-slice_bitcast_fusion.2
  777.2 2.3 copy-done
  779.5 25.6 %collective-permute-start.7 = (bf16[1536,640]{0,1:T(8,128)(2,1)}, bf16[1536,640]{0,1:T(8,128)(2,1)}, u32[]{:S(2)}, u32[]{:S(2)}) collective-permute-start(bf16[1536,640]{0,1:T(8,128)(2,1)} %get-tuple-element.163), channel_id=1, source_target_pairs={{0,3},{1,0},{2,1},{3,2},{4,7},{5,4},{6,5},{7,6},{8,11},{9,8},{10,9... | collective-permute-start | bytes 5898248 | tf_op jit(solution)/shard_map/ppermute | solution.py:51
  806.1 1.4 convolution_convert_fusion.1
  807.6 1.9 dynamic-slice_bitcast_fusion.5
  809.4 1.0 copy-done.1
  810.4 1.4 collective-permute-start.15
  811.8 2.5 collective-permute-start.14
  814.3 141.1 %expert_weights.1 = (f32[3,1536,512]{2,1,0:T(8,128)}, f32[3,1536,512]{2,1,0:T(8,128)}, f32[3,512,1536]{2,1,0:T(8,128)}) custom-call(bf16[2048,1664]{1,0:T(8,128)(2,1)} %bitcast.138, bf16[2048,1664]{1,0:T(8,128)(2,1)} %bitcast.173, bf16[2048,1536]{1,0:T(8,128)(2,1)} %bitcast.178, bf16[2048,1536]{1,0:T(8,128)(2,1)} %bitcast.177, ...), custom_call_target="tpu_custom_call" | custom-call | flops 115964116992 | bytes 117964800 | tf_op jit(solution)/shard_map/expert_weights/pallas_call | solution.py:1148
  955.6 2.3 fusion.5
  958.0 1.5 collective-permute-start.19
  960.3 4.5 collective-permute-done.19
  965.3 1.2 maximum_bitcast_fusion
  967.9 6.3 collective-permute-done.18
  974.3 0.9 bitcast_dynamic-update-slice_fusion.5
  975.2 2.2 collective-permute-start.20
  977.4 13.5 %collective-permute-done.5 = bf16[1536,640]{0,1:T(8,128)(2,1)} collective-permute-done((bf16[1536,640]{0,1:T(8,128)(2,1)}, bf16[1536,640]{0,1:T(8,128)(2,1)}, u32[]{:S(2)}, u32[]{:S(2)}) %collective-permute-start.5) | collective-permute-done | bytes 1966112 | tf_op jit(solution)/shard_map/ppermute | solution.py:51
  990.8 4.3 fusion.2
  995.4 2.2 collective-permute-start.9
  997.6 1.4 collective-permute-start.8
  999.0 1.5 fusion.43
  1001.2 3.0 collective-permute-done.10
  1004.2 16.0 %collective-permute-done.9 = bf16[384,640]{0,1:T(8,128)(2,1)S(1)} collective-permute-done((bf16[384,640]{0,1:T(8,128)(2,1)S(1)}, bf16[384,640]{0,1:T(8,128)(2,1)S(1)}, u32[]{:S(2)}, u32[]{:S(2)}) %collective-permute-start.9) | collective-permute-done | bytes 491552 | tf_op jit(solution)/shard_map/ppermute | solution.py:51
  1020.4 1.1 bitcast_dynamic-update-slice_fusion.2
  1021.5 1.3 copy-done.2
  1022.8 1.0 copy.48
  1024.5 7.4 dynamic_update_slice.33
  1031.9 1.5 collective-permute-start.12
  1033.7 2.0 reshape.259
  1035.7 2.9 collective-permute-start.13
  1038.6 1.9 bitcast_dynamic-update-slice_fusion.1
  1041.1 1.9 bitcast_dynamic-update-slice_fusion
  1043.0 4.8 copy.45
  1047.8 0.9 copy.46
  1048.6 18.3 %dynamic_update_slice.29 = bf16[4,384,640]{2,0,1:T(4,128)(2,1)} dynamic-update-slice(bf16[4,384,640]{2,0,1:T(4,128)(2,1)} %copy.45, bf16[1,384,640]{2,0,1:T(2,128)(2,1)S(1)} %copy.46, s32[]{:T(128)S(6)} %select_n.362, s32[]{:T(128)} %constant.148.clone.1, s32[]{:T(128)} %constant.148.clone.1) | dynamic-update-slice | bytes 983044 | tf_op jit(solution)/shard_map/jit(dynamic_update_index_in_dim)/dynamic_update_slice | solution.py:1425
  1066.9 1.6 convert_bitcast_fusion.1
  1068.5 2.1 convert_bitcast_fusion.2
  1070.6 2.0 reshape.255
  1072.5 2.3 reshape.256
  1074.9 1.2 reshape.257
  (126 shorter events, 19.7 us)
Async XLA Ops:
  7.2 151.8 %copy-start.3 = (bf16[2,128,1536]{2,1,0:T(8,128)(2,1)S(1)}, bf16[2,128,1536]{2,1,0:T(8,128)(2,1)}, u32[]{:S(2)}) copy-start(bf16[2,128,1536]{2,1,0:T(8,128)(2,1)} %param.14) | copy-start | bytes 2359300
  7.2 959.3 %all-reduce.3.cloned.1.call-start = ((), (), s32[]{:S(2)}) async-start(), calls=%async_computation | async-start | bytes 196608 | tf_op jit(solution)/shard_map/psum | solution.py:1451
  8.8 151.0 %copy-start.27 = (s32[2,512]{1,0:T(2,128)S(1)}, s32[2,512]{1,0:T(2,128)}, u32[]{:S(2)}) copy-start(s32[2,512]{1,0:T(2,128)} %param.16) | copy-start | bytes 12292
  8.8 151.0 %copy-start.22 = (s32[1,2,128,8]{2,3,1,0:T(8,128)S(1)}, s32[1,2,128,8]{2,3,1,0:T(8,128)}, u32[]{:S(2)}) copy-start(s32[1,2,128,8]{2,3,1,0:T(8,128)} %param.17) | copy-start | bytes 24580
  157.6 6.1 collective-permute-start
  163.7 0.6 copy-start.28
  215.1 96.6 %collective-permute-start.1 = (bf16[128,1536]{1,0:T(8,128)(2,1)}, bf16[128,1536]{1,0:T(8,128)(2,1)S(1)}, u32[]{:S(2)}, u32[]{:S(2)}) collective-permute-start(bf16[128,1536]{1,0:T(8,128)(2,1)} %get-tuple-element.79), channel_id=1, source_target_pairs={{0,16},{1,17},{2,18},{3,19},{4,20},{5,21},{6,22},{7,23},{8,24},{9,... | collective-permute-start | bytes 1179656 | tf_op jit(solution)/shard_map/ppermute | solution.py:63
  312.5 84.8 %copy-start.4 = (bf16[2,128,1536]{2,1,0:T(8,128)(2,1)S(1)}, bf16[2,128,1536]{2,1,0:T(8,128)(2,1)}, u32[]{:S(2)}) copy-start(bf16[2,128,1536]{2,1,0:T(8,128)(2,1)} %param.15) | copy-start | bytes 2359300
  396.0 2.8 collective-permute-start.2
  398.8 0.7 copy-start.9
  399.6 73.9 %copy-start.12 = (bf16[128,1536]{1,0:T(8,128)(2,1)S(1)}, bf16[128,1536]{1,0:T(8,128)(2,1)}, u32[]{:S(2)}) copy-start(bf16[128,1536]{1,0:T(8,128)(2,1)} %get-tuple-element.79) | copy-start | bytes 1179652
  399.6 73.9 %copy-start.19 = (bf16[128,1536]{1,0:T(8,128)(2,1)S(1)}, bf16[128,1536]{1,0:T(8,128)(2,1)}, u32[]{:S(2)}) copy-start(bf16[128,1536]{1,0:T(8,128)(2,1)} %get-tuple-element.81) | copy-start | bytes 1179652
  474.9 12.7 %copy-start.11 = (bf16[128,1536]{1,0:T(8,128)(2,1)S(1)}, bf16[128,1536]{1,0:T(8,128)(2,1)}, u32[]{:S(2)}) copy-start(bf16[128,1536]{1,0:T(8,128)(2,1)} %get-tuple-element.118) | copy-start | bytes 1179652
  474.9 12.7 %copy-start.17 = (bf16[128,1536]{1,0:T(8,128)(2,1)S(1)}, bf16[128,1536]{1,0:T(8,128)(2,1)}, u32[]{:S(2)}) copy-start(bf16[128,1536]{1,0:T(8,128)(2,1)} %get-tuple-element.119) | copy-start | bytes 1179652
  486.2 1.6 copy-start.10
  486.2 1.6 copy-start.16
  486.2 1.6 copy-start.18
  486.2 109.7 %collective-permute-start.3 = (bf16[128,1536]{1,0:T(8,128)(2,1)}, bf16[128,1536]{1,0:T(8,128)(2,1)S(1)}, u32[]{:S(2)}, u32[]{:S(2)}) collective-permute-start(bf16[128,1536]{1,0:T(8,128)(2,1)} %get-tuple-element.91), channel_id=1, source_target_pairs={{16,0},{17,1},{18,2},{19,3},{20,4},{21,5},{22,6},{23,7},{24,8},{25... | collective-permute-start | bytes 1179656 | tf_op jit(solution)/shard_map/ppermute | solution.py:63
  596.7 87.5 %copy-start.21 = (bf16[128,128]{1,0:T(8,128)(2,1)S(1)}, bf16[128,128]{1,0:T(8,128)(2,1)}, u32[]{:S(2)}) copy-start(bf16[128,128]{1,0:T(8,128)(2,1)} %get-tuple-element.107) | copy-start | bytes 98308
  682.0 3.8 collective-permute-start.4
  685.8 0.7 copy-start.29
  686.6 81.3 %copy-start.20 = (bf16[128,128]{1,0:T(8,128)(2,1)S(1)}, bf16[128,128]{1,0:T(8,128)(2,1)}, u32[]{:S(2)}) copy-start(bf16[128,128]{1,0:T(8,128)(2,1)} %get-tuple-element.106) | copy-start | bytes 98308
  686.6 82.2 %copy-start.24 = (f32[1,1536]{1,0:T(1,128)S(1)}, f32[1,1536]{1,0:T(1,128)}, u32[]{:S(2)}) copy-start(f32[1,1536]{1,0:T(1,128)} %get-tuple-element.111) | copy-start | bytes 18436
  686.6 82.2 %copy-start.26 = (f32[1,1536]{1,0:T(1,128)S(1)}, f32[1,1536]{1,0:T(1,128)}, u32[]{:S(2)}) copy-start(f32[1,1536]{1,0:T(1,128)} %get-tuple-element.110) | copy-start | bytes 18436
  686.6 83.0 %copy-start.23 = (f32[1,1536]{1,0:T(1,128)S(1)}, f32[1,1536]{1,0:T(1,128)}, u32[]{:S(2)}) copy-start(f32[1,1536]{1,0:T(1,128)} %get-tuple-element.109) | copy-start | bytes 18436
  686.6 83.0 %copy-start.25 = (f32[1,1536]{1,0:T(1,128)S(1)}, f32[1,1536]{1,0:T(1,128)}, u32[]{:S(2)}) copy-start(f32[1,1536]{1,0:T(1,128)} %get-tuple-element.108) | copy-start | bytes 18436
  686.6 84.4 %copy-start.8 = (bf16[4,640,128]{2,1,0:T(8,128)(2,1)S(1)}, bf16[4,640,128]{2,1,0:T(8,128)(2,1)}, u32[]{:S(2)}) copy-start(bf16[4,640,128]{2,1,0:T(8,128)(2,1)} %get-tuple-element.116) | copy-start | bytes 1966084
  774.6 4.9 copy-start
  774.6 31.1 %copy-start.13 = (bf16[128,1536]{1,0:T(8,128)(2,1)S(1)}, bf16[128,1536]{1,0:T(8,128)(2,1)}, u32[]{:S(2)}) copy-start(bf16[128,1536]{1,0:T(8,128)(2,1)} %get-tuple-element.122) | copy-start | bytes 1179652
  774.6 31.1 %copy-start.14 = (bf16[128,1536]{1,0:T(8,128)(2,1)S(1)}, bf16[128,1536]{1,0:T(8,128)(2,1)}, u32[]{:S(2)}) copy-start(bf16[128,1536]{1,0:T(8,128)(2,1)} %get-tuple-element.121) | copy-start | bytes 1179652
  774.6 31.1 %copy-start.15 = (bf16[128,1536]{1,0:T(8,128)(2,1)S(1)}, bf16[128,1536]{1,0:T(8,128)(2,1)}, u32[]{:S(2)}) copy-start(bf16[128,1536]{1,0:T(8,128)(2,1)} %get-tuple-element.123) | copy-start | bytes 1179652
  779.5 197.9 %collective-permute-start.7 = (bf16[1536,640]{0,1:T(8,128)(2,1)}, bf16[1536,640]{0,1:T(8,128)(2,1)}, u32[]{:S(2)}, u32[]{:S(2)}) collective-permute-start(bf16[1536,640]{0,1:T(8,128)(2,1)} %get-tuple-element.163), channel_id=1, source_target_pairs={{0,3},{1,0},{2,1},{3,2},{4,7},{5,4},{6,5},{7,6},{8,11},{9,8},{10,9... | collective-permute-start | bytes 5898248 | tf_op jit(solution)/shard_map/ppermute | solution.py:51
  805.1 172.3 %collective-permute-start.6 = (bf16[1536,640]{0,1:T(8,128)(2,1)}, bf16[1536,640]{0,1:T(8,128)(2,1)}, u32[]{:S(2)}, u32[]{:S(2)}) collective-permute-start(bf16[1536,640]{0,1:T(8,128)(2,1)} %get-tuple-element.164), channel_id=1, source_target_pairs={{0,2},{1,3},{2,0},{3,1},{4,6},{5,7},{6,4},{7,5},{8,10},{9,11},{10,... | collective-permute-start | bytes 5898248 | tf_op jit(solution)/shard_map/ppermute | solution.py:51
  807.6 2.8 copy-start.1
  810.4 145.0 %collective-permute-start.16 = (bf16[1536,384]{0,1:T(8,128)(2,1)}, bf16[1536,384]{0,1:T(8,128)(2,1)S(1)}, u32[]{:S(2)}, u32[]{:S(2)}) collective-permute-start(bf16[1536,384]{0,1:T(8,128)(2,1)} %get-tuple-element.166), channel_id=1, source_target_pairs={{0,3},{1,0},{2,1},{3,2},{4,7},{5,4},{6,5},{7,6},{8,11},{9,8},{10,9... | collective-permute-start | bytes 3538952 | tf_op jit(solution)/shard_map/ppermute | solution.py:51
  810.4 145.1 %collective-permute-start.15 = (bf16[1536,384]{0,1:T(8,128)(2,1)}, bf16[1536,384]{0,1:T(8,128)(2,1)S(1)}, u32[]{:S(2)}, u32[]{:S(2)}) collective-permute-start(bf16[1536,384]{0,1:T(8,128)(2,1)} %get-tuple-element.167), channel_id=1, source_target_pairs={{0,2},{1,3},{2,0},{3,1},{4,6},{5,7},{6,4},{7,5},{8,10},{9,11},{10,... | collective-permute-start | bytes 3538952 | tf_op jit(solution)/shard_map/ppermute | solution.py:51
  811.8 143.7 %collective-permute-start.14 = (bf16[1536,384]{0,1:T(8,128)(2,1)S(1)}, bf16[1536,384]{0,1:T(8,128)(2,1)}, u32[]{:S(2)}, u32[]{:S(2)}) collective-permute-start(bf16[1536,384]{0,1:T(8,128)(2,1)S(1)} %get-tuple-element.165), channel_id=1, source_target_pairs={{0,1},{1,2},{2,3},{3,0},{4,5},{5,6},{6,7},{7,4},{8,9},{9,10},{10,1... | collective-permute-start | bytes 3538952 | tf_op jit(solution)/shard_map/ppermute | solution.py:51
  955.4 35.4 %collective-permute-start.5 = (bf16[1536,640]{0,1:T(8,128)(2,1)}, bf16[1536,640]{0,1:T(8,128)(2,1)}, u32[]{:S(2)}, u32[]{:S(2)}) collective-permute-start(bf16[1536,640]{0,1:T(8,128)(2,1)} %get-tuple-element.162), channel_id=1, source_target_pairs={{0,1},{1,2},{2,3},{3,0},{4,5},{5,6},{6,7},{7,4},{8,9},{9,10},{10,1... | collective-permute-start | bytes 5898248 | tf_op jit(solution)/shard_map/ppermute | solution.py:51
  955.5 3.9 copy-start.7
  957.8 1.6 copy-start.5
  957.8 1.6 copy-start.6
  958.0 6.8 collective-permute-start.19
  959.6 14.5 %collective-permute-start.18 = (bf16[384,384]{0,1:T(8,128)(2,1)S(1)}, bf16[384,384]{0,1:T(8,128)(2,1)S(1)}, u32[]{:S(2)}, u32[]{:S(2)}) collective-permute-start(bf16[384,384]{0,1:T(8,128)(2,1)S(1)} %get-tuple-element.177), channel_id=1, source_target_pairs={{0,8},{4,12},{8,0},{12,4},{1,9},{5,13},{9,1},{13,5},{2,10},{6,14},... | collective-permute-start | bytes 884744 | tf_op jit(solution)/shard_map/ppermute | solution.py:51
  964.8 9.4 collective-permute-start.17
  975.2 25.9 %collective-permute-start.20 = (bf16[384,384]{0,1:T(8,128)(2,1)}, bf16[384,384]{0,1:T(8,128)(2,1)S(1)}, u32[]{:S(2)}, u32[]{:S(2)}) collective-permute-start(bf16[384,384]{0,1:T(8,128)(2,1)} %get-tuple-element.159), channel_id=1, source_target_pairs={{0,1},{1,2},{2,3},{3,0},{4,5},{5,6},{6,7},{7,4},{8,9},{9,10},{10,1... | collective-permute-start | bytes 884744 | tf_op jit(solution)/shard_map/ppermute | solution.py:51
  995.3 8.9 collective-permute-start.10
  995.4 24.8 %collective-permute-start.9 = (bf16[384,640]{0,1:T(8,128)(2,1)S(1)}, bf16[384,640]{0,1:T(8,128)(2,1)S(1)}, u32[]{:S(2)}, u32[]{:S(2)}) collective-permute-start(bf16[384,640]{0,1:T(8,128)(2,1)S(1)} %get-tuple-element.172), channel_id=1, source_target_pairs={{0,8},{4,12},{8,0},{12,4},{1,9},{5,13},{9,1},{13,5},{2,10},{6,14},... | collective-permute-start | bytes 1474568 | tf_op jit(solution)/shard_map/ppermute | solution.py:51
  997.6 22.6 %collective-permute-start.8 = (bf16[384,640]{0,1:T(8,128)(2,1)S(1)}, bf16[384,640]{0,1:T(8,128)(2,1)S(1)}, u32[]{:S(2)}, u32[]{:S(2)}) collective-permute-start(bf16[384,640]{0,1:T(8,128)(2,1)S(1)} %get-tuple-element.170), channel_id=1, source_target_pairs={{0,4},{4,8},{8,12},{12,0},{1,5},{5,9},{9,13},{13,1},{2,6},{6,10},{... | collective-permute-start | bytes 1474568 | tf_op jit(solution)/shard_map/ppermute | solution.py:51
  1000.5 22.3 %collective-permute-start.21 = (bf16[384,384]{0,1:T(8,128)(2,1)}, bf16[384,384]{0,1:T(8,128)(2,1)S(1)}, u32[]{:S(2)}, u32[]{:S(2)}) collective-permute-start(bf16[384,384]{0,1:T(8,128)(2,1)} %get-tuple-element.159), channel_id=1, source_target_pairs={{0,2},{1,3},{2,0},{3,1},{4,6},{5,7},{6,4},{7,5},{8,10},{9,11},{10,... | collective-permute-start | bytes 884744 | tf_op jit(solution)/shard_map/ppermute | solution.py:51
  1001.1 22.7 %collective-permute-start.22 = (bf16[384,384]{0,1:T(8,128)(2,1)}, bf16[384,384]{0,1:T(8,128)(2,1)S(1)}, u32[]{:S(2)}, u32[]{:S(2)}) collective-permute-start(bf16[384,384]{0,1:T(8,128)(2,1)} %get-tuple-element.159), channel_id=1, source_target_pairs={{0,3},{1,0},{2,1},{3,2},{4,7},{5,4},{6,5},{7,6},{8,11},{9,8},{10,9... | collective-permute-start | bytes 884744 | tf_op jit(solution)/shard_map/ppermute | solution.py:51
  1021.5 1.3 copy-start.2
  1022.7 15.9 %collective-permute-start.11 = (bf16[384,640]{0,1:T(8,128)(2,1)}, bf16[384,640]{0,1:T(8,128)(2,1)}, u32[]{:S(2)}, u32[]{:S(2)}) collective-permute-start(bf16[384,640]{0,1:T(8,128)(2,1)} %get-tuple-element.161), channel_id=1, source_target_pairs={{0,1},{1,2},{2,3},{3,0},{4,5},{5,6},{6,7},{7,4},{8,9},{9,10},{10,1... | collective-permute-start | bytes 1474568 | tf_op jit(solution)/shard_map/ppermute | solution.py:51
  1031.9 9.2 collective-permute-start.12
  1035.7 12.1 %collective-permute-start.13 = (bf16[384,640]{0,1:T(8,128)(2,1)}, bf16[384,640]{0,1:T(8,128)(2,1)S(1)}, u32[]{:S(2)}, u32[]{:S(2)}) collective-permute-start(bf16[384,640]{0,1:T(8,128)(2,1)} %get-tuple-element.161), channel_id=1, source_target_pairs={{0,3},{1,0},{2,1},{3,2},{4,7},{5,4},{6,5},{7,6},{8,11},{9,8},{10,9... | collective-permute-start | bytes 1474568 | tf_op jit(solution)/shard_map/ppermute | solution.py:51
Sparse Core Ops, SparseCore 0:
  771.1 150.8 all-reduce.2

commit v2 on v1

--- a/solution.py
+++ b/solution.py
@@ -20,6 +20,9 @@
 LOW = 64
 SCALE = HD ** (-0.5)
 VMEM = 60 * 1024 * 1024
+PREPARED = 8192
+SMALL = 24
+LARGE = 63 * 1024 * 1024
 
 F32 = jnp.float32
 BF16 = jnp.bfloat16
@@ -123,187 +126,280 @@
 
 def relay_sems(blocks, members):
     line = (2, members - 1)
-    plane = (members - 1, blocks - 2)
-    return [pltpu.SemaphoreType.DMA(dims) for dims in (line, line, plane, plane, (1,))]
+    plane = (members - 1, blocks - 1)
+    return [pltpu.SemaphoreType.DMA(dims) for dims in (line, line, plane, plane, (blocks,))]
 
 
 class Relay:
-    def __init__(self, near, dest, sems):
-        self.near, self.dest = near, dest
+    def __init__(self, section, stages, near, dest, pair, sems):
+        self.section, self.near, self.dest = section, near, dest
+        self.keeps, self.lines, self.planes = ("keep" in stages, "line" in stages, "plane" in stages)
         self.members, self.blocks = dest.shape[:2]
+        self.me, self.place = lax.axis_index("expert"), lax.axis_index("dp")
+        self.reach = self.blocks - 1 if pair else self.blocks
+        self.sent = range(2 if pair else 1)
         self.line_send, self.line_recv, self.plane_send, self.plane_recv, self.near_sem = sems
 
     def line(self, which, k):
         slot = which * (self.blocks - 1)
+        target = self.dest.at[self.place, partner(self.me, slot)]
         return send(
-            self.near.at[slot],
-            self.dest.at[k, slot],
+            self.near.at[slot] if self.keeps else target,
+            target,
             self.line_send.at[which, k - 1],
             self.line_recv.at[which, k - 1],
             line_peers(self.members)[k - 1],
         )
 
     def plane(self, k, d):
+        block = self.dest.at[lax.rem(self.place + self.members - k, self.members), self.me]
         return send(
-            self.dest.at[k, 0],
-            self.dest.at[k, d],
+            block,
+            block,
             self.plane_send.at[k - 1, d - 1],
             self.plane_recv.at[k - 1, d - 1],
             plane_peers(self.blocks)[d - 1],
         )
 
     def start(self, which):
-        for k in range(1, self.members):
-            self.line(which, k).start()
+        if self.lines and which in self.sent:
+            for k in range(1, self.members):
+                self.line(which, k).start()
+
+    def copies(self):
+        return [
+            pltpu.make_async_copy(
+                self.near.at[d],
+                self.dest.at[self.place, partner(self.me, d)],
+                self.near_sem.at[d],
+            )
+            for d in range(self.blocks)
+        ]
 
     def keep(self):
-        return pltpu.make_async_copy(self.near, self.dest.at[0], self.near_sem.at[0])
+        if self.keeps:
+            for copy in self.copies():
+                copy.start()
+
+    def open(self):
+        if not self.keeps:
+            self.start(0)
+            self.start(1)
 
     def forward(self):
-        for k in range(1, self.members):
-            self.line(0, k).wait_recv()
-            for d in range(1, self.blocks - 1):
-                self.plane(k, d).start()
+        if self.planes:
+            for k in range(1, self.members):
+                if self.lines:
+                    self.line(0, k).wait_recv()
+                for d in range(1, self.reach):
+                    self.plane(k, d).start()
 
     def finish(self):
         for k in range(1, self.members):
-            self.line(1, k).wait_recv()
-            for which in range(2):
-                self.line(which, k).wait_send()
-            for d in range(1, self.blocks - 1):
-                self.plane(k, d).wait()
-        self.keep().wait()
-
-
-def gather_kernel(section, chained, *refs):
-    q_ref, k_ref, v_ref, o_ref, router_ref = refs[:5]
-    refs = refs[9:] if chained else refs[5:]
-    inner, out, router, local_sem, line_sem, plane_sem, router_sem, own_sem = refs
+            if self.lines:
+                for which in self.sent:
+                    if which or not self.planes:
+                        self.line(which, k).wait_recv()
+                    self.line(which, k).wait_send()
+            if self.planes:
+                for d in range(1, self.reach):
+                    self.plane(k, d).wait()
+        if self.keeps:
+            for copy in self.copies():
+                copy.wait()
+
+
+def make_relays(tasks, near, names, dests, take):
+    return [
+        Relay(
+            section,
+            stages,
+            near if "keep" in stages else None,
+            dests[names.index(name)].at[batch],
+            pair,
+            take(5),
+        )
+        for section, stages, name, batch, pair in tasks
+    ]
+
+
+def run_relays(relays, step, sections=None, outside=False):
+    for relay in relays:
+        if sections is None or (relay.section in sections) != outside:
+            in_section(relay.section)(lambda relay=relay: step(relay))
+
+
+def relay_arrays(tasks, arrays):
+    names = sorted({task[2] for task in tasks}, key=lambda name: arrays[name][0] is None)
+    held = [arrays[name][0] for name in names if arrays[name][0] is not None]
+    return names, held, [arrays[name][1] for name in names]
+
+
+def enter(sections, relays, blocks):
+    for section in range(lax.axis_size("section")):
+        peers = []
+        own = [relay for relay in relays if relay.section == section]
+        if section in sections or any(relay.planes for relay in own):
+            peers = plane_peers(blocks)
+        if any(relay.lines for relay in own):
+            peers = peers + line_peers(own[0].members)
+        if peers:
+            in_section(section)(lambda peers=peers: greet(peers))
+
+
+def gather_kernel(q_ref, k_ref, v_ref, o_ref, router_ref, inner, out, router, *sems):
+    local_sem, line_sem, plane_sem, router_sem, turn_sem = sems
     blocks = inner.shape[0]
     depth = q_ref.shape[0]
     members = inner.shape[1] // depth
     me = lax.axis_index("expert")
     place = lax.axis_index("dp")
+    section = lax.axis_index("section")
+    diagonal = partner(me, blocks - 1)
+    gathered = (inner, out)
+    pieces = []
+    at = 0
+    for source in (q_ref, k_ref, v_ref):
+        pieces.append((source, inner, at, source.shape[1] // blocks))
+        at += source.shape[1] // blocks
+    pieces.append((o_ref, out, 0, o_ref.shape[1] // blocks))
+    sent = [(i, me) for i in range(4)] + [(3, diagonal)] + [(i, diagonal) for i in range(3)]
 
     def rows(member):
         return pl.ds(pl.multiple_of(member * depth, depth), depth)
 
-    def local(e):
-        copies = []
-        at = 0
-        for source, target, start in (
-            (q_ref, inner, 0),
-            (k_ref, inner, q_ref.shape[1] // blocks),
-            (v_ref, inner, (q_ref.shape[1] + k_ref.shape[1]) // blocks),
-            (o_ref, out, 0),
-        ):
-            part = source.shape[1] // blocks
-            copies.append(
-                pltpu.make_async_copy(
-                    source.at[:, pl.ds(pl.multiple_of(e * part, LANES), part)],
-                    target.at[e, rows(place), pl.ds(start, part)],
-                    local_sem.at[at],
-                )
-            )
-            at += 1
-        return copies
-
-    @in_section(section)
+    def ends(i, e):
+        source, target, start, part = pieces[i]
+        return (
+            source.at[:, pl.ds(pl.multiple_of(e * part, LANES), part)],
+            target.at[e, rows(place), pl.ds(start, part)],
+        )
+
+    def line(which, k):
+        source, target = ends(*sent[which])
+        return send(
+            source,
+            target,
+            line_sem.at[0, which, k - 1],
+            line_sem.at[1, which, k - 1],
+            line_peers(members)[k - 1],
+        )
+
+    def plane(which, k, d):
+        piece = gathered[which].at[me, rows(lax.rem(place + members - k, members))]
+        return send(
+            piece,
+            piece,
+            plane_sem.at[0, which, k - 1, d - 1],
+            plane_sem.at[1, which, k - 1, d - 1],
+            plane_peers(blocks)[d - 1],
+        )
+
+    def narrow(k):
+        return send(
+            router_ref,
+            router.at[rows(place)],
+            router_sem.at[0, k - 1],
+            router_sem.at[1, k - 1],
+            line_peers(members)[k - 1],
+        )
+
+    other = (1 - section, place, me)
+    greet(plane_peers(blocks) + line_peers(members) + [other])
+
+    @in_section(1)
     def _():
-        diagonal = partner(me, blocks - 1)
-        for copy in local(me):
-            copy.start()
-        mine = pltpu.make_async_copy(router_ref, router.at[rows(place)], own_sem.at[0])
-        mine.start()
-        greet(plane_peers(blocks) + line_peers(members))
-        for copy in local(me):
-            copy.wait()
-
-        def line(which, k):
-            target, column = ((inner, me), (out, me), (out, diagonal))[which]
-            piece = target.at[column, rows(place)]
-            return send(
-                piece,
-                piece,
-                line_sem.at[0, which, k - 1],
-                line_sem.at[1, which, k - 1],
-                line_peers(members)[k - 1],
-            )
-
-        def plane(which, k, d):
-            target = (inner, out)[which]
-            piece = target.at[me, rows(lax.rem(place + members - k, members))]
-            return send(
-                piece,
-                piece,
-                plane_sem.at[0, which, k - 1, d - 1],
-                plane_sem.at[1, which, k - 1, d - 1],
-                plane_peers(blocks)[d - 1],
-            )
-
-        def narrow(k):
-            piece = router.at[rows(place)]
-            return send(
-                piece, piece, router_sem.at[0, k - 1], router_sem.at[1, k - 1], line_peers(members)[k - 1]
-            )
-
-        for which in range(2):
+        pl.semaphore_wait(turn_sem, 1)
+
+    for which in range(5):
+        for k in range(1, members):
+            line(which, k).start()
+    for k in range(1, members):
+        narrow(k).start()
+
+    @in_section(1)
+    def _():
+        for which in range(5, 8):
             for k in range(1, members):
                 line(which, k).start()
-        for d in range(1, blocks):
-            for copy in local(partner(me, d)):
-                copy.start()
-            for copy in local(partner(me, d)):
-                copy.wait()
-        mine.wait()
-        for k in range(1, members):
-            line(2, k).start()
-        for k in range(1, members):
-            narrow(k).start()
-        reach = (blocks, blocks - 1)
+
+    copies = [pltpu.make_async_copy(router_ref, router.at[rows(place)], local_sem.at[4 * blocks])]
+    for e in range(blocks):
+        for i in range(4):
+            copies.append(pltpu.make_async_copy(*ends(i, e), local_sem.at[4 * e + i]))
+    for copy in copies:
+        copy.start()
+    for k in range(1, members):
+        for which in range(3):
+            line(which, k).wait_recv()
+        for d in range(1, blocks - 1):
+            plane(0, k, d).start()
+
+        @in_section(0)
+        def _(k=k):
+            plane(0, k, blocks - 1).start()
+
+    for k in range(1, members):
+        line(3, k).wait_recv()
+        for d in range(1, blocks - 1):
+            plane(1, k, d).start()
+    for k in range(1, members):
+        line(4, k).wait_recv()
+        narrow(k).wait()
+
+    @in_section(0)
+    def _():
+        pl.semaphore_signal(
+            turn_sem, inc=1, device_id=other, device_id_type=pl.DeviceIdType.MESH
+        )
+
+    for k in range(1, members):
+        for which in range(5):
+            line(which, k).wait_send()
         for which in range(2):
-            for k in range(1, members):
-                line(which, k).wait_recv()
-                for d in range(1, reach[which]):
-                    plane(which, k, d).start()
-        for k in range(1, members):
-            line(2, k).wait_recv()
-            narrow(k).wait()
-            for which in range(3):
-                line(which, k).wait_send()
-            for which in range(2):
-                for d in range(1, reach[which]):
-                    plane(which, k, d).wait()
-
-
-def gather_weights(section, number, sources, before=None, after=None):
-    q, k, v, o, router = sources
+            for d in range(1, blocks - 1):
+                plane(which, k, d).wait()
+
+        @in_section(0)
+        def _(k=k):
+            plane(0, k, blocks - 1).wait()
+
+        @in_section(1)
+        def _(k=k):
+            for which in range(5, 8):
+                line(which, k).wait()
+
+    for copy in copies:
+        copy.wait()
+
+
+def gather_weights(number, q, k, v, o, router):
     blocks = lax.axis_size("expert")
     members = lax.axis_size("dp")
-    depth = q.shape[0] * members
+    depth = q.shape[0]
     wide = (q.shape[1] + k.shape[1] + v.shape[1]) // blocks
-    shapes = [
-        shape((blocks, depth, wide), BF16),
-        shape((blocks, depth, o.shape[1] // blocks), BF16),
-        shape((depth, LANES), BF16),
-    ]
-    chained = before is not None
+    anywhere = pl.BlockSpec(memory_space=pl.ANY)
     return pl.pallas_call(
-        functools.partial(gather_kernel, section, chained),
-        in_specs=[pl.BlockSpec(memory_space=pl.ANY)] * (9 if chained else 5),
-        out_specs=[pl.BlockSpec(memory_space=pl.ANY)] * 3,
-        out_shape=shapes,
+        gather_kernel,
+        in_specs=[whole()] * 5,
+        out_specs=[anywhere] * 3,
+        out_shape=[
+            shape((blocks, depth * members, wide), BF16),
+            shape((blocks, depth * members, o.shape[1] // blocks), BF16),
+            shape((depth * members, LANES), BF16),
+        ],
         scratch_shapes=[
-            pltpu.SemaphoreType.DMA((4,)),
-            pltpu.SemaphoreType.DMA((2, 3, members - 1)),
+            pltpu.SemaphoreType.DMA((1 + 4 * blocks,)),
+            pltpu.SemaphoreType.DMA((2, 8, members - 1)),
             pltpu.SemaphoreType.DMA((2, 2, members - 1, blocks - 1)),
             pltpu.SemaphoreType.DMA((2, members - 1)),
-            pltpu.SemaphoreType.DMA((1,)),
+            pltpu.SemaphoreType.REGULAR,
         ],
-        input_output_aliases={5: 0, 6: 1, 7: 2} if chained else {},
-        compiler_params=pltpu.CompilerParams(collective_id=number, has_side_effects=True),
+        compiler_params=pltpu.CompilerParams(
+            vmem_limit_bytes=VMEM, collective_id=number, has_side_effects=True
+        ),
         name="gather_weights",
-    )(*sources, *((*before, after) if chained else ()))
+    )(q, k, v, o, router)
 
 
 def group_of(ref, group):
@@ -332,37 +428,20 @@
         ).astype(BF16)
 
 
-def enter(sections, relays, blocks):
-    for section in range(lax.axis_size("section")):
-        peers = []
-        own = [relay for at, relay in relays if at == section]
-        if section in sections or own:
-            peers = plane_peers(blocks)
-        if own:
-            peers = peers + line_peers(own[0].members)
-        if peers:
-            in_section(section)(lambda peers=peers: greet(peers))
-
-
-def open_relay(relay):
-    relay.keep().start()
-    relay.start(0)
-    relay.start(1)
-
-
-def forward_kernel(sections, tasks, fresh, reused, groups_of_blocks, *refs):
-    sources = [refs[14 + i] for i in range(len(tasks))]
-    inputs = refs[:14]
-    at = 14 + len(tasks) + reused
-    outputs = refs[at : at + 8]
-    dests = refs[at + 8 : at + 8 + fresh + reused]
-    at = at + 8 + fresh + reused
-    scratch = refs[at : at + 23]
-    relay_refs = refs[at + 23 :]
-    relays = [
-        (section, Relay(sources[i], dests[dest], relay_refs[5 * i : 5 * i + 5]))
-        for i, (section, dest) in enumerate(tasks)
-    ]
+def forward_kernel(sections, tasks, names, held, groups_of_blocks, *refs):
+    refs = list(refs)
+
+    def take(count):
+        taken = refs[:count]
+        del refs[:count]
+        return taken
+
+    inputs = take(14)
+    take(held)
+    outputs = take(8)
+    dests = take(len(names))
+    scratch = take(23)
+    relays = make_relays(tasks, scratch[11], names, dests, take)
     (
     entry_ref,
     gain_one_ref,
@@ -422,8 +501,7 @@
     part = width // blocks
 
     enter(sections, relays, blocks)
-    for section, relay in relays:
-        in_section(section)(lambda relay=relay: open_relay(relay))
+    run_relays(relays, Relay.open)
 
     @in_sections(sections)
     def _():
@@ -482,6 +560,7 @@
         for copy in kv_copies:
             copy.wait()
         save(kv, kv_out)
+        run_relays(relays, Relay.forward, sections)
 
         def one(group, carry):
             query_group = group_of(query, group)
@@ -498,9 +577,6 @@
             return carry
 
         lax.fori_loop(0, kv.shape[2] // HD, one, 0)
-        for section, relay in relays:
-            if section in sections:
-                in_section(section)(relay.forward)
         save(att, att_out)
         save(lse, lse_out)
         attended = att[...].T
@@ -561,6 +637,7 @@
                 else:
                     own[...] = middle[...] + piece
         save(payload, payload_out)
+        run_relays(relays, Relay.keep, sections)
         total = own[...]
         for d in range(1, blocks):
             back_copies[d - 1].wait_recv()
@@ -573,10 +650,8 @@
         for copy in saves:
             copy.wait()
 
-    for section, relay in relays:
-        if section not in sections:
-            in_section(section)(relay.forward)
-        in_section(section)(relay.finish)
+    run_relays(relays, Relay.forward, sections, outside=True)
+    run_relays(relays, Relay.finish)
 
 
 def forward_layer(
@@ -592,14 +667,14 @@
     chosen,
     pick,
     weights,
-    tasks=(),
-    fresh=0,
-    reused=(),
+    tasks,
+    arrays,
 ):
     inner, out, gate_all, up_all, down_all = weights
     rows, width = entry.shape
     blocks = inner.shape[0]
     members = lax.axis_size("dp")
+    names, before, dests = relay_arrays(tasks, arrays)
     local, _, hidden = gate_all.shape
     keys = KVH * HD
     flops = 2 * rows * width * (H + 2 * KVH) * HD + 4 * rows * rows * blocks * H * HD
@@ -607,18 +682,12 @@
     groups_of_blocks = [[0], list(range(1, blocks - 1)), [blocks - 1]]
     pair = (2, blocks - 1)
     anywhere = pl.BlockSpec(memory_space=pl.ANY)
-    first_reused = 14 + len(tasks)
     results = pl.pallas_call(
         functools.partial(
-            forward_kernel,
-            sections,
-            [(section, dest) for section, _, dest in tasks],
-            fresh,
-            len(reused),
-            groups_of_blocks,
+            forward_kernel, sections, tasks, names, len(before), groups_of_blocks
         ),
-        in_specs=[whole()] * 9 + [anywhere] * (5 + len(tasks) + len(reused)),
-        out_specs=[anywhere] * (8 + len(reused) + fresh),
+        in_specs=[whole()] * 9 + [anywhere] * (5 + len(before)),
+        out_specs=[anywhere] * (8 + len(names)),
         out_shape=[
             shape((rows, width), BF16),
             shape((H * HD, rows), BF16),
@@ -628,8 +697,8 @@
             shape((rows, width), F32),
             shape((blocks, rows, width + LANES), BF16),
             shape((rows, width), BF16),
-        ]
-        + [shape((members, blocks, rows, width + LANES), BF16)] * (len(reused) + fresh),
+            *dests,
+        ],
         scratch_shapes=[
             pltpu.VMEM(inner.shape, BF16),
             pltpu.VMEM(out.shape, BF16),
@@ -656,7 +725,7 @@
             pltpu.SemaphoreType.DMA((8,)),
         ]
         + relay_sems(blocks, members) * len(tasks),
-        input_output_aliases={first_reused + i: 8 + i for i in range(len(reused))},
+        input_output_aliases={14 + i: 8 + i for i in range(len(before))},
         compiler_params=pltpu.CompilerParams(
             vmem_limit_bytes=VMEM, collective_id=number, has_side_effects=True
         ),
@@ -677,10 +746,9 @@
         gate_all,
         up_all,
         down_all,
-        *[payloads for _, payloads, _ in tasks],
-        *reused,
+        *before,
     )
-    return results[:8], results[8:]
+    return results[:8], dict(zip(names, results[8:]))
 
 
 def activation(gate, up, hidden_grad):
@@ -702,7 +770,7 @@
 HELD = 7
 
 
-def backward_kernel(sections, holders, tasks, grad_dests, fresh, reused, groups_of_blocks, *refs):
+def backward_kernel(sections, holders, tasks, names, before, groups_of_blocks, *refs):
     refs = list(refs)
 
     def take(count):
@@ -713,10 +781,9 @@
     g_ref, gain_one_ref, gain_two_ref, router_ref, cos_ref, sin_ref, pick_ref, mark_ref = take(8)
     inner_hbm, out_hbm, gate_hbm, up_hbm, down_hbm = take(5)
     sets = [take(HELD) for _ in holders]
-    sources = take(len(tasks))
-    take(reused)
+    take(before)
     outputs = take(7)
-    dests = take(fresh + reused)
+    dests = take(len(names))
     gates_w, ups_w, downs_w, out, inner = take(5)
     held = take(HELD)
     entry, bias_v, query, kv, lse, middle, payload = held
@@ -724,10 +791,8 @@
     branch, logit, middle_grad, datt = take(4)
     own_kv, sent_kv, back_kv, turned, entry_grad, entry_low, gain_one_v, gain_two_v = take(8)
     expert_sem, out_sem, inner_sem, held_sem, grads_sem, back_sem, kv_sem, save_sem = take(8)
-    relays = [
-        (section, Relay(sources[i], dests[dest], take(5))) for i, (section, dest) in enumerate(tasks)
-    ]
-    grad_relays = [(section, Relay(grads, dests[dest], take(5))) for section, dest in grad_dests]
+    relays = make_relays(tasks, grads, names, dests, take)
+    grad_relays = [relay for relay in relays if relay.keeps]
 
     blocks, rows, width = grads.shape
     local, _, hidden_width = gates_w.shape
@@ -736,9 +801,8 @@
     queries = H * HD // blocks
     own_keys = keys // blocks
 
-    enter(sections, relays + grad_relays, blocks)
-    for section, relay in relays:
-        in_section(section)(lambda relay=relay: open_relay(relay))
+    enter(sections, relays, blocks)
+    run_relays(relays, Relay.open)
 
     @in_sections(sections)
     def _():
@@ -793,8 +857,7 @@
                 copy.start()
         out_copy.start()
         inner_copy.start()
-        for section, relay in grad_relays:
-            in_section(section)(lambda relay=relay: relay.start(0))
+        run_relays(grad_relays, lambda relay: relay.start(0))
 
         saves = []
 
@@ -825,12 +888,8 @@
                 if d:
                     grads_copies[d - 1].wait_recv()
             if blocks - 1 in members:
-                for section, relay in grad_relays:
-
-                    @in_section(section)
-                    def _(relay=relay):
-                        relay.start(1)
-                        relay.keep().start()
+                run_relays(grad_relays, lambda relay: relay.start(1))
+                run_relays(grad_relays, Relay.keep)
 
             held_rows = slice(members[0] * rows, (members[-1] + 1) * rows)
             grad = jnp.concatenate([grads[d] for d in members], axis=0)
@@ -862,8 +921,6 @@
             if at == 0:
                 for index in order[1:]:
                     fetch(0, index).wait()
-        for section, relay in grad_relays + [item for item in relays if item[0] in sections]:
-            in_section(section)(relay.forward)
 
         total = own[:, :width]
         share = own[:, width:]
@@ -871,6 +928,7 @@
             back_copies[d - 1].wait_recv()
             total = total + back[d - 1, :, :width].astype(F32)
             share = share + back[d - 1, :, width:].astype(F32)
+        run_relays(relays, Relay.forward, sections)
         first = lax.broadcasted_iota(jnp.int32, (1, LANES), 1) < LOW
         shares = payload[0, :, width:].astype(F32)
         shares = jnp.where(first, shares + pltpu.roll(shares, LOW, 1), 0.0)
@@ -974,11 +1032,8 @@
         for copy in saves:
             copy.wait()
 
-    for section, relay in relays:
-        if section not in sections:
-            in_section(section)(relay.forward)
-    for section, relay in relays + grad_relays:
-        in_section(section)(relay.finish)
+    run_relays(relays, Relay.forward, sections, outside=True)
+    run_relays(relays, Relay.finish)
 
 
 def backward_layer(
@@ -994,11 +1049,10 @@
     pick,
     mark,
     weights,
-    tasks=(),
-    grad_dests=(),
-    fresh=(),
-    reused=(),
+    tasks,
+    arrays,
 ):
+    names, before, dests = relay_arrays(tasks, arrays)
     inner, out, gate_all, up_all, down_all = weights
     rows, width = grad.shape
     blocks = inner.shape[0]
@@ -1011,22 +1065,21 @@
     groups_of_blocks = [[0], list(range(1, blocks - 1)), [blocks - 1]]
     pair = (2, blocks - 1)
     anywhere = pl.BlockSpec(memory_space=pl.ANY)
-    first_reused = 13 + HELD * len(sets) + len(tasks)
+    first_before = 13 + HELD * len(sets)
     held = sets[0][1]
     results = pl.pallas_call(
         functools.partial(
             backward_kernel,
             sections,
             [section for section, _ in sets],
-            [(section, dest) for section, _, dest in tasks],
-            grad_dests,
-            len(fresh),
-            len(reused),
+            tasks,
+            names,
+            len(before),
             groups_of_blocks,
         ),
         in_specs=[whole()] * 8
-        + [anywhere] * (5 + HELD * len(sets) + len(tasks) + len(reused)),
-        out_specs=[anywhere] * (7 + len(reused) + len(fresh)),
+        + [anywhere] * (5 + HELD * len(sets) + len(before)),
+        out_specs=[anywhere] * (7 + len(names)),
         out_shape=[
             shape((rows, width), F32),
             shape((rows, width), BF16),
@@ -1035,9 +1088,8 @@
             shape((rows, LANES), BF16),
             shape((1, width), F32),
             shape((1, width), F32),
-        ]
-        + [shape(dest.shape, BF16) for dest in reused]
-        + [shape((members, blocks, rows, columns), BF16) for columns in fresh],
+            *dests,
+        ],
         scratch_shapes=[
             pltpu.VMEM(gate_all.shape, BF16),
             pltpu.VMEM(up_all.shape, BF16),
@@ -1074,8 +1126,8 @@
             pltpu.SemaphoreType.DMA((2, 2, blocks - 1)),
             pltpu.SemaphoreType.DMA((7,)),
         ]
-        + relay_sems(blocks, members) * (len(tasks) + len(grad_dests)),
-        input_output_aliases={first_reused + i: 7 + i for i in range(len(reused))},
+        + relay_sems(blocks, members) * len(tasks),
+        input_output_aliases={first_before + i: 7 + i for i in range(len(before))},
         compiler_params=pltpu.CompilerParams(
             vmem_limit_bytes=VMEM, collective_id=number, has_side_effects=True
         ),
@@ -1095,88 +1147,559 @@
         gate_all,
         up_all,
         down_all,
-        *[array for _, arrays in sets for array in arrays],
-        *[payloads for _, payloads, _ in tasks],
-        *reused,
+        *[array for _, held_arrays in sets for array in held_arrays],
+        *before,
     )
-    return results[:7], results[7:]
-
-
-def expert_weights_kernel(batches, *refs):
-    token_refs = refs[:batches]
-    grad_refs = refs[batches : 2 * batches]
-    pick_ref, gate_ref, up_ref, down_ref, dgate_ref, dup_ref, ddown_ref = refs[2 * batches :]
-    tile = pl.program_id(1)
-    tiles = pl.num_programs(1) // batches
-    width = grad_refs[0].shape[1]
-
-    @pl.when(tile == 0)
+    return results[:7], dict(zip(names, results[7:]))
+
+
+def prepare_kernel(tile, batches, *refs):
+    tokens, (pick, gate_w, up_w, *outputs) = refs[:batches], refs[batches:]
+    local, width, hidden_width = gate_w.shape
+    count = tokens[0].shape[0] // tile
+
+    def body(x_ref, pick_ref, gate_ref, up_ref, hidden_ref, gate_factor_ref, up_factor_ref):
+        entry = x_ref[:, :width]
+        weight = jnp.sum(x_ref[:, width:].astype(F32) * pick_ref[0], axis=-1, keepdims=True)
+        gate = dot(entry, gate_ref[0], ((1,), (0,)))
+        up = dot(entry, up_ref[0], ((1,), (0,)))
+        held, gate_part, up_part = activation(gate, up, weight)
+        hidden_ref[...] = (held * weight).astype(BF16)
+        gate_factor_ref[...] = gate_part.astype(BF16)
+        up_factor_ref[...] = up_part.astype(BF16)
+
+    @in_section(0)
     def _():
-        for out in (dgate_ref, dup_ref, ddown_ref):
+        weight = pl.BlockSpec((1, width, hidden_width), lambda t, e: (e, 0, 0))
+        for batch, x_hbm in enumerate(tokens):
+            piece = pl.BlockSpec((tile, hidden_width), lambda t, e: (batch * count + t, e))
+            pltpu.emit_pipeline(
+                body,
+                grid=(count, local),
+                in_specs=[
+                    pl.BlockSpec((tile, width + LANES), lambda t, e: (t, 0)),
+                    pl.BlockSpec((1, 1, LANES), lambda t, e: (e, 0, 0)),
+                    weight,
+                    weight,
+                ],
+                out_specs=[piece] * 3,
+            )(x_hbm, pick, gate_w, up_w, *outputs)
+
+
+def prepare(tokens, pick, gate_all, up_all, tile=512):
+    local, width, hidden = gate_all.shape
+    rows = sum(block.shape[0] for block in tokens)
+    anywhere = pl.BlockSpec(memory_space=pl.ANY)
+    return pl.pallas_call(
+        functools.partial(prepare_kernel, min(tile, tokens[0].shape[0]), len(tokens)),
+        in_specs=[anywhere] * (3 + len(tokens)),
+        out_specs=[anywhere] * 3,
+        out_shape=[shape((rows, local * hidden), BF16)] * 3,
+        compiler_params=params(),
+        cost_estimate=cost(4 * rows * local * width * hidden, rows * width * 8),
+        name="prepare",
+    )(*tokens, pick, gate_all, up_all)
+
+
+def weights_step(ready, x_ref, g_ref, down_ref, held, outs):
+    width = g_ref.shape[1]
+    entry = x_ref[:, :width]
+    grad = g_ref[...]
+    hidden_grad = dot(grad, down_ref[0], ((1,), (1,)))
+    if ready:
+        hidden = held[0][...]
+        gate_part = hidden_grad * held[1][...].astype(F32)
+        up_part = hidden_grad * held[2][...].astype(F32)
+    else:
+        pick_ref, gate_ref, up_ref = held[-3:]
+        weight = jnp.sum(x_ref[:, width:].astype(F32) * pick_ref[0], axis=-1, keepdims=True)
+        gate = dot(entry, gate_ref[0], ((1,), (0,)))
+        up = dot(entry, up_ref[0], ((1,), (0,)))
+        hidden, gate_part, up_part = activation(gate, up, hidden_grad * weight)
+        hidden = (hidden * weight).astype(BF16)
+    dgate_ref, dup_ref, ddown_ref = outs
+    dgate_ref[0] += dot(entry, gate_part.astype(BF16), ((0,), (0,)))
+    dup_ref[0] += dot(entry, up_part.astype(BF16), ((0,), (0,)))
+    ddown_ref[0] += dot(hidden, grad, ((0,), (0,)))
+
+
+def weights_specs(ready, first, tile, expert, shapes):
+    width, hidden = shapes
+    columns = pl.BlockSpec((1, width, hidden), lambda e, t: (expert(e), 0, 0))
+    bands = pl.BlockSpec((1, hidden, width), lambda e, t: (expert(e), 0, 0))
+    piece = pl.BlockSpec((tile, hidden), lambda e, t: (first + t, expert(e)))
+    specs = [
+        pl.BlockSpec((tile, width + LANES), lambda e, t: (t, 0)),
+        pl.BlockSpec((tile, width), lambda e, t: (t, 0)),
+        bands,
+    ]
+    if ready:
+        specs += [piece] * 3
+    specs += [pl.BlockSpec((1, 1, LANES), lambda e, t: (expert(e), 0, 0)), columns, columns]
+    return specs, [columns, columns, bands]
+
+
+def weights_both(ready, x_ref, g_ref, down_ref, held, outs):
+    if not ready:
+        weights_step(False, x_ref, g_ref, down_ref, held, outs)
+        return
+    for section in range(2):
+
+        @in_section(section)
+        def _(section=section):
+            weights_step(section == 0, x_ref, g_ref, down_ref, held, outs)
+
+
+def first_weights_kernel(ready, tasks, names, *refs):
+    refs = list(refs)
+
+    def take(count):
+        taken = refs[:count]
+        del refs[:count]
+        return taken
+
+    x_ref, g_ref, down_ref, *held = take(9 if ready else 6)
+    take(len(names))
+    outs = take(3)
+    dests = take(len(names))
+    relays = make_relays(tasks, None, names, dests, take)
+    step = pl.program_id(0) * pl.num_programs(1) + pl.program_id(1)
+
+    early = [relay for relay in relays if relay.section == 0]
+    late = [relay for relay in relays if relay.section != 0]
+
+    @pl.when(step == 0)
+    def _():
+        enter([], early, dests[0].shape[2])
+        run_relays(early, Relay.forward)
+
+    @pl.when(pl.program_id(1) == 0)
+    def _():
+        for out in outs:
             out[...] = jnp.zeros_like(out)
 
+    weights_both(ready, x_ref, g_ref, down_ref, held, outs)
+
+    @pl.when(step == pl.num_programs(0) * pl.num_programs(1) - 1)
+    def _():
+        enter([], late, dests[0].shape[2])
+        run_relays(late, Relay.forward)
+        run_relays(relays, Relay.finish)
+
+
+def first_weights(number, tasks, arrays, tokens, grads, down_all, prepared, forward, tile=512):
+    local, hidden, width = down_all.shape
+    names, before, dests = relay_arrays(tasks, arrays)
+    _, members, blocks, _, _ = dests[0].shape
+    rows = grads.shape[0]
+    tile = min(tile, rows)
+    ready = prepared is not None
+    specs, outs = weights_specs(ready, 0, tile, lambda e: e, (width, hidden))
+    anywhere = pl.BlockSpec(memory_space=pl.ANY)
+    results = pl.pallas_call(
+        functools.partial(first_weights_kernel, ready, tasks, names),
+        grid=(1, rows // tile),
+        in_specs=specs + [anywhere] * len(names),
+        out_specs=outs + [anywhere] * len(names),
+        out_shape=[
+            shape((local, width, hidden), F32),
+            shape((local, width, hidden), F32),
+            shape((local, hidden, width), F32),
+            *dests,
+        ],
+        scratch_shapes=relay_sems(blocks, members) * len(tasks),
+        input_output_aliases={len(specs) + i: 3 + i for i in range(len(names))},
+        compiler_params=pltpu.CompilerParams(
+            vmem_limit_bytes=VMEM,
+            collective_id=number,
+            has_side_effects=True,
+            dimension_semantics=("arbitrary", "arbitrary"),
+        ),
+        cost_estimate=cost(8 * rows * width * hidden, rows * (4 * width + 6 * hidden)),
+        name="first_weights",
+    )(tokens, grads, down_all, *(prepared if ready else ()), *forward, *before)
+    return results[:3], dict(zip(names, results[3:]))
+
+
+def whole_weights_kernel(ready, batches, *refs):
+    x_refs, refs = refs[:batches], refs[batches:]
+    g_refs, (down_ref, *rest) = refs[:batches], refs[batches:]
+    held = rest[: 6 if ready else 3]
+    outs = rest[-3:]
+    tiles = pl.num_programs(0) // batches
+
+    @pl.when(pl.program_id(0) == 0)
+    def _():
+        for out in outs:
+            out[...] = jnp.zeros_like(out)
+
     for batch in range(batches):
 
-        @pl.when(tile // tiles == batch)
-        def _(x_ref=token_refs[batch], g_ref=grad_refs[batch]):
-            entry = x_ref[:, :width]
-            grad = g_ref[...]
-            weight = jnp.sum(x_ref[:, width:].astype(F32) * pick_ref[0], axis=-1, keepdims=True)
-            gate = dot(entry, gate_ref[0], ((1,), (0,)))
-            up = dot(entry, up_ref[0], ((1,), (0,)))
-            hidden_grad = dot(grad, down_ref[0], ((1,), (1,)))
-            hidden, gate_part, up_part = activation(gate, up, hidden_grad * weight)
-            dgate_ref[0] += dot(entry, gate_part.astype(BF16), ((0,), (0,)))
-            dup_ref[0] += dot(entry, up_part.astype(BF16), ((0,), (0,)))
-            ddown_ref[0] += dot((hidden * weight).astype(BF16), grad, ((0,), (0,)))
-
-
-def expert_weights(tokens, grads, pick, gate_all, up_all, down_all, tile=512):
-    local, width, hidden = gate_all.shape
+        @pl.when(pl.program_id(0) // tiles == batch)
+        def _(batch=batch):
+            weights_both(ready, x_refs[batch], g_refs[batch], down_ref, held, outs)
+
+
+def whole_weights(expert, tokens, grads, down_all, prepared, forward, chain=None, tile=512):
+    local, hidden, width = down_all.shape
     batches = len(tokens)
-    total = tokens[0].shape[0]
-    tile = min(tile, total)
-    tiles = total // tile
-    columns = pl.BlockSpec((1, width, hidden), lambda e, t: (e, 0, 0))
-    bands = pl.BlockSpec((1, hidden, width), lambda e, t: (e, 0, 0))
-
-    def rows(batch, lanes):
-        return pl.BlockSpec(
-            (tile, lanes), lambda e, t: (jnp.clip(t - batch * tiles, 0, tiles - 1), 0)
-        )
-
+    rows = grads[0].shape[0]
+    tile = min(tile, rows)
+    tiles = rows // tile
+    ready = prepared is not None
+    chained = chain is not None
+
+    def band(batch, lanes):
+        return pl.BlockSpec((tile, lanes), lambda t: (jnp.clip(t - batch * tiles, 0, tiles - 1), 0))
+
+    columns = pl.BlockSpec((1, width, hidden), lambda t: (expert, 0, 0))
+    bands = pl.BlockSpec((1, hidden, width), lambda t: (expert, 0, 0))
+    specs = [band(batch, width + LANES) for batch in range(batches)]
+    specs += [band(batch, width) for batch in range(batches)] + [bands]
+    if ready:
+        specs += [pl.BlockSpec((tile, hidden), lambda t: (t, expert))] * 3
+    specs += [pl.BlockSpec((1, 1, LANES), lambda t: (expert, 0, 0)), columns, columns]
     return pl.pallas_call(
-        functools.partial(expert_weights_kernel, batches),
-        grid=(local, batches * tiles),
-        in_specs=[rows(batch, width + LANES) for batch in range(batches)]
-        + [rows(batch, width) for batch in range(batches)]
-        + [pl.BlockSpec((1, 1, LANES), lambda e, t: (e, 0, 0)), columns, columns, bands],
+        functools.partial(whole_weights_kernel, ready, batches),
+        grid=(batches * tiles,),
+        in_specs=specs + [pl.BlockSpec(memory_space=pl.ANY)] * (3 if chained else 0),
         out_specs=[columns, columns, bands],
         out_shape=[
             shape((local, width, hidden), F32),
             shape((local, width, hidden), F32),
             shape((local, hidden, width), F32),
         ],
-        compiler_params=params("arbitrary", "arbitrary"),
+        input_output_aliases={len(specs) + i: i for i in range(3)} if chained else {},
+        compiler_params=pltpu.CompilerParams(
+            vmem_limit_bytes=LARGE, dimension_semantics=("arbitrary",)
+        ),
         cost_estimate=cost(
-            2 * total * batches * local * 6 * width * hidden,
-            local * 3 * width * hidden * 6 + total * batches * local * width * 4,
+            8 * rows * batches * width * hidden, rows * batches * (4 * width + 6 * hidden)
         ),
-        name="expert_weights",
-    )(*tokens, *grads, pick, gate_all, up_all, down_all)
+        name="whole_weights",
+    )(
+        *tokens,
+        *grads,
+        down_all,
+        *(prepared if ready else ()),
+        *forward,
+        *(chain if chained else ()),
+    )
+
+
+def last_weights_kernel(ready, chained, *refs):
+    x_ref, g_ref, down_ref, *rest = refs
+    count = 6 if ready else 3
+    held, before = rest[:count], rest[count : count + 3]
+    outs = rest[count + 6 :] if chained else rest[count + 3 :]
+
+    @pl.when(pl.program_id(1) == 0)
+    def _():
+        for out, source in zip(outs, before):
+            out[...] = source[...]
+
+    weights_both(ready, x_ref, g_ref, down_ref, held, outs)
+
+
+def last_weights(experts, tokens, grads, down_all, prepared, forward, before, chain=None, tile=512):
+    in_place = chain is before
+    if in_place:
+        chain = None
+    local, hidden, width = down_all.shape
+    rows = grads.shape[0]
+    tile = min(tile, rows)
+    chained = chain is not None
+    ready = prepared is not None
+    first = (prepared[0].shape[0] - rows) // tile if ready else 0
+    specs, outs = weights_specs(ready, first, tile, lambda e: experts[0] + e, (width, hidden))
+    held = [
+        pl.BlockSpec(spec.block_shape, spec.index_map, pipeline_mode=pl.Buffered(1)) for spec in outs
+    ]
+    count = len(specs)
+    anywhere = pl.BlockSpec(memory_space=pl.ANY)
+    return pl.pallas_call(
+        functools.partial(last_weights_kernel, ready, chained),
+        grid=(experts[1] - experts[0], rows // tile),
+        in_specs=specs + held + [anywhere] * (3 if chained else 0),
+        out_specs=outs,
+        out_shape=[
+            shape((local, width, hidden), F32),
+            shape((local, width, hidden), F32),
+            shape((local, hidden, width), F32),
+        ],
+        input_output_aliases={count + (3 if chained else 0) + i: i for i in range(3)}
+        if chained or in_place
+        else {},
+        compiler_params=pltpu.CompilerParams(
+            vmem_limit_bytes=LARGE, dimension_semantics=("arbitrary", "arbitrary")
+        ),
+        cost_estimate=cost(
+            8 * rows * width * hidden * (experts[1] - experts[0]), rows * (4 * width + 6 * hidden)
+        ),
+        name="last_weights",
+    )(
+        tokens,
+        grads,
+        down_all,
+        *(prepared if ready else ()),
+        *forward,
+        *before,
+        *(chain if chained else ()),
+    )
+
+
+def attention_weights_kernel(section, batches, blocks, members, by_rows, *refs):
+    sets = [refs[8 * m : 8 * m + 8] for m in range(batches)]
+    refs = refs[8 * batches :]
+    count = members if by_rows else blocks
+    outputs = refs[:count]
+    small_out = refs[count]
+    held = refs[count + 1 : count + 1 + blocks]
+    normed, turned, attended, branch, mixed, logit, gains, small, sems, save_sems = refs[
+        count + 1 + blocks :
+    ]
+    place = lax.axis_index("dp")
+    depth = held[0].shape[0] // members
+    rows = normed.shape[0] // batches
+    me = lax.axis_index("expert")
+    part = branch.shape[1] // blocks
+    columns = turned.shape[1]
+
+    @in_section(section)
+    def _():
+        copies = []
+        for m in range(batches):
+            band = pl.ds(m * rows, rows)
+            targets = (
+                normed.at[band],
+                turned.at[:, :, band],
+                attended.at[:, band],
+                branch.at[band],
+                mixed.at[band],
+                logit.at[band],
+                gains.at[m, 0],
+                gains.at[m, 1],
+            )
+            for i, (source, target) in enumerate(zip(sets[m], targets)):
+                copies.append(pltpu.make_async_copy(source, target, sems.at[m, i]))
+        for copy in copies:
+            copy.start()
+        for copy in copies:
+            copy.wait()
+        router = dot(logit[...], mixed[:, : normed.shape[1]], ((0,), (0,)))
+        small[...] = router[: small.shape[0]]
+        for i in range(2):
+            total = gains[0, i]
+            for m in range(1, batches):
+                total = total + gains[m, i]
+            small[pl.ds(small.shape[0] - 2 + i, 1), :] = total
+        saves = [pltpu.make_async_copy(small, small_out, save_sems.at[blocks, 0])]
+        saves[0].start()
+        for d in [*range(1, blocks), 0]:
+            e = partner(me, d)
+            at = pl.multiple_of(e * part, LANES)
+            held[d][:, :columns] = dot(normed[...], turned[e], ((0,), (1,))).astype(BF16)
+            held[d][:, columns:] = dot(
+                attended[...], branch[:, pl.ds(at, part)], ((1,), (0,))
+            ).astype(BF16)
+            if not by_rows:
+                saves.append(pltpu.make_async_copy(held[d], outputs[d], save_sems.at[d, 0]))
+                saves[-1].start()
+                continue
+            for k in range(members):
+                at = pl.multiple_of(lax.rem(place + k, members) * depth, depth)
+                save = pltpu.make_async_copy(
+                    held[d].at[pl.ds(at, depth)],
+                    outputs[k].at[pl.ds(d * depth, depth)],
+                    save_sems.at[d, k],
+                )
+                save.start()
+                saves.append(save)
+        for save in saves:
+            save.wait()
+
+
+def attention_weights(section, sets, by_rows):
+    members = lax.axis_size("dp")
+    batches = len(sets)
+    normed, turned, attended, branch, mixed, logit, _, _ = sets[0]
+    blocks, columns, rows = turned.shape
+    width = branch.shape[1]
+    wide = columns + width // blocks
+    flat = [array for one in sets for array in one]
+    anywhere = pl.BlockSpec(memory_space=pl.ANY)
+    return pl.pallas_call(
+        functools.partial(
+            attention_weights_kernel, section, batches, blocks, members, by_rows
+        ),
+        in_specs=[anywhere] * len(flat),
+        out_specs=[anywhere] * (1 + (members if by_rows else blocks)),
+        out_shape=(
+            [shape((width * blocks // members, wide), BF16)] * members
+            if by_rows
+            else [shape((width, wide), BF16)] * blocks
+        )
+        + [shape((SMALL, width), F32)],
+        scratch_shapes=[pltpu.VMEM((width, wide), BF16)] * blocks
+        + [
+            pltpu.VMEM((batches * rows, width), BF16),
+            pltpu.VMEM((blocks, columns, batches * rows), BF16),
+            pltpu.VMEM((attended.shape[0], batches * rows), BF16),
+            pltpu.VMEM((batches * rows, width), BF16),
+            pltpu.VMEM((batches * rows, mixed.shape[1]), BF16),
+            pltpu.VMEM((batches * rows, logit.shape[1]), BF16),
+            pltpu.VMEM((batches, 2, 1, width), F32),
+            pltpu.VMEM((SMALL, width), F32),
+            pltpu.SemaphoreType.DMA((batches, 8)),
+            pltpu.SemaphoreType.DMA((blocks + 1, members)),
+        ],
+        compiler_params=params(),
+        cost_estimate=cost(2 * batches * rows * width * wide * blocks, 2e7),
+        name="attention_weights",
+    )(*flat)
+
+
+def sum_kernel(counts, depth, *refs):
+    output = refs[-1]
+    wide = output.shape[1]
+    tile = depth // 2
+    at = 0
+    for section, (terms, bands) in enumerate(counts):
+
+        def body(*tiles, terms=terms):
+            total = tiles[0][...].astype(F32)
+            for piece in tiles[1:terms]:
+                total = total + piece[...].astype(F32)
+            tiles[terms][...] = total.astype(BF16)
+
+        @in_section(section)
+        def _(at=at, terms=terms, bands=bands, section=section, body=body):
+            first = 2 * lax.axis_index("dp") if section == 0 else 0
+            pltpu.emit_pipeline(
+                body,
+                grid=(2 * bands,),
+                in_specs=[
+                    pl.BlockSpec((tile, wide), lambda i: (lax.rem(first + i, 2 * bands), 0))
+                ]
+                * terms,
+                out_specs=[pl.BlockSpec((tile, wide), lambda i: (i, 0))],
+            )(*refs[at : at + terms], output)
+
+        at += terms
+
+
+def sum_blocks(upper, lower, depth):
+    wide = upper[0].shape[1]
+    rows = max(upper[0].shape[0], lower[0].shape[0])
+    counts = [(len(terms), terms[0].shape[0] // depth) for terms in (upper, lower)]
+    anywhere = pl.BlockSpec(memory_space=pl.ANY)
+    total = pl.pallas_call(
+        functools.partial(sum_kernel, counts, depth),
+        in_specs=[anywhere] * (len(upper) + len(lower)),
+        out_specs=anywhere,
+        out_shape=shape((rows, wide), BF16),
+        compiler_params=params(),
+        cost_estimate=cost(0, rows * wide * 2 * (len(upper) + 1)),
+        name="sum_blocks",
+    )(*upper, *lower)
+    return jnp.split(total, rows // depth, axis=0)
+
+
+def small_kernel(upper, lower, total, own, plane, line, fetch_sem, plane_sem, line_sem):
+    blocks = plane.shape[0] + 1
+    members = line.shape[0] + 1
+    for section, source in ((0, upper), (1, lower)):
+
+        @in_section(section)
+        def _(source=source):
+            fetch = pltpu.make_async_copy(source, own, fetch_sem)
+            fetch.start()
+            fetch.wait()
+
+    greet(plane_peers(blocks) + line_peers(members))
+    for peers, room, sems in (
+        (plane_peers(blocks), plane, plane_sem),
+        (line_peers(members), line, line_sem),
+    ):
+        copies = [
+            send(own, room.at[i], sems.at[0, i], sems.at[1, i], peer) for i, peer in enumerate(peers)
+        ]
+        for copy in copies:
+            copy.start()
+        for copy in copies:
+            copy.wait()
+        held = own[...]
+        for i in range(len(peers)):
+            held = held + room[i]
+        own[...] = held
+    total[...] = own[...]
+
+
+def sum_small(number, upper, lower):
+    blocks = lax.axis_size("expert")
+    members = lax.axis_size("dp")
+    return pl.pallas_call(
+        small_kernel,
+        in_specs=[pl.BlockSpec(memory_space=pl.ANY)] * 2,
+        out_specs=whole(),
+        out_shape=shape(upper.shape, F32),
+        scratch_shapes=[
+            pltpu.VMEM(upper.shape, F32),
+            pltpu.VMEM((blocks - 1,) + upper.shape, F32),
+            pltpu.VMEM((members - 1,) + upper.shape, F32),
+            pltpu.SemaphoreType.DMA(()),
+            pltpu.SemaphoreType.DMA((2, blocks - 1)),
+            pltpu.SemaphoreType.DMA((2, members - 1)),
+        ],
+        compiler_params=pltpu.CompilerParams(
+            vmem_limit_bytes=VMEM, collective_id=number, has_side_effects=True
+        ),
+        name="sum_small",
+    )(upper, lower)
+
+
+def assemble_kernel(blocks, *refs):
+    outputs = refs[blocks:]
+    me = lax.axis_index("expert")
+    for d in range(blocks):
+        e = partner(me, d)
+        at = 0
+        for out in outputs:
+            part = out.shape[1] // blocks
+            start = pl.multiple_of(e * part, LANES)
+            out[:, pl.ds(start, part)] = refs[d][:, at : at + part].astype(F32)
+            at += part
+
+
+def assemble(shards, widths):
+    rows = shards[0].shape[0]
+    return pl.pallas_call(
+        functools.partial(assemble_kernel, len(shards)),
+        in_specs=[whole()] * len(shards),
+        out_specs=[whole()] * len(widths),
+        out_shape=[shape((rows, columns), F32) for columns in widths],
+        compiler_params=params(),
+        cost_estimate=cost(0, rows * sum(widths) * 6),
+        name="assemble",
+    )(*shards)
 
 
 def pad_lanes(block):
     return jnp.pad(block, ((0, 0), (0, LANES - block.shape[1])))
 
 
-def scatter_sum(blocks_of, axis):
-    count = lax.axis_size(axis)
-    me = lax.axis_index(axis)
-    total = blocks_of(me).astype(F32)
-    for distance in range(1, count):
-        total = total + shift(blocks_of((me + distance) % count), axis, distance).astype(F32)
-    return total
+def swap(block, distance, sections):
+    count = lax.axis_size("expert")
+    route = [
+        (section * count + i, section * count + (i ^ distance))
+        for section in sections
+        for i in range(count)
+    ]
+    return lax.ppermute(block, ("section", "expert"), route)
+
+
+def total_of(blocks):
+    return functools.reduce(jnp.add, [block.astype(F32) for block in blocks]).astype(BF16)
 
 
 def body(
@@ -1237,16 +1760,14 @@
     biases = [bias_of(batch) for batch in range(batches)]
     chosens = [chosen_of(batch) for batch in range(batches)]
 
-    sources = (
+    inner, out, router = gather_weights(
+        0,
         query_weight[0],
         key_weight[0],
         value_weight[0],
         output_weight[0],
         pad_lanes(router_weight[0]),
     )
-    gathered = gather_weights(0, 0, sources)
-    done = from_behind(gathered[2][:8], 1)
-    inner, out, router = gather_weights(1, 1, sources, gathered, done)
     gain_one = attention_gain
     gain_two = mixture_gain
     gate_all, up_all, down_all = (expert_gate[0], expert_up[0], expert_down[0])
@@ -1255,20 +1776,53 @@
     def active(moment):
         return [s for s in range(2) if 0 <= moment - s < batches]
 
-    payload_all = [None] * batches
-    grads_all = [None] * batches
     stored = []
     produced = []
     inbound = jnp.zeros((rows, width), BF16)
-
-    def plan_tasks(moment):
-        tasks, reused, fresh = [], [], []
-        for section in active(moment - 1):
-            batch = moment - 1 - section
-            (fresh if payload_all[batch] is None else reused).append((section, batch))
-        for at, (section, batch) in enumerate(reused + fresh):
-            tasks.append((section, stored[moment - 1]["payloads"], at))
-        return tasks, [batch for _, batch in reused], [batch for _, batch in fresh]
+    arrays = {
+        "p0": [None, shape((1, members, groups, rows, width + LANES), BF16)],
+        "p1": [None, shape((1, members, groups, rows, width + LANES), BF16)],
+        "g0": [None, shape((1, members, groups, rows, width), BF16)],
+        "g1": [None, shape((1, members, groups, rows, width), BF16)],
+    }
+
+    def keep_arrays(made):
+        for name, array in made.items():
+            arrays[name][0] = array
+
+    plans = {
+        ("forward", 0): [(0, ("keep",), "p0", 0, True)],
+        ("forward", 1): [
+            (0, ("line",), "p0", 0, True),
+            (0, ("keep",), "p1", 0, True),
+            (1, ("keep",), "p0", 0, True),
+        ],
+        ("forward", 2): [
+            (1, ("line",), "p0", 0, True),
+            (0, ("line", "plane"), "p1", 0, False),
+            (0, ("plane",), "p0", 0, True),
+            (1, ("keep",), "p1", 0, True),
+        ],
+        ("backward", 0): [
+            (1, ("keep", "line"), "g0", 0, True),
+            (1, ("line",), "p1", 0, True),
+            (1, ("plane",), "p0", 0, True),
+        ],
+        ("backward", 1): [
+            (0, ("keep", "line"), "g0", 0, True),
+            (1, ("keep", "line"), "g1", 0, True),
+            (1, ("plane",), "g0", 0, True),
+        ],
+        ("backward", 2): [
+            (0, ("keep", "line"), "g1", 0, False),
+            (0, ("plane",), "g0", 0, True),
+        ],
+        ("weights", 0): [
+            (0, ("plane",), "g1", 0, False),
+            (1, ("plane",), "g1", 0, True),
+            (1, ("plane",), "p1", 0, True),
+        ],
+    }
 
     for moment in range(batches + 1):
         sections = active(moment)
@@ -1283,10 +1837,9 @@
                 (layer_input[early], biases[early], chosens[early]),
                 (inbound, biases[late], chosens[late]),
             )
-        tasks, reused, fresh = plan_tasks(moment)
-        results, dests = forward_layer(
+        results, made = forward_layer(
             sections,
-            2 + moment,
+            1 + moment,
             entry,
             gain_one,
             cosine,
@@ -1297,12 +1850,10 @@
             chosen,
             pick,
             weights,
-            tasks,
-            len(fresh),
-            [payload_all[batch] for batch in reused],
+            plans["forward", moment],
+            arrays,
         )
-        for batch, dest in zip(reused + fresh, dests):
-            payload_all[batch] = dest
+        keep_arrays(made)
         normed, queries, kv, attended, lse, middle, payloads, output = results
         produced.append(output)
         if moment < batches:
@@ -1316,6 +1867,32 @@
             )
         )
 
+    def attention_terms(section):
+        parts = list(
+            attention_weights(
+            section,
+            [
+                (
+                    stored[batch + section]["normed"],
+                    moments[batch + 1 - section][1],
+                    stored[batch + section]["attended"],
+                    moments[batch + 1 - section][2],
+                    stored[batch + section]["payloads"][0],
+                    *moments[batch + 1 - section][3:],
+                )
+                for batch in range(batches)
+            ],
+            section == 1,
+        ))
+        small[section] = parts.pop()
+        if section == 1:
+            return [parts[0]] + [shift(parts[k], "dp", k, [1]) for k in range(1, members)]
+        return [parts[0]] + [swap(parts[d], d, [0]) for d in range(1, groups)]
+
+    prepared = None
+    terms = [None, None]
+    small = [None, None]
+
     received = None
     moments = []
     for moment in range(batches + 1):
@@ -1327,18 +1904,9 @@
         sets = [
             (s, stored[moment - 1 if s == 0 else moment + 1]["held"]) for s in sections
         ]
-        tasks, reused, fresh = plan_tasks(batches + 1) if moment == 0 else ([], [], [])
-        wanted = [(s, moment - (1 - s)) for s in sections]
-        old = [(s, batch) for s, batch in wanted if grads_all[batch] is not None]
-        new = [(s, batch) for s, batch in wanted if grads_all[batch] is None]
-        grad_dests = []
-        for at, (s, batch) in enumerate(old):
-            grad_dests.append((s, len(reused) + at))
-        for at, (s, batch) in enumerate(new):
-            grad_dests.append((s, len(reused) + len(old) + len(fresh) + at))
-        results, dests = backward_layer(
+        results, made = backward_layer(
             sections,
-            3 + batches + moment,
+            2 + batches + moment,
             grad,
             sets,
             gain_one,
@@ -1349,106 +1917,98 @@
             pick,
             mark,
             weights,
-            tasks,
-            grad_dests,
-            [width + LANES] * len(fresh) + [width] * len(new),
-            [payload_all[batch] for batch in reused] + [grads_all[batch] for _, batch in old],
+            plans["backward", moment],
+            arrays,
         )
-        dests = list(dests)
-        for batch in reused:
-            payload_all[batch] = dests.pop(0)
-        for _, batch in old:
-            grads_all[batch] = dests.pop(0)
-        for batch in fresh:
-            payload_all[batch] = dests.pop(0)
-        for _, batch in new:
-            grads_all[batch] = dests.pop(0)
+        keep_arrays(made)
         entry_grad, sent, turned, branch, logit_grad, gain_one_part, gain_two_part = results
         moments.append((entry_grad, turned, branch, logit_grad, gain_one_part, gain_two_part))
+        if moment == 0:
+            both = [arrays[name][0].reshape(-1, width + LANES) for name in ("p0", "p1")]
+            if sum(block.shape[0] for block in both) <= PREPARED:
+                prepared = prepare(both, pick, gate_all, up_all)
         if moment < batches:
             received = from_behind(sent, -1)
-
-    gate_grad, up_grad, down_grad = expert_weights(
-        [block.reshape(-1, width + LANES) for block in payload_all],
-        [block.reshape(-1, width) for block in grads_all],
-        pick,
-        gate_all,
-        up_all,
+            if moment == 0:
+                received, prepared = lax.optimization_barrier((received, prepared))
+
+    moments, stored = lax.optimization_barrier((moments, stored))
+    terms[1] = attention_terms(1)
+
+    forward = (pick, gate_all, up_all)
+    tight = prepared is None
+
+    def halfway(terms):
+        pieces = sum_blocks(terms[0], terms[1], width // members)
+        arrived = [pieces[0]]
+        for k in range(1, max(members, groups)):
+            route = []
+            for i in range(members):
+                for e in range(groups):
+                    if k < members:
+                        route.append((i * groups + e, (i + k) % members * groups + e))
+                    if k < groups:
+                        base = (members + i) * groups
+                        route.append((base + e, base + (e ^ k)))
+            arrived.append(lax.ppermute(pieces[k], ("section", "dp", "expert"), route))
+        return arrived
+
+    first_grads = arrays["g0"][0].reshape(-1, width)
+    terms[0] = attention_terms(0) if tight else None
+    if tight:
+        shards = halfway(terms)
+        shards, first_grads = lax.optimization_barrier((shards, first_grads))
+    partial, made = first_weights(
+        3 + 2 * batches,
+        plans["weights", 0],
+        arrays,
+        arrays["p0"][0].reshape(-1, width + LANES),
+        first_grads,
         down_all,
+        prepared,
+        forward,
     )
-
-    kept = [
-        choose(
-            (stored[batch]["payloads"][0], stored[batch]["normed"], stored[batch]["attended"]),
-            (
-                stored[batch + 1]["payloads"][0],
-                stored[batch + 1]["normed"],
-                stored[batch + 1]["attended"],
-            ),
-        )
-        for batch in range(batches)
-    ]
+    keep_arrays(made)
+    if not tight:
+        stored, partial = lax.optimization_barrier((stored, partial))
+        terms[0] = attention_terms(0)
+    tokens = [arrays[name][0].reshape(-1, width + LANES) for name in ("p0", "p1")]
+    grads = [arrays[name][0].reshape(-1, width) for name in ("g0", "g1")]
+    totals = partial if tight else None
+    for expert in range(1, local):
+        totals = whole_weights(expert, tokens, grads, down_all, prepared, forward, totals)
+    small, terms, totals = lax.optimization_barrier((small, terms, totals))
+    small = sum_small(4 + 2 * batches, small[0], small[1])
+    if not tight:
+        terms, small = lax.optimization_barrier((terms, small))
+        shards = halfway(terms)
+    if totals is None:
+        totals = partial
+    totals = last_weights(
+        (0, 1),
+        tokens[-1],
+        grads[-1],
+        down_all,
+        prepared,
+        forward,
+        totals if tight else partial,
+        totals,
+    )
+    shards, totals = lax.optimization_barrier((shards, totals))
+    shard = total_of(shards)
+    shards = [shard] + [swap(shard, d, [0, 1]) for d in range(1, groups)]
+    gate_grad, up_grad, down_grad = totals
+    query_grad, key_grad, value_grad, out_grad = assemble(
+        shards,
+        [H * HD, KVH * HD, KVH * HD, width],
+    )
+
     final = [choose(moments[batch + 1], moments[batch]) for batch in range(batches)]
     layer_outputs = jnp.stack(
         [choose(produced[batch], produced[batch + 1]) for batch in range(batches)]
     )
     input_grads = jnp.stack([part[0] for part in final])
 
-    def stack(parts, axis):
-        return jnp.concatenate(parts, axis=axis)
-
-    normed_all = stack([kept[batch][1] for batch in range(batches)], 0)
-    attended_all = stack([kept[batch][2] for batch in range(batches)], 1)
-    turned_all = stack([part[1] for part in final], 2)
-    branch_all = stack([part[2] for part in final], 0)
-    part_width = width // groups
-    inner_grad = jnp.einsum(
-        "td,ect->edc", normed_all, turned_all, preferred_element_type=F32
-    ).astype(BF16)
-    out_grad = jnp.einsum(
-        "ct,ted->ecd",
-        attended_all,
-        branch_all.reshape(-1, groups, part_width),
-        preferred_element_type=F32,
-    ).astype(BF16)
-
-    def settle(blocks):
-        mine = scatter_sum(
-            lambda i: lax.dynamic_index_in_dim(blocks, i, 0, keepdims=False), "expert"
-        ).astype(BF16)
-        depth = mine.shape[0] // members
-        shard = scatter_sum(
-            lambda i: lax.dynamic_slice_in_dim(mine, i * depth, depth, 0), "dp"
-        ).astype(BF16)
-        everyone = jnp.zeros((groups,) + shard.shape, BF16)
-        for distance, piece in enumerate(spread(shard)):
-            everyone = lax.dynamic_update_index_in_dim(
-                everyone, piece, (me - distance) % groups, 0
-            )
-        return everyone
-
-    def join(block):
-        return jnp.moveaxis(block, 0, 1).reshape(block.shape[1], -1).astype(F32)
-
-    inner_grad = settle(inner_grad)
-    out_grad = settle(out_grad)
-    q_cols = H * HD // groups
-    kv_cols = KVH * HD // groups
-    query_grad = join(inner_grad[:, :, :q_cols])
-    key_grad = join(inner_grad[:, :, q_cols : q_cols + kv_cols])
-    value_grad = join(inner_grad[:, :, q_cols + kv_cols :])
-    out_grad = join(out_grad)
-
-    small = 0.0
-    for batch in range(batches):
-        router_part = jnp.einsum(
-            "te,td->ed",
-            final[batch][3][:, :experts_all],
-            kept[batch][0][:, :width],
-            preferred_element_type=F32,
-        )
-        small = small + jnp.concatenate([router_part, final[batch][4], final[batch][5]], axis=0)
-    small = lax.psum(small, ("dp", "expert"))
     depth = width // members
     router_grad = lax.dynamic_slice_in_dim(
         small[:experts_all], lax.axis_index("dp") * depth, depth, 1
@@ -1456,13 +2016,13 @@
     return (
         layer_outputs[None],
         input_grads[None],
-        small[experts_all][None],
+        small[SMALL - 2][None],
         query_grad[None],
         key_grad[None],
         value_grad[None],
         out_grad[None],
         router_grad[None],
-        small[experts_all + 1][None],
+        small[SMALL - 1][None],
         gate_grad[None],
         up_grad[None],
         down_grad[None],

time: 1090 us -> 811 us (0.74)
  the two profiles are of different devices: /device:TPU:0 before, /device:TPU:9 now
where the time goes in v2:
time: 811 us; the launch traced here: 798 us
  Pallas kernels  697 us (86%)
  waiting for transfers between devices  37 us (5%)
  starting transfers between devices  31.8 us (4%)
  local copies, waits for them, and re-layouts  18.1 us (2%)
  other arithmetic  13.1 us (2%)
    pallas_call x3, Pallas kernels, backward_layer(): pl.pallas_call(functools.partial(backward_kernel, sections, [section for...  168 us
    pallas_call x3, Pallas kernels, forward_layer(): pl.pallas_call(functools.partial(forward_kernel, sections, tasks, names,...  133 us
    pallas_call x1, Pallas kernels, gather_weights(): pl.pallas_call(gather_kernel, in_specs=[whole()] * 5, out_specs=[anywhere...  132 us
    pallas_call x2, Pallas kernels, whole_weights(): pl.pallas_call(functools.partial(whole_weights_kernel, ready, batches), g...  108 us
    pallas_call x1, Pallas kernels, first_weights(): pl.pallas_call(functools.partial(first_weights_kernel, ready, tasks, name...  79.8 us
    pallas_call x1, Pallas kernels, last_weights(): pl.pallas_call(functools.partial(last_weights_kernel, ready, chained), gr...  33.6 us
    ppermute x6, waiting for transfers between devices, swap(): return lax.ppermute(block, ('section', 'expert'), route)  25.5 us
    pallas_call x1, Pallas kernels, sum_small(): pl.pallas_call(small_kernel, in_specs=[pl.BlockSpec(memory_space=pl.ANY)]...  17.3 us
  transfers between devices with their start and end apart: 16, of which 6 were waited for; matrix products, arithmetic and copies ran while one was open for 1% of the time, Pallas kernels for 28%

profile of v2, /device:TPU:9, one launch (start us, length us, event | category | flops | bytes accessed | tf_op | source)
XLA Modules:
  0.0 797.7 jit_solution(5639835349584303568)
XLA Ops:
  0.7 0.8 fusion.22
  1.5 0.7 slice_bitcast_fusion.6
  2.4 0.8 copy.46
  3.3 1.8 slice_bitcast_fusion.5.refs_0_.refs_13_
  5.0 0.6 fusion.10.refs_8_.refs_6_.refs_2_
  5.7 0.8 multiply_sine_fusion
  6.4 0.4 fusion
  6.8 0.7 pad.4.router_ref
  7.5 0.7 broadcast_select_fusion.1
  8.2 132.2 %gather_weights.1 = (bf16[4,1536,640]{2,1,0:T(8,128)(2,1)}, bf16[4,1536,384]{2,1,0:T(8,128)(2,1)}, bf16[1536,128]{1,0:T(8,128)(2,1)}) custom-call(bf16[384,1536]{1,0:T(8,128)(2,1)} %bitcast.121, bf16[384,512]{1,0:T(8,128)(2,1)} %bitcast.123, bf16[384,512]{1,0:T(8,128)(2,1)} %bitcast.124, bf16[384,1536]{1,0:T(8,128)(2,1)} %bitcast.122, ...), custom_call_target="tpu_custom_call" | custom-call | tf_op jit(solution)/shard_map/gather_weights/pallas_call | solution.py:382
  140.7 0.9 pad_maximum_fusion.1
  141.6 2.0 forward_layer.3
  143.6 1.3 collective-permute-start
  144.9 0.6 compare_convert_fusion.1.refs_7_
  145.6 1.9 collective-permute-done
  147.5 0.8 bitcast_select_fusion.1.refs_0_.refs_13_
  148.3 61.4 %forward_layer.4 = (bf16[128,1536]{1,0:T(8,128)(2,1)}, bf16[1536,128]{1,0:T(8,128)(2,1)}, bf16[4,2,512,128]{3,2,1,0:T(8,128)(2,1)}, bf16[1536,128]{1,0:T(8,128)(...) custom-call(bf16[128,1536]{1,0:T(8,128)(2,1)} %bitcast_select_fusion, ...), custom_call_target="tpu_custom_call", output_to_operand_aliasing={{8}: (14, {})} | custom-call | flops 9261023232 | bytes 30000000 | tf_op jit(solution)/shard_map/forward_layer/pallas_call | solution.py:685
  209.6 1.3 collective-permute-start.1
  210.9 0.8 slice_bitcast_fusion.4.refs_0_
  211.7 6.6 collective-permute-done.1.refs_0_.refs_20_
  218.3 0.7 copy-done.8
  219.1 69.5 %forward_layer.5 = (bf16[128,1536]{1,0:T(8,128)(2,1)}, bf16[1536,128]{1,0:T(8,128)(2,1)}, bf16[4,2,512,128]{3,2,1,0:T(8,128)(2,1)}, bf16[1536,128]{1,0:T(8,128)(...) custom-call(bf16[128,1536]{1,0:T(8,128)(2,1)} %copy-done.8, ...), custom_call_target="tpu_custom_call", output_to_operand_aliasing={{8}: (14, {}), {9}: (15, {})} | custom-call | flops 9261023232 | bytes 30000000 | tf_op jit(solution)/shard_map/forward_layer/pallas_call | solution.py:685
  288.5 86.6 %backward_layer.3 = (f32[128,1536]{1,0:T(8,128)}, bf16[128,1536]{1,0:T(8,128)(2,1)}, bf16[4,640,128]{2,1,0:T(8,128)(2,1)}, bf16[128,1536]{1,0:T(8,128)(2,1)}, bf...) custom-call(bf16[128,1536]{1,0:T(8,128)(2,1)} %slice_bitcast_fusion., ...), custom_call_target="tpu_custom_call", output_to_operand_aliasing={{7}: (20, {}), {8}: (21, {})} | custom-call | flops 15703474176 | bytes 40000000 | tf_op jit(solution)/shard_map/backward_layer/pallas_call | solution.py:1070
  375.2 1.3 collective-permute-start.2
  376.5 1.5 collective-permute-done.2
  378.0 0.8 bitcast_select_fusion.refs_0_
  378.8 75.1 %backward_layer.4 = (f32[128,1536]{1,0:T(8,128)}, bf16[128,1536]{1,0:T(8,128)(2,1)}, bf16[4,640,128]{2,1,0:T(8,128)(2,1)}, bf16[128,1536]{1,0:T(8,128)(2,1)}, bf...) custom-call(bf16[128,1536]{1,0:T(8,128)(2,1)} %bitcast_select_fusion, ...), custom_call_target="tpu_custom_call", output_to_operand_aliasing={{7}: (27, {})} | custom-call | flops 15703474176 | bytes 40000000 | tf_op jit(solution)/shard_map/backward_layer/pallas_call | solution.py:1070
  453.9 5.9 collective-permute-start.3
  459.9 1.5 collective-permute-done.3.refs_0_
  461.4 0.7 copy-done.12
  462.2 6.6 backward_layer.5
  468.7 1.8 slice_bitcast_fusion.refs_12_
  470.5 0.8 slice_bitcast_fusion.1.refs_4_
  471.3 10.6 %attention_weights.3 = (bf16[1536,1024]{1,0:T(8,128)(2,1)}, bf16[1536,1024]{1,0:T(8,128)(2,1)}, bf16[1536,1024]{1,0:T(8,128)(2,1)}, bf16[1536,1024]{1,0:T(8,128)(2,1)}, f32[24,1536]{1,0:T(8,128)}) custom-call(bf16[128,1536]{1,0:T(8,128)(2,1)} %get-tuple-element.260.refs_8_.refs_0_, bf16[4,640,128]{2,1,0:T(8,128)(2,1)} %get-tuple-element.269.refs_1_, ...), custom_call_target="tpu_custom_call" | custom-call | flops 3221225472 | bytes 20000000 | tf_op jit(solution)/shard_map/attention_weights/pallas_call | solution.py:1531
  481.9 2.2 collective-permute-start.7
  484.2 0.9 maximum_bitcast_fusion.1
  485.2 4.9 collective-permute-start.8
  490.0 2.4 collective-permute-start.9
  492.4 79.8 %first_weights.1 = (f32[3,1536,512]{2,1,0:T(8,128)}, f32[3,1536,512]{2,1,0:T(8,128)}, f32[3,512,1536]{2,1,0:T(8,128)}, bf16[1,4,4,128,1664]{4,3,2,1,0:T(8,128)(2,1)}, bf16[1,4,4,128,1536]{4,3,2,1,0:T(8,128)(2,1)}) custom-call(bf16[2048,1664]{1,0:T(8,128)(2,1)} %bitcast.105, ...), custom_call_target="tpu_custom_call", output_to_operand_aliasing={{3}: (9, {}), {4}: (10, {})} | custom-call | flops 12884901888 | bytes 18874368 | tf_op jit(solution)/shard_map/first_weights/pallas_call | solution.py:1299
  572.2 0.8 slice_bitcast_fusion.2.refs_12_
  573.0 1.8 slice_bitcast_fusion.3.refs_4_
  574.8 0.3 attention_weights.2
  575.1 2.3 collective-permute-start.4
  577.5 2.3 collective-permute-start.5
  579.8 2.3 collective-permute-start.6
  582.1 53.9 %whole_weights.2 = (f32[3,1536,512]{2,1,0:T(8,128)}, f32[3,1536,512]{2,1,0:T(8,128)}, f32[3,512,1536]{2,1,0:T(8,128)}) custom-call(bf16[2048,1664]{1,0:T(8,128)(2,1)} %bitcast.106, bf16[2048,1664]{1,0:T(8,128)(2,1)} %bitcast.109, bf16[2048,1536]{1,0:T(8,128)(2,1)} %bitcast.119, bf16[2048,1536]{1,0:T(8,128)(2,1)} %bitcast.112, ...), custom_call_target="tpu_custom_call" | custom-call | flops 25769803776 | bytes 37748736 | tf_op jit(solution)/shard_map/whole_weights/pallas_call | solution.py:1362
  635.9 2.4 select_bitcast_fusion.1
  638.3 54.3 %whole_weights.3 = (f32[3,1536,512]{2,1,0:T(8,128)}, f32[3,1536,512]{2,1,0:T(8,128)}, f32[3,512,1536]{2,1,0:T(8,128)}) custom-call(bf16[2048,1664]{1,0:T(8,128)(2,1)} %bitcast.107, bf16[2048,1664]{1,0:T(8,128)(2,1)} %bitcast.110, bf16[2048,1536]{1,0:T(8,128)(2,1)} %bitcast.120, ...), custom_call_target="tpu_custom_call", output_to_operand_aliasing={{0}: (11, {}), {1}: (12, {}), {2}: (13, {})} | custom-call | flops 25769803776 | bytes 37748736 | tf_op jit(solution)/shard_map/whole_weights/pallas_call | solution.py:1362
  692.6 17.3 %sum_small.1 = f32[24,1536]{1,0:T(8,128)} custom-call(f32[24,1536]{1,0:T(8,128)} %get-tuple-element.299.upper, f32[24,1536]{1,0:T(8,128)} %get-tuple-element.300.lower), custom_call_target="tpu_custom_call" | custom-call | tf_op jit(solution)/shard_map/sum_small/pallas_call | solution.py:1641
  709.9 8.6 %sum_blocks.1 = bf16[1536,1024]{1,0:T(8,128)(2,1)} custom-call(bf16[1536,1024]{1,0:T(8,128)(2,1)} %get-tuple-element.302.refs_0_, bf16[1536,1024]{1,0:T(8,128)(2,1)} %collective-permute-done.4.refs_1_, bf16[1536,1024]{1,0:T(8,128)(2,1)} %collective-permute-done.5.refs_2_, bf16[1536,1024]{1,0:T(8,128)(2,1)} %collective-permute-done.6.refs_3_, ...), custom_call_target="tpu_custom_call" | custom-call | bytes 15728640 | tf_op jit(solution)/shard_map/sum_blocks/pallas_call | solution.py:1596
  718.5 3.6 fusion.20
  722.0 1.6 collective-permute-start.10
  723.6 1.2 collective-permute-start.12
  724.8 33.6 %last_weights.1 = (f32[3,1536,512]{2,1,0:T(8,128)}, f32[3,1536,512]{2,1,0:T(8,128)}, f32[3,512,1536]{2,1,0:T(8,128)}) custom-call(bf16[2048,1664]{1,0:T(8,128)(2,1)} %bitcast.111, bf16[2048,1536]{1,0:T(8,128)(2,1)} %bitcast.114, bf16[3,512,1536]{2,1,0:T(8,128)(2,1)} %bitcast.103, ...), custom_call_target="tpu_custom_call", output_to_operand_aliasing={{0}: (12, {}), {1}: (13, {}), {2}: (14, {})} | custom-call | flops 12884901888 | bytes 18874368 | tf_op jit(solution)/shard_map/last_weights/pallas_call | solution.py:1420
  758.4 2.5 add_convert_fusion.refs_0_
  761.0 1.5 collective-permute-start.13
  762.5 1.3 collective-permute-start.15
  763.8 1.3 maximum_bitcast_fusion
  765.0 0.6 copy.49
  765.7 0.6 fusion.21
  766.3 14.5 %collective-permute-done.13.refs_1_ = bf16[384,1024]{1,0:T(8,128)(2,1)S(1)} collective-permute-done((bf16[384,1024]{1,0:T(8,128)(2,1)S(1)}, bf16[384,1024]{1,0:T(8,128)(2,1)S(1)}, u32[]{:S(2)}, u32[]{:S(2)}) %collective-permute-start.13) | collective-permute-done | bytes 786464 | tf_op jit(solution)/shard_map/ppermute | solution.py:1698
  780.8 10.9 %collective-permute-done.14.refs_2_ = bf16[384,1024]{1,0:T(8,128)(2,1)S(1)} collective-permute-done((bf16[384,1024]{1,0:T(8,128)(2,1)S(1)}, bf16[384,1024]{1,0:T(8,128)(2,1)S(1)}, u32[]{:S(2)}, u32[]{:S(2)}) %collective-permute-start.14) | collective-permute-done | bytes 786464 | tf_op jit(solution)/shard_map/ppermute | solution.py:1698
  791.7 0.9 copy-done.5
  792.6 4.9 assemble.1
  (49 shorter events, 0.7 us)
Async XLA Ops:
  141.6 5.9 copy-start.2
  143.6 3.8 collective-permute-start
  148.3 62.7 %copy-start.3 = (bf16[2,128,1536]{2,1,0:T(8,128)(2,1)S(1)}, bf16[2,128,1536]{2,1,0:T(8,128)(2,1)}, u32[]{:S(2)}) copy-start(bf16[2,128,1536]{2,1,0:T(8,128)(2,1)} %param.15) | copy-start | bytes 2359300
  209.6 8.7 %collective-permute-start.1 = (bf16[128,1536]{1,0:T(8,128)(2,1)}, bf16[128,1536]{1,0:T(8,128)(2,1)S(1)}, u32[]{:S(2)}, u32[]{:S(2)}) collective-permute-start(bf16[128,1536]{1,0:T(8,128)(2,1)} %get-tuple-element.176), channel_id=1, source_target_pairs={{0,16},{1,17},{2,18},{3,19},{4,20},{5,21},{6,22},{7,23},{8,24},{9,... | collective-permute-start | bytes 1179656 | tf_op jit(solution)/shard_map/ppermute | solution.py:66
  218.3 0.7 copy-start.8
  375.2 2.8 collective-permute-start.2
  453.9 7.5 collective-permute-start.3
  461.4 0.7 copy-start.12
  462.2 8.4 %copy-start.7 = (bf16[4,128,1664]{2,1,0:T(8,128)(2,1)S(1)}, bf16[4,128,1664]{2,1,0:T(8,128)(2,1)}, u32[]{:S(2)}) copy-start(bf16[4,128,1664]{2,1,0:T(8,128)(2,1)} %get-tuple-element.264.refs_19_) | copy-start | bytes 5111812
  471.3 12.8 %copy-start.9 = (bf16[128,1536]{1,0:T(8,128)(2,1)S(1)}, bf16[128,1536]{1,0:T(8,128)(2,1)}, u32[]{:S(2)}) copy-start(bf16[128,1536]{1,0:T(8,128)(2,1)} %get-tuple-element.174) | copy-start | bytes 1179652
  471.3 12.8 %copy-start.10 = (bf16[128,1536]{1,0:T(8,128)(2,1)S(1)}, bf16[128,1536]{1,0:T(8,128)(2,1)}, u32[]{:S(2)}) copy-start(bf16[128,1536]{1,0:T(8,128)(2,1)} %get-tuple-element.176) | copy-start | bytes 1179652
  471.3 12.8 %copy-start.11 = (bf16[128,1536]{1,0:T(8,128)(2,1)S(1)}, bf16[128,1536]{1,0:T(8,128)(2,1)}, u32[]{:S(2)}) copy-start(bf16[128,1536]{1,0:T(8,128)(2,1)} %get-tuple-element.179) | copy-start | bytes 1179652
  481.9 97.9 %collective-permute-start.7 = (bf16[1536,1024]{1,0:T(8,128)(2,1)}, bf16[1536,1024]{1,0:T(8,128)(2,1)}, u32[]{:S(2)}, u32[]{:S(2)}) collective-permute-start(bf16[1536,1024]{1,0:T(8,128)(2,1)} %get-tuple-element.280), channel_id=1, source_target_pairs={{16,20},{20,24},{24,28},{28,16},{17,21},{21,25},{25,29},{29,17},{1... | collective-permute-start | bytes 9437192 | tf_op jit(solution)/shard_map/ppermute | solution.py:60
  485.2 207.4 %collective-permute-start.8 = (bf16[1536,1024]{1,0:T(8,128)(2,1)}, bf16[1536,1024]{1,0:T(8,128)(2,1)}, u32[]{:S(2)}, u32[]{:S(2)}) collective-permute-start(bf16[1536,1024]{1,0:T(8,128)(2,1)} %get-tuple-element.281), channel_id=1, source_target_pairs={{16,24},{20,28},{24,16},{28,20},{17,25},{21,29},{25,17},{29,21},{1... | collective-permute-start | bytes 9437192 | tf_op jit(solution)/shard_map/ppermute | solution.py:60
  490.0 202.6 %collective-permute-start.9 = (bf16[1536,1024]{1,0:T(8,128)(2,1)}, bf16[1536,1024]{1,0:T(8,128)(2,1)}, u32[]{:S(2)}, u32[]{:S(2)}) collective-permute-start(bf16[1536,1024]{1,0:T(8,128)(2,1)} %get-tuple-element.282), channel_id=1, source_target_pairs={{16,28},{20,16},{24,20},{28,24},{17,29},{21,17},{25,21},{29,25},{1... | collective-permute-start | bytes 9437192 | tf_op jit(solution)/shard_map/ppermute | solution.py:60
  575.1 117.5 %collective-permute-start.4 = (bf16[1536,1024]{1,0:T(8,128)(2,1)}, bf16[1536,1024]{1,0:T(8,128)(2,1)}, u32[]{:S(2)}, u32[]{:S(2)}) collective-permute-start(bf16[1536,1024]{1,0:T(8,128)(2,1)} %get-tuple-element.276), channel_id=1, source_target_pairs={{0,1},{1,0},{2,3},{3,2},{4,5},{5,4},{6,7},{7,6},{8,9},{9,8},{10,11... | collective-permute-start | bytes 9437192 | tf_op jit(solution)/shard_map/ppermute | solution.py:1698
  577.5 115.2 %collective-permute-start.5 = (bf16[1536,1024]{1,0:T(8,128)(2,1)}, bf16[1536,1024]{1,0:T(8,128)(2,1)}, u32[]{:S(2)}, u32[]{:S(2)}) collective-permute-start(bf16[1536,1024]{1,0:T(8,128)(2,1)} %get-tuple-element.277), channel_id=1, source_target_pairs={{0,2},{1,3},{2,0},{3,1},{4,6},{5,7},{6,4},{7,5},{8,10},{9,11},{10,... | collective-permute-start | bytes 9437192 | tf_op jit(solution)/shard_map/ppermute | solution.py:1698
  579.8 112.8 %collective-permute-start.6 = (bf16[1536,1024]{1,0:T(8,128)(2,1)}, bf16[1536,1024]{1,0:T(8,128)(2,1)}, u32[]{:S(2)}, u32[]{:S(2)}) collective-permute-start(bf16[1536,1024]{1,0:T(8,128)(2,1)} %get-tuple-element.278), channel_id=1, source_target_pairs={{0,3},{1,2},{2,1},{3,0},{4,7},{5,6},{6,5},{7,4},{8,11},{9,10},{10,... | collective-permute-start | bytes 9437192 | tf_op jit(solution)/shard_map/ppermute | solution.py:1698
  722.0 36.3 %collective-permute-start.10 = (bf16[384,1024]{1,0:T(8,128)(2,1)}, bf16[384,1024]{1,0:T(8,128)(2,1)}, u32[]{:S(2)}, u32[]{:S(2)}) collective-permute-start(bf16[384,1024]{1,0:T(8,128)(2,1)} %get-tuple-element.356), channel_id=1, source_target_pairs={{0,4},{16,17},{1,5},{17,16},{2,6},{18,19},{3,7},{19,18},{4,8},{20,... | collective-permute-start | bytes 2359304 | tf_op jit(solution)/shard_map/ppermute | solution.py:1953
  723.6 34.8 %collective-permute-start.11 = (bf16[384,1024]{1,0:T(8,128)(2,1)}, bf16[384,1024]{1,0:T(8,128)(2,1)}, u32[]{:S(2)}, u32[]{:S(2)}) collective-permute-start(bf16[384,1024]{1,0:T(8,128)(2,1)} %get-tuple-element.355), channel_id=1, source_target_pairs={{0,8},{16,18},{1,9},{17,19},{2,10},{18,16},{3,11},{19,17},{4,12},{... | collective-permute-start | bytes 2359304 | tf_op jit(solution)/shard_map/ppermute | solution.py:1953
  723.6 34.8 %collective-permute-start.12 = (bf16[384,1024]{1,0:T(8,128)(2,1)}, bf16[384,1024]{1,0:T(8,128)(2,1)}, u32[]{:S(2)}, u32[]{:S(2)}) collective-permute-start(bf16[384,1024]{1,0:T(8,128)(2,1)} %get-tuple-element.354), channel_id=1, source_target_pairs={{0,12},{16,19},{1,13},{17,18},{2,14},{18,17},{3,15},{19,16},{4,0},... | collective-permute-start | bytes 2359304 | tf_op jit(solution)/shard_map/ppermute | solution.py:1953
  758.4 5.4 copy-start
  758.4 6.6 slice-start
  758.4 7.3 copy-start.6
  761.0 30.8 %copy-start.1 = (bf16[384,1024]{1,0:T(8,128)(2,1)}, bf16[384,1024]{1,0:T(8,128)(2,1)S(1)}, u32[]{:S(2)}) copy-start(bf16[384,1024]{1,0:T(8,128)(2,1)S(1)} %add_convert_fusion.refs_0_) | copy-start | bytes 2359300
  761.0 19.8 %collective-permute-start.13 = (bf16[384,1024]{1,0:T(8,128)(2,1)S(1)}, bf16[384,1024]{1,0:T(8,128)(2,1)S(1)}, u32[]{:S(2)}, u32[]{:S(2)}) collective-permute-start(bf16[384,1024]{1,0:T(8,128)(2,1)S(1)} %add_convert_fusion.refs_0_), channel_id=1, source_target_pairs={{0,1},{1,0},{2,3},{3,2},{16,17},{17,16},{18,19},{19,18},{4,5},{5,4... | collective-permute-start | bytes 2359304 | tf_op jit(solution)/shard_map/ppermute | solution.py:1698
  762.5 29.2 %collective-permute-start.14 = (bf16[384,1024]{1,0:T(8,128)(2,1)S(1)}, bf16[384,1024]{1,0:T(8,128)(2,1)S(1)}, u32[]{:S(2)}, u32[]{:S(2)}) collective-permute-start(bf16[384,1024]{1,0:T(8,128)(2,1)S(1)} %add_convert_fusion.refs_0_), channel_id=1, source_target_pairs={{0,2},{1,3},{2,0},{3,1},{16,18},{17,19},{18,16},{19,17},{4,6},{5,7... | collective-permute-start | bytes 2359304 | tf_op jit(solution)/shard_map/ppermute | solution.py:1698
  762.5 29.2 %collective-permute-start.15 = (bf16[384,1024]{1,0:T(8,128)(2,1)S(1)}, bf16[384,1024]{1,0:T(8,128)(2,1)}, u32[]{:S(2)}, u32[]{:S(2)}) collective-permute-start(bf16[384,1024]{1,0:T(8,128)(2,1)S(1)} %add_convert_fusion.refs_0_), channel_id=1, source_target_pairs={{0,3},{1,2},{2,1},{3,0},{16,19},{17,18},{18,17},{19,16},{4,7},{5,6... | collective-permute-start | bytes 2359304 | tf_op jit(solution)/shard_map/ppermute | solution.py:1698
  780.8 11.0 %copy-start.4 = (bf16[384,1024]{1,0:T(8,128)(2,1)}, bf16[384,1024]{1,0:T(8,128)(2,1)S(1)}, u32[]{:S(2)}) copy-start(bf16[384,1024]{1,0:T(8,128)(2,1)S(1)} %collective-permute-done.13.refs_1_) | copy-start | bytes 2359300
  791.7 0.9 copy-start.5

commit v3 on v2

--- a/solution.py
+++ b/solution.py
@@ -21,7 +21,7 @@
 SCALE = HD ** (-0.5)
 VMEM = 60 * 1024 * 1024
 PREPARED = 8192
-SMALL = 24
+SMALL = 16
 LARGE = 63 * 1024 * 1024
 
 F32 = jnp.float32
@@ -247,8 +247,8 @@
             in_section(section)(lambda peers=peers: greet(peers))
 
 
-def gather_kernel(q_ref, k_ref, v_ref, o_ref, router_ref, inner, out, router, *sems):
-    local_sem, line_sem, plane_sem, router_sem, turn_sem = sems
+def gather_kernel(q_ref, k_ref, v_ref, o_ref, router_ref, inner, out, router, *scratch):
+    inner_room, out_room, local_sem, line_sem, plane_sem, router_sem, turn_sem = scratch
     blocks = inner.shape[0]
     depth = q_ref.shape[0]
     members = inner.shape[1] // depth
@@ -257,29 +257,28 @@
     section = lax.axis_index("section")
     diagonal = partner(me, blocks - 1)
     gathered = (inner, out)
-    pieces = []
-    at = 0
-    for source in (q_ref, k_ref, v_ref):
-        pieces.append((source, inner, at, source.shape[1] // blocks))
-        at += source.shape[1] // blocks
-    pieces.append((o_ref, out, 0, o_ref.shape[1] // blocks))
-    sent = [(i, me) for i in range(4)] + [(3, diagonal)] + [(i, diagonal) for i in range(3)]
+    rooms = (inner_room, out_room)
+    sent = ((0, 0), (1, 0), (1, blocks - 1), (0, blocks - 1))
 
     def rows(member):
         return pl.ds(pl.multiple_of(member * depth, depth), depth)
 
-    def ends(i, e):
-        source, target, start, part = pieces[i]
-        return (
-            source.at[:, pl.ds(pl.multiple_of(e * part, LANES), part)],
-            target.at[e, rows(place), pl.ds(start, part)],
-        )
+    def fill(d):
+        e = partner(me, d)
+        at = 0
+        for source in (q_ref, k_ref, v_ref):
+            part = source.shape[1] // blocks
+            columns = pl.ds(pl.multiple_of(e * part, LANES), part)
+            inner_room[d, :, at : at + part] = source[:, columns]
+            at += part
+        part = o_ref.shape[1] // blocks
+        out_room[d] = o_ref[:, pl.ds(pl.multiple_of(e * part, LANES), part)]
 
     def line(which, k):
-        source, target = ends(*sent[which])
+        array, d = sent[which]
         return send(
-            source,
-            target,
+            rooms[array].at[d],
+            gathered[array].at[partner(me, d), rows(place)],
             line_sem.at[0, which, k - 1],
             line_sem.at[1, which, k - 1],
             line_peers(members)[k - 1],
@@ -305,13 +304,15 @@
         )
 
     other = (1 - section, place, me)
+    fill(0)
+    fill(blocks - 1)
     greet(plane_peers(blocks) + line_peers(members) + [other])
 
     @in_section(1)
     def _():
         pl.semaphore_wait(turn_sem, 1)
 
-    for which in range(5):
+    for which in range(3):
         for k in range(1, members):
             line(which, k).start()
     for k in range(1, members):
@@ -319,32 +320,36 @@
 
     @in_section(1)
     def _():
-        for which in range(5, 8):
-            for k in range(1, members):
-                line(which, k).start()
-
-    copies = [pltpu.make_async_copy(router_ref, router.at[rows(place)], local_sem.at[4 * blocks])]
-    for e in range(blocks):
-        for i in range(4):
-            copies.append(pltpu.make_async_copy(*ends(i, e), local_sem.at[4 * e + i]))
+        for k in range(1, members):
+            line(3, k).start()
+
+    for d in range(1, blocks - 1):
+        fill(d)
+    copies = [pltpu.make_async_copy(router_ref, router.at[rows(place)], local_sem.at[2 * blocks])]
+    for d in range(blocks):
+        for array in range(2):
+            copies.append(
+                pltpu.make_async_copy(
+                    rooms[array].at[d],
+                    gathered[array].at[partner(me, d), rows(place)],
+                    local_sem.at[2 * d + array],
+                )
+            )
     for copy in copies:
         copy.start()
+    for which in range(2):
+        for k in range(1, members):
+            line(which, k).wait_recv()
+            for d in range(1, blocks - 1):
+                plane(which, k, d).start()
+            if which == 0:
+
+                @in_section(0)
+                def _(k=k):
+                    plane(0, k, blocks - 1).start()
+
     for k in range(1, members):
-        for which in range(3):
-            line(which, k).wait_recv()
-        for d in range(1, blocks - 1):
-            plane(0, k, d).start()
-
-        @in_section(0)
-        def _(k=k):
-            plane(0, k, blocks - 1).start()
-
-    for k in range(1, members):
-        line(3, k).wait_recv()
-        for d in range(1, blocks - 1):
-            plane(1, k, d).start()
-    for k in range(1, members):
-        line(4, k).wait_recv()
+        line(2, k).wait_recv()
         narrow(k).wait()
 
     @in_section(0)
@@ -354,7 +359,7 @@
         )
 
     for k in range(1, members):
-        for which in range(5):
+        for which in range(3):
             line(which, k).wait_send()
         for which in range(2):
             for d in range(1, blocks - 1):
@@ -366,8 +371,7 @@
 
         @in_section(1)
         def _(k=k):
-            for which in range(5, 8):
-                line(which, k).wait()
+            line(3, k).wait()
 
     for copy in copies:
         copy.wait()
@@ -389,8 +393,10 @@
             shape((depth * members, LANES), BF16),
         ],
         scratch_shapes=[
-            pltpu.SemaphoreType.DMA((1 + 4 * blocks,)),
-            pltpu.SemaphoreType.DMA((2, 8, members - 1)),
+            pltpu.VMEM((blocks, depth, wide), BF16),
+            pltpu.VMEM((blocks, depth, o.shape[1] // blocks), BF16),
+            pltpu.SemaphoreType.DMA((1 + 2 * blocks,)),
+            pltpu.SemaphoreType.DMA((2, 4, members - 1)),
             pltpu.SemaphoreType.DMA((2, 2, members - 1, blocks - 1)),
             pltpu.SemaphoreType.DMA((2, members - 1)),
             pltpu.SemaphoreType.REGULAR,
@@ -1278,16 +1284,19 @@
         for out in outs:
             out[...] = jnp.zeros_like(out)
 
-    weights_both(ready, x_ref, g_ref, down_ref, held, outs)
-
     @pl.when(step == pl.num_programs(0) * pl.num_programs(1) - 1)
     def _():
         enter([], late, dests[0].shape[2])
         run_relays(late, Relay.forward)
+
+    weights_both(ready, x_ref, g_ref, down_ref, held, outs)
+
+    @pl.when(step == pl.num_programs(0) * pl.num_programs(1) - 1)
+    def _():
         run_relays(relays, Relay.finish)
 
 
-def first_weights(number, tasks, arrays, tokens, grads, down_all, prepared, forward, tile=512):
+def first_weights(number, tasks, arrays, experts, tokens, grads, down_all, prepared, forward, tile=512):
     local, hidden, width = down_all.shape
     names, before, dests = relay_arrays(tasks, arrays)
     _, members, blocks, _, _ = dests[0].shape
@@ -1298,7 +1307,7 @@
     anywhere = pl.BlockSpec(memory_space=pl.ANY)
     results = pl.pallas_call(
         functools.partial(first_weights_kernel, ready, tasks, names),
-        grid=(1, rows // tile),
+        grid=(experts, rows // tile),
         in_specs=specs + [anywhere] * len(names),
         out_specs=outs + [anywhere] * len(names),
         out_shape=[
@@ -1315,7 +1324,9 @@
             has_side_effects=True,
             dimension_semantics=("arbitrary", "arbitrary"),
         ),
-        cost_estimate=cost(8 * rows * width * hidden, rows * (4 * width + 6 * hidden)),
+        cost_estimate=cost(
+            8 * rows * width * hidden * experts, rows * (4 * width + 6 * hidden) * experts
+        ),
         name="first_weights",
     )(tokens, grads, down_all, *(prepared if ready else ()), *forward, *before)
     return results[:3], dict(zip(names, results[3:]))
@@ -1605,7 +1616,7 @@
     return jnp.split(total, rows // depth, axis=0)
 
 
-def small_kernel(upper, lower, total, own, plane, line, fetch_sem, plane_sem, line_sem):
+def small_kernel(upper, lower, total, own, sent, plane, line, fetch_sem, plane_sem, line_sem):
     blocks = plane.shape[0] + 1
     members = line.shape[0] + 1
     for section, source in ((0, upper), (1, lower)):
@@ -1621,8 +1632,9 @@
         (plane_peers(blocks), plane, plane_sem),
         (line_peers(members), line, line_sem),
     ):
+        sent[...] = own[...].astype(BF16)
         copies = [
-            send(own, room.at[i], sems.at[0, i], sems.at[1, i], peer) for i, peer in enumerate(peers)
+            send(sent, room.at[i], sems.at[0, i], sems.at[1, i], peer) for i, peer in enumerate(peers)
         ]
         for copy in copies:
             copy.start()
@@ -1630,7 +1642,7 @@
             copy.wait()
         held = own[...]
         for i in range(len(peers)):
-            held = held + room[i]
+            held = held + room[i].astype(F32)
         own[...] = held
     total[...] = own[...]
 
@@ -1645,8 +1657,9 @@
         out_shape=shape(upper.shape, F32),
         scratch_shapes=[
             pltpu.VMEM(upper.shape, F32),
-            pltpu.VMEM((blocks - 1,) + upper.shape, F32),
-            pltpu.VMEM((members - 1,) + upper.shape, F32),
+            pltpu.VMEM(upper.shape, BF16),
+            pltpu.VMEM((blocks - 1,) + upper.shape, BF16),
+            pltpu.VMEM((members - 1,) + upper.shape, BF16),
             pltpu.SemaphoreType.DMA(()),
             pltpu.SemaphoreType.DMA((2, blocks - 1)),
             pltpu.SemaphoreType.DMA((2, members - 1)),
@@ -1798,15 +1811,15 @@
             (1, ("keep",), "p0", 0, True),
         ],
         ("forward", 2): [
-            (1, ("line",), "p0", 0, True),
-            (0, ("line", "plane"), "p1", 0, False),
+            (1, ("line",), "p0", 0, False),
+            (0, ("line", "plane"), "p1", 0, True),
             (0, ("plane",), "p0", 0, True),
             (1, ("keep",), "p1", 0, True),
         ],
         ("backward", 0): [
             (1, ("keep", "line"), "g0", 0, True),
             (1, ("line",), "p1", 0, True),
-            (1, ("plane",), "p0", 0, True),
+            (1, ("plane",), "p0", 0, False),
         ],
         ("backward", 1): [
             (0, ("keep", "line"), "g0", 0, True),
@@ -1937,6 +1950,7 @@
 
     forward = (pick, gate_all, up_all)
     tight = prepared is None
+    some = 1
 
     def halfway(terms):
         pieces = sum_blocks(terms[0], terms[1], width // members)
@@ -1962,6 +1976,7 @@
         3 + 2 * batches,
         plans["weights", 0],
         arrays,
+        some,
         arrays["p0"][0].reshape(-1, width + LANES),
         first_grads,
         down_all,
@@ -1975,28 +1990,32 @@
     tokens = [arrays[name][0].reshape(-1, width + LANES) for name in ("p0", "p1")]
     grads = [arrays[name][0].reshape(-1, width) for name in ("g0", "g1")]
     totals = partial if tight else None
-    for expert in range(1, local):
+    for expert in range(some, local):
         totals = whole_weights(expert, tokens, grads, down_all, prepared, forward, totals)
-    small, terms, totals = lax.optimization_barrier((small, terms, totals))
-    small = sum_small(4 + 2 * batches, small[0], small[1])
     if not tight:
-        terms, small = lax.optimization_barrier((terms, small))
+        terms, totals = lax.optimization_barrier((terms, totals))
         shards = halfway(terms)
     if totals is None:
         totals = partial
-    totals = last_weights(
-        (0, 1),
-        tokens[-1],
-        grads[-1],
-        down_all,
-        prepared,
-        forward,
-        totals if tight else partial,
-        totals,
-    )
+    for expert in range(some):
+        totals = last_weights(
+            (expert, expert + 1),
+            tokens[-1],
+            grads[-1],
+            down_all,
+            prepared,
+            forward,
+            totals if tight else partial,
+            totals,
+        )
+        if expert == max(some - 2, 0):
+            shards, totals, small = lax.optimization_barrier((shards, totals, small))
+            shard = total_of(shards)
+            shard, small = lax.optimization_barrier((shard, small))
+            small = sum_small(4 + 2 * batches, small[0], small[1])
+            shard, small = lax.optimization_barrier((shard, small))
+            shards = [shard] + [swap(shard, d, [0, 1]) for d in range(1, groups)]
     shards, totals = lax.optimization_barrier((shards, totals))
-    shard = total_of(shards)
-    shards = [shard] + [swap(shard, d, [0, 1]) for d in range(1, groups)]
     gate_grad, up_grad, down_grad = totals
     query_grad, key_grad, value_grad, out_grad = assemble(
         shards,

time: 811 us -> 775 us (0.956)
  the two profiles are of different devices: /device:TPU:9 before, /device:TPU:0 now
where the time goes in v3:
time: 775 us; the launch traced here: 765 us
  Pallas kernels  664 us (86%)
  starting transfers between devices  40.3 us (5%)
  waiting for transfers between devices  27 us (3%)
  local copies, waits for them, and re-layouts  19.7 us (3%)
  other arithmetic  13.1 us (2%)
    pallas_call x3, Pallas kernels, forward_layer(): pl.pallas_call(functools.partial(forward_kernel, sections, tasks, names,...  208 us
    pallas_call x3, Pallas kernels, backward_layer(): pl.pallas_call(functools.partial(backward_kernel, sections, [section for...  141 us
    pallas_call x2, Pallas kernels, whole_weights(): pl.pallas_call(functools.partial(whole_weights_kernel, ready, batches), g...  78.6 us
    pallas_call x1, Pallas kernels, prepare(): pl.pallas_call(functools.partial(prepare_kernel, min(tile, tokens[0].shap...  64.1 us
    pallas_call x1, Pallas kernels, gather_weights(): pl.pallas_call(gather_kernel, in_specs=[whole()] * 5, out_specs=[anywhere...  60.9 us
    pallas_call x1, Pallas kernels, first_weights(): pl.pallas_call(functools.partial(first_weights_kernel, ready, tasks, name...  42.1 us
    pallas_call x1, Pallas kernels, last_weights(): pl.pallas_call(functools.partial(last_weights_kernel, ready, chained), gr...  26.2 us
    ppermute x6, waiting for transfers between devices, swap(): return lax.ppermute(block, ('section', 'expert'), route)  22.7 us
  transfers between devices with their start and end apart: 16, of which 6 were waited for; matrix products, arithmetic and copies ran while one was open for 2% of the time, Pallas kernels for 29%

profile of v3, /device:TPU:0, one launch (start us, length us, event | category | flops | bytes accessed | tf_op | source)
XLA Modules:
  0.0 765.1 jit_solution(3036813659268038177)
XLA Ops:
  0.7 0.8 fusion.22
  1.5 0.7 slice_bitcast_fusion.6
  2.4 0.8 copy.46
  3.3 1.8 slice_bitcast_fusion.5.refs_0_.refs_13_
  5.0 0.6 fusion.10.refs_8_.refs_6_.refs_2_
  5.7 0.8 multiply_sine_fusion
  6.8 0.7 pad.4.router_ref
  7.5 0.7 broadcast_select_fusion.1
  8.2 60.9 %gather_weights.1 = (bf16[4,1536,640]{2,1,0:T(8,128)(2,1)}, bf16[4,1536,384]{2,1,0:T(8,128)(2,1)}, bf16[1536,128]{1,0:T(8,128)(2,1)}) custom-call(bf16[384,1536]{1,0:T(8,128)(2,1)} %bitcast.122, bf16[384,512]{1,0:T(8,128)(2,1)} %bitcast.124, bf16[384,512]{1,0:T(8,128)(2,1)} %bitcast.125, bf16[384,1536]{1,0:T(8,128)(2,1)} %bitcast.123, ...), custom_call_target="tpu_custom_call" | custom-call | tf_op jit(solution)/shard_map/gather_weights/pallas_call | solution.py:386
  69.4 0.9 pad_maximum_fusion.1
  70.3 60.3 %forward_layer.3 = (bf16[128,1536]{1,0:T(8,128)(2,1)}, bf16[1536,128]{1,0:T(8,128)(2,1)}, bf16[4,2,512,128]{3,2,1,0:T(8,128)(2,1)}, bf16[1536,128]{1,0:T(8,128)(...) custom-call(bf16[128,1536]{1,0:T(8,128)(2,1)} %slice_bitcast_fusion., ...), custom_call_target="tpu_custom_call" | custom-call | flops 9261023232 | bytes 30000000 | tf_op jit(solution)/shard_map/forward_layer/pallas_call | solution.py:691
  130.6 11.6 %collective-permute-start = (bf16[128,1536]{1,0:T(8,128)(2,1)}, bf16[128,1536]{1,0:T(8,128)(2,1)S(1)}, u32[]{:S(2)}, u32[]{:S(2)}) collective-permute-start(bf16[128,1536]{1,0:T(8,128)(2,1)} %get-tuple-element.177), channel_id=1, source_target_pairs={{0,16},{1,17},{2,18},{3,19},{4,20},{5,21},{6,22},{7,23},{8,24},{9,... | collective-permute-start | bytes 1179656 | tf_op jit(solution)/shard_map/ppermute | solution.py:66
  142.2 0.6 compare_convert_fusion.1.refs_7_
  142.8 0.9 collective-permute-done
  143.7 0.8 bitcast_select_fusion.1.refs_0_.refs_13_
  144.5 66.6 %forward_layer.4 = (bf16[128,1536]{1,0:T(8,128)(2,1)}, bf16[1536,128]{1,0:T(8,128)(2,1)}, bf16[4,2,512,128]{3,2,1,0:T(8,128)(2,1)}, bf16[1536,128]{1,0:T(8,128)(...) custom-call(bf16[128,1536]{1,0:T(8,128)(2,1)} %bitcast_select_fusion, ...), custom_call_target="tpu_custom_call", output_to_operand_aliasing={{8}: (14, {})} | custom-call | flops 9261023232 | bytes 30000000 | tf_op jit(solution)/shard_map/forward_layer/pallas_call | solution.py:691
  211.1 1.3 collective-permute-start.1
  212.5 0.8 slice_bitcast_fusion.4.refs_0_
  213.2 0.7 collective-permute-done.1.refs_0_.refs_20_
  214.0 0.7 copy-done.7
  214.7 81.5 %forward_layer.5 = (bf16[128,1536]{1,0:T(8,128)(2,1)}, bf16[1536,128]{1,0:T(8,128)(2,1)}, bf16[4,2,512,128]{3,2,1,0:T(8,128)(2,1)}, bf16[1536,128]{1,0:T(8,128)(...) custom-call(bf16[128,1536]{1,0:T(8,128)(2,1)} %copy-done.7, ...), custom_call_target="tpu_custom_call", output_to_operand_aliasing={{8}: (14, {}), {9}: (15, {})} | custom-call | flops 9261023232 | bytes 30000000 | tf_op jit(solution)/shard_map/forward_layer/pallas_call | solution.py:691
  296.3 6.1 backward_layer.3
  302.4 1.3 collective-permute-start.2
  303.7 64.1 %prepare.1 = (bf16[4096,1536]{1,0:T(8,128)(2,1)}, bf16[4096,1536]{1,0:T(8,128)(2,1)}, bf16[4096,1536]{1,0:T(8,128)(2,1)}) custom-call(bf16[2048,1664]{1,0:T(8,128)(2,1)} %bitcast.105, bf16[2048,1664]{1,0:T(8,128)(2,1)} %bitcast.109, f32[3,1,128]{2,1,0:T(1,128)} %fusion.10.refs_8_.refs_6_.refs_2_, bf16[3,1536,512]{2,1,0:T(8,128)(2,1)} %bitcast.77, ...), custom_call_target="tpu_custom_call" | custom-call | flops 38654705664 | bytes 50331648 | tf_op jit(solution)/shard_map/prepare/pallas_call | solution.py:1199
  367.8 0.8 bitcast_select_fusion.refs_0_
  368.6 76.2 %backward_layer.4 = (f32[128,1536]{1,0:T(8,128)}, bf16[128,1536]{1,0:T(8,128)(2,1)}, bf16[4,640,128]{2,1,0:T(8,128)(2,1)}, bf16[128,1536]{1,0:T(8,128)(2,1)}, bf...) custom-call(bf16[128,1536]{1,0:T(8,128)(2,1)} %bitcast_select_fusion, ...), custom_call_target="tpu_custom_call", output_to_operand_aliasing={{7}: (27, {})} | custom-call | flops 15703474176 | bytes 40000000 | tf_op jit(solution)/shard_map/backward_layer/pallas_call | solution.py:1076
  444.8 1.3 collective-permute-start.3
  446.1 2.5 collective-permute-done.3.refs_0_
  448.6 0.7 copy-done.11
  449.4 58.8 %backward_layer.5 = (f32[128,1536]{1,0:T(8,128)}, bf16[128,1536]{1,0:T(8,128)(2,1)}, bf16[4,640,128]{2,1,0:T(8,128)(2,1)}, bf16[128,1536]{1,0:T(8,128)(2,1)}, bf...) custom-call(bf16[128,1536]{1,0:T(8,128)(2,1)} %copy-done.11, ...), custom_call_target="tpu_custom_call", output_to_operand_aliasing={{7}: (20, {}), {8}: (21, {})} | custom-call | flops 15703474176 | bytes 40000000 | tf_op jit(solution)/shard_map/backward_layer/pallas_call | solution.py:1076
  508.2 1.8 slice_bitcast_fusion.refs_12_
  510.0 0.8 slice_bitcast_fusion.1.refs_4_
  511.1 2.5 collective-permute-start.7
  513.7 0.9 maximum_bitcast_fusion.1
  514.6 2.4 collective-permute-start.8
  517.0 2.5 collective-permute-start.9
  519.5 42.1 %first_weights.1 = (f32[3,1536,512]{2,1,0:T(8,128)}, f32[3,1536,512]{2,1,0:T(8,128)}, f32[3,512,1536]{2,1,0:T(8,128)}, bf16[1,4,4,128,1664]{4,3,2,1,0:T(8,128)(2,1)}, bf16[1,4,4,128,1536]{4,3,2,1,0:T(8,128)(2,1)}) custom-call(bf16[2048,1664]{1,0:T(8,128)(2,1)} %bitcast.106, ...), custom_call_target="tpu_custom_call", output_to_operand_aliasing={{3}: (9, {}), {4}: (10, {})} | custom-call | flops 12884901888 | bytes 18874368 | tf_op jit(solution)/shard_map/first_weights/pallas_call | solution.py:1308
  561.7 0.8 slice_bitcast_fusion.2.refs_12_
  562.5 1.8 slice_bitcast_fusion.3.refs_4_
  564.3 8.9 %attention_weights.2 = (bf16[1536,1024]{1,0:T(8,128)(2,1)}, bf16[1536,1024]{1,0:T(8,128)(2,1)}, bf16[1536,1024]{1,0:T(8,128)(2,1)}, bf16[1536,1024]{1,0:T(8,128)(2,1)}, f32[16,1536]{1,0:T(8,128)}) custom-call(bf16[128,1536]{1,0:T(8,128)(2,1)} %get-tuple-element.255.refs_0_, bf16[4,640,128]{2,1,0:T(8,128)(2,1)} %get-tuple-element.256.refs_1_.refs_9_, ...), custom_call_target="tpu_custom_call" | custom-call | flops 3221225472 | bytes 20000000 | tf_op jit(solution)/shard_map/attention_weights/pallas_call | solution.py:1542
  573.2 3.4 collective-permute-start.4
  576.6 2.5 collective-permute-start.5
  579.1 3.4 collective-permute-start.6
  582.5 39.4 %whole_weights.2 = (f32[3,1536,512]{2,1,0:T(8,128)}, f32[3,1536,512]{2,1,0:T(8,128)}, f32[3,512,1536]{2,1,0:T(8,128)}) custom-call(bf16[2048,1664]{1,0:T(8,128)(2,1)} %bitcast.107, bf16[2048,1664]{1,0:T(8,128)(2,1)} %bitcast.110, bf16[2048,1536]{1,0:T(8,128)(2,1)} %bitcast.120, bf16[2048,1536]{1,0:T(8,128)(2,1)} %bitcast.113, ...), custom_call_target="tpu_custom_call" | custom-call | flops 25769803776 | bytes 37748736 | tf_op jit(solution)/shard_map/whole_weights/pallas_call | solution.py:1373
  621.8 2.4 select_bitcast_fusion.1
  624.2 39.2 %whole_weights.3 = (f32[3,1536,512]{2,1,0:T(8,128)}, f32[3,1536,512]{2,1,0:T(8,128)}, f32[3,512,1536]{2,1,0:T(8,128)}) custom-call(bf16[2048,1664]{1,0:T(8,128)(2,1)} %bitcast.108, bf16[2048,1664]{1,0:T(8,128)(2,1)} %bitcast.111, bf16[2048,1536]{1,0:T(8,128)(2,1)} %bitcast.121, ...), custom_call_target="tpu_custom_call", output_to_operand_aliasing={{0}: (11, {}), {1}: (12, {}), {2}: (13, {})} | custom-call | flops 25769803776 | bytes 37748736 | tf_op jit(solution)/shard_map/whole_weights/pallas_call | solution.py:1373
  663.5 8.5 %sum_blocks.1 = bf16[1536,1024]{1,0:T(8,128)(2,1)} custom-call(bf16[1536,1024]{1,0:T(8,128)(2,1)} %get-tuple-element.292.refs_0_, bf16[1536,1024]{1,0:T(8,128)(2,1)} %collective-permute-done.4.refs_1_, bf16[1536,1024]{1,0:T(8,128)(2,1)} %collective-permute-done.5.refs_2_, bf16[1536,1024]{1,0:T(8,128)(2,1)} %collective-permute-done.6.refs_3_, ...), custom_call_target="tpu_custom_call" | custom-call | bytes 15728640 | tf_op jit(solution)/shard_map/sum_blocks/pallas_call | solution.py:1607
  672.1 3.6 fusion.20
  675.6 1.0 collective-permute-start.10
  676.6 0.7 collective-permute-start.11
  677.4 2.9 collective-permute-start.12
  680.3 26.2 %last_weights.1 = (f32[3,1536,512]{2,1,0:T(8,128)}, f32[3,1536,512]{2,1,0:T(8,128)}, f32[3,512,1536]{2,1,0:T(8,128)}) custom-call(bf16[2048,1664]{1,0:T(8,128)(2,1)} %bitcast.112, bf16[2048,1536]{1,0:T(8,128)(2,1)} %bitcast.115, bf16[3,512,1536]{2,1,0:T(8,128)(2,1)} %bitcast.104, ...), custom_call_target="tpu_custom_call", output_to_operand_aliasing={{0}: (12, {}), {1}: (13, {}), {2}: (14, {})} | custom-call | flops 12884901888 | bytes 18874368 | tf_op jit(solution)/shard_map/last_weights/pallas_call | solution.py:1431
  706.6 2.5 add_convert_fusion.refs_0_
  709.2 19.4 %sum_small.1 = f32[16,1536]{1,0:T(8,128)} custom-call(f32[16,1536]{1,0:T(8,128)} %get-tuple-element.318.upper, f32[16,1536]{1,0:T(8,128)} %get-tuple-element.319.lower), custom_call_target="tpu_custom_call" | custom-call | tf_op jit(solution)/shard_map/sum_small/pallas_call | solution.py:1653
  728.6 1.1 collective-permute-start.13
  729.7 0.9 collective-permute-start.14
  730.7 1.5 collective-permute-start.15
  732.1 1.2 maximum_bitcast_fusion
  733.4 0.7 dynamic-slice_bitcast_fusion
  734.7 1.5 fusion.21
  736.2 12.9 %collective-permute-done.13.refs_1_ = bf16[384,1024]{1,0:T(8,128)(2,1)S(1)} collective-permute-done((bf16[384,1024]{1,0:T(8,128)(2,1)S(1)}, bf16[384,1024]{1,0:T(8,128)(2,1)S(1)}, u32[]{:S(2)}, u32[]{:S(2)}) %collective-permute-start.13) | collective-permute-done | bytes 786464 | tf_op jit(solution)/shard_map/ppermute | solution.py:1711
  749.1 9.8 %collective-permute-done.14.refs_2_ = bf16[384,1024]{1,0:T(8,128)(2,1)S(1)} collective-permute-done((bf16[384,1024]{1,0:T(8,128)(2,1)S(1)}, bf16[384,1024]{1,0:T(8,128)(2,1)S(1)}, u32[]{:S(2)}, u32[]{:S(2)}) %collective-permute-start.14) | collective-permute-done | bytes 786464 | tf_op jit(solution)/shard_map/ppermute | solution.py:1711
  758.9 0.9 copy-done.5
  759.8 4.9 assemble.1
  (45 shorter events, 2.2 us)
Async XLA Ops:
  70.3 73.4 %copy-start.2 = (bf16[2,128,1536]{2,1,0:T(8,128)(2,1)S(1)}, bf16[2,128,1536]{2,1,0:T(8,128)(2,1)}, u32[]{:S(2)}) copy-start(bf16[2,128,1536]{2,1,0:T(8,128)(2,1)} %param.14) | copy-start | bytes 2359300
  130.6 13.1 %collective-permute-start = (bf16[128,1536]{1,0:T(8,128)(2,1)}, bf16[128,1536]{1,0:T(8,128)(2,1)S(1)}, u32[]{:S(2)}, u32[]{:S(2)}) collective-permute-start(bf16[128,1536]{1,0:T(8,128)(2,1)} %get-tuple-element.177), channel_id=1, source_target_pairs={{0,16},{1,17},{2,18},{3,19},{4,20},{5,21},{6,22},{7,23},{8,24},{9,... | collective-permute-start | bytes 1179656 | tf_op jit(solution)/shard_map/ppermute | solution.py:66
  144.5 68.0 %copy-start.3 = (bf16[2,128,1536]{2,1,0:T(8,128)(2,1)S(1)}, bf16[2,128,1536]{2,1,0:T(8,128)(2,1)}, u32[]{:S(2)}) copy-start(bf16[2,128,1536]{2,1,0:T(8,128)(2,1)} %param.15) | copy-start | bytes 2359300
  211.1 2.8 collective-permute-start.1
  214.0 0.7 copy-start.7
  302.4 65.4 %collective-permute-start.2 = (bf16[128,1536]{1,0:T(8,128)(2,1)}, bf16[128,1536]{1,0:T(8,128)(2,1)S(1)}, u32[]{:S(2)}, u32[]{:S(2)}) collective-permute-start(bf16[128,1536]{1,0:T(8,128)(2,1)} %get-tuple-element.196), channel_id=1, source_target_pairs={{16,0},{17,1},{18,2},{19,3},{20,4},{21,5},{22,6},{23,7},{24,8},{25... | collective-permute-start | bytes 1179656 | tf_op jit(solution)/shard_map/ppermute | solution.py:66
  444.8 3.8 collective-permute-start.3
  448.6 0.7 copy-start.11
  449.4 60.6 %copy-start.6 = (bf16[4,128,1664]{2,1,0:T(8,128)(2,1)S(1)}, bf16[4,128,1664]{2,1,0:T(8,128)(2,1)}, u32[]{:S(2)}) copy-start(bf16[4,128,1664]{2,1,0:T(8,128)(2,1)} %get-tuple-element.267.refs_19_) | copy-start | bytes 5111812
  510.8 2.8 copy-start.8
  510.8 2.8 copy-start.9
  510.8 2.8 copy-start.10
  511.1 67.9 %collective-permute-start.7 = (bf16[1536,1024]{1,0:T(8,128)(2,1)}, bf16[1536,1024]{1,0:T(8,128)(2,1)}, u32[]{:S(2)}, u32[]{:S(2)}) collective-permute-start(bf16[1536,1024]{1,0:T(8,128)(2,1)} %get-tuple-element.281), channel_id=1, source_target_pairs={{16,20},{20,24},{24,28},{28,16},{17,21},{21,25},{25,29},{29,17},{1... | collective-permute-start | bytes 9437192 | tf_op jit(solution)/shard_map/ppermute | solution.py:60
  514.6 148.9 %collective-permute-start.8 = (bf16[1536,1024]{1,0:T(8,128)(2,1)}, bf16[1536,1024]{1,0:T(8,128)(2,1)}, u32[]{:S(2)}, u32[]{:S(2)}) collective-permute-start(bf16[1536,1024]{1,0:T(8,128)(2,1)} %get-tuple-element.282), channel_id=1, source_target_pairs={{16,24},{20,28},{24,16},{28,20},{17,25},{21,29},{25,17},{29,21},{1... | collective-permute-start | bytes 9437192 | tf_op jit(solution)/shard_map/ppermute | solution.py:60
  517.0 146.5 %collective-permute-start.9 = (bf16[1536,1024]{1,0:T(8,128)(2,1)}, bf16[1536,1024]{1,0:T(8,128)(2,1)}, u32[]{:S(2)}, u32[]{:S(2)}) collective-permute-start(bf16[1536,1024]{1,0:T(8,128)(2,1)} %get-tuple-element.283), channel_id=1, source_target_pairs={{16,28},{20,16},{24,20},{28,24},{17,29},{21,17},{25,21},{29,25},{1... | collective-permute-start | bytes 9437192 | tf_op jit(solution)/shard_map/ppermute | solution.py:60
  573.2 90.3 %collective-permute-start.4 = (bf16[1536,1024]{1,0:T(8,128)(2,1)}, bf16[1536,1024]{1,0:T(8,128)(2,1)}, u32[]{:S(2)}, u32[]{:S(2)}) collective-permute-start(bf16[1536,1024]{1,0:T(8,128)(2,1)} %get-tuple-element.272), channel_id=1, source_target_pairs={{0,1},{1,0},{2,3},{3,2},{4,5},{5,4},{6,7},{7,6},{8,9},{9,8},{10,11... | collective-permute-start | bytes 9437192 | tf_op jit(solution)/shard_map/ppermute | solution.py:1711
  576.6 86.9 %collective-permute-start.5 = (bf16[1536,1024]{1,0:T(8,128)(2,1)}, bf16[1536,1024]{1,0:T(8,128)(2,1)}, u32[]{:S(2)}, u32[]{:S(2)}) collective-permute-start(bf16[1536,1024]{1,0:T(8,128)(2,1)} %get-tuple-element.273), channel_id=1, source_target_pairs={{0,2},{1,3},{2,0},{3,1},{4,6},{5,7},{6,4},{7,5},{8,10},{9,11},{10,... | collective-permute-start | bytes 9437192 | tf_op jit(solution)/shard_map/ppermute | solution.py:1711
  579.1 84.5 %collective-permute-start.6 = (bf16[1536,1024]{1,0:T(8,128)(2,1)}, bf16[1536,1024]{1,0:T(8,128)(2,1)}, u32[]{:S(2)}, u32[]{:S(2)}) collective-permute-start(bf16[1536,1024]{1,0:T(8,128)(2,1)} %get-tuple-element.274), channel_id=1, source_target_pairs={{0,3},{1,2},{2,1},{3,0},{4,7},{5,6},{6,5},{7,4},{8,11},{9,10},{10,... | collective-permute-start | bytes 9437192 | tf_op jit(solution)/shard_map/ppermute | solution.py:1711
  675.6 30.8 %collective-permute-start.10 = (bf16[384,1024]{1,0:T(8,128)(2,1)}, bf16[384,1024]{1,0:T(8,128)(2,1)}, u32[]{:S(2)}, u32[]{:S(2)}) collective-permute-start(bf16[384,1024]{1,0:T(8,128)(2,1)} %get-tuple-element.362), channel_id=1, source_target_pairs={{0,4},{16,17},{1,5},{17,16},{2,6},{18,19},{3,7},{19,18},{4,8},{20,... | collective-permute-start | bytes 2359304 | tf_op jit(solution)/shard_map/ppermute | solution.py:1967
  676.6 30.0 %collective-permute-start.11 = (bf16[384,1024]{1,0:T(8,128)(2,1)}, bf16[384,1024]{1,0:T(8,128)(2,1)}, u32[]{:S(2)}, u32[]{:S(2)}) collective-permute-start(bf16[384,1024]{1,0:T(8,128)(2,1)} %get-tuple-element.361), channel_id=1, source_target_pairs={{0,8},{16,18},{1,9},{17,19},{2,10},{18,16},{3,11},{19,17},{4,12},{... | collective-permute-start | bytes 2359304 | tf_op jit(solution)/shard_map/ppermute | solution.py:1967
  677.4 29.3 %collective-permute-start.12 = (bf16[384,1024]{1,0:T(8,128)(2,1)}, bf16[384,1024]{1,0:T(8,128)(2,1)}, u32[]{:S(2)}, u32[]{:S(2)}) collective-permute-start(bf16[384,1024]{1,0:T(8,128)(2,1)} %get-tuple-element.360), channel_id=1, source_target_pairs={{0,12},{16,19},{1,13},{17,18},{2,14},{18,17},{3,15},{19,16},{4,0},... | collective-permute-start | bytes 2359304 | tf_op jit(solution)/shard_map/ppermute | solution.py:1967
  706.5 25.7 %copy-start = (f32[1,128,1536]{2,1,0:T(8,128)S(1)}, f32[1,128,1536]{2,1,0:T(8,128)}, u32[]{:S(2)}) copy-start(f32[1,128,1536]{2,1,0:T(8,128)} %get-tuple-element.365) | copy-start | bytes 2359300
  709.2 49.8 %copy-start.1 = (bf16[384,1024]{1,0:T(8,128)(2,1)}, bf16[384,1024]{1,0:T(8,128)(2,1)S(1)}, u32[]{:S(2)}) copy-start(bf16[384,1024]{1,0:T(8,128)(2,1)S(1)} %add_convert_fusion.refs_0_) | copy-start | bytes 2359300
  728.6 20.5 %collective-permute-start.13 = (bf16[384,1024]{1,0:T(8,128)(2,1)S(1)}, bf16[384,1024]{1,0:T(8,128)(2,1)S(1)}, u32[]{:S(2)}, u32[]{:S(2)}) collective-permute-start(bf16[384,1024]{1,0:T(8,128)(2,1)S(1)} %add_convert_fusion.refs_0_), channel_id=1, source_target_pairs={{0,1},{1,0},{2,3},{3,2},{16,17},{17,16},{18,19},{19,18},{4,5},{5,4... | collective-permute-start | bytes 2359304 | tf_op jit(solution)/shard_map/ppermute | solution.py:1711
  729.7 29.2 %collective-permute-start.14 = (bf16[384,1024]{1,0:T(8,128)(2,1)S(1)}, bf16[384,1024]{1,0:T(8,128)(2,1)S(1)}, u32[]{:S(2)}, u32[]{:S(2)}) collective-permute-start(bf16[384,1024]{1,0:T(8,128)(2,1)S(1)} %add_convert_fusion.refs_0_), channel_id=1, source_target_pairs={{0,2},{1,3},{2,0},{3,1},{16,18},{17,19},{18,16},{19,17},{4,6},{5,7... | collective-permute-start | bytes 2359304 | tf_op jit(solution)/shard_map/ppermute | solution.py:1711
  730.7 28.2 %collective-permute-start.15 = (bf16[384,1024]{1,0:T(8,128)(2,1)S(1)}, bf16[384,1024]{1,0:T(8,128)(2,1)}, u32[]{:S(2)}, u32[]{:S(2)}) collective-permute-start(bf16[384,1024]{1,0:T(8,128)(2,1)S(1)} %add_convert_fusion.refs_0_), channel_id=1, source_target_pairs={{0,3},{1,2},{2,1},{3,0},{16,19},{17,18},{18,17},{19,16},{4,7},{5,6... | collective-permute-start | bytes 2359304 | tf_op jit(solution)/shard_map/ppermute | solution.py:1711
  749.1 9.8 %copy-start.4 = (bf16[384,1024]{1,0:T(8,128)(2,1)}, bf16[384,1024]{1,0:T(8,128)(2,1)S(1)}, u32[]{:S(2)}) copy-start(bf16[384,1024]{1,0:T(8,128)(2,1)S(1)} %collective-permute-done.13.refs_1_) | copy-start | bytes 2359300
  758.9 0.9 copy-start.5
